TPU v7x, 256 devices: a whole 4x4x8 slice. The times are simulated.
256 devices in a mesh: rows: 32 (over z, x), cols: 8 (over y, core).
Axes of the slice: x: 4, y: 4, z: 8, core: 2. Of those that a mesh axis runs over, the one named last changes fastest.
Arguments:
- features: bfloat16 [256, 131072], P('cols', 'rows'), may hold values from -6 to 6
- weight: bfloat16 [256, 256], replicated, may hold values from -0.375 to 0.375
- adj_tiles: bfloat16 [32768, 128, 128], P('rows'), may hold values from -0.09375 to 0.09375
- tile_rows: int32 [32768], P('rows'), may hold values from 0 to 31
- tile_cols: int32 [32768], P('rows'), may hold values from 0 to 1023
- tile_count: int32 [32], P('rows'), may hold values from 512 to 1024, as said below
- cotangent: bfloat16 [256, 131072], P('cols', 'rows'), may hold values from -6 to 6
Outputs:
- aggregated: bfloat16 [256, 131072], P('cols', 'rows')
- grad_features: bfloat16 [256, 131072], P('cols', 'rows')
- grad_weight: float32 [256, 256], replicated
Inputs may be any that keep to these rules, and one draw needn't show every extreme that they name: `tile_count`: some index of rows uses all 1024 slots in every draw.
All inputs are finite; a program needn't handle non-finite values.
Results may differ from a plain program's by a relative error of at most 0.005.
Values may be sent and summed in bfloat16 or wider, within the bound.
No kernel may reach another device: no remote copies, remote signals or barrier semaphores. Data moves between devices by JAX's collectives and lax.ppermute only.
A program may use at most 192 MiB of HBM per device.

v0:
```python
import jax
import jax.numpy as jnp
from jax import lax
from jax.sharding import PartitionSpec as P


def on_device(features, weight, adj_tiles, tile_rows, tile_cols, tile_count, cotangent):
    side = adj_tiles.shape[1]
    slots = adj_tiles.shape[0]
    narrow = features.shape[0]
    local_nodes = features.shape[1]
    local_blocks = local_nodes // side
    total_blocks = local_blocks * lax.axis_size("rows")
    valid = (jnp.arange(slots, dtype=jnp.int32) < tile_count[0]).astype(jnp.float32)
    full_inputs = lax.all_to_all(features, "cols", split_axis=1, concat_axis=0, tiled=True)
    hidden_full = lax.dot_general(
        weight, full_inputs, (((0,), (0,)), ((), ())), preferred_element_type=jnp.float32
    ).astype(jnp.bfloat16)
    hidden_panel = lax.all_to_all(hidden_full, "cols", split_axis=0, concat_axis=1, tiled=True)
    whole_panel = lax.all_gather(hidden_panel, "rows", axis=1, tiled=True)
    blocked = whole_panel.reshape(narrow, total_blocks, side)
    picked = jnp.take(blocked, tile_cols, axis=1)
    terms = jnp.einsum("tij,ftj->tfi", adj_tiles, picked, preferred_element_type=jnp.float32)
    terms = terms * valid[:, None, None]
    summed = jax.ops.segment_sum(terms, tile_rows, local_blocks)
    aggregated = jnp.transpose(summed, (1, 0, 2)).reshape(narrow, local_nodes).astype(jnp.bfloat16)
    grad_blocked = cotangent.reshape(narrow, local_blocks, side)
    grad_picked = jnp.take(grad_blocked, tile_rows, axis=1)
    reverse = jnp.einsum("tij,fti->tfj", adj_tiles, grad_picked, preferred_element_type=jnp.float32)
    reverse = reverse * valid[:, None, None]
    spread = jax.ops.segment_sum(reverse, tile_cols, total_blocks)
    spread = jnp.transpose(spread, (1, 0, 2)).reshape(narrow, total_blocks * side)
    dhidden = lax.psum_scatter(spread, "rows", scatter_dimension=1, tiled=True).astype(jnp.bfloat16)
    grad_full = lax.all_to_all(dhidden, "cols", split_axis=1, concat_axis=0, tiled=True)
    feature_grad_full = jnp.dot(weight, grad_full, preferred_element_type=jnp.float32).astype(
        jnp.bfloat16
    )
    grad_features = lax.all_to_all(
        feature_grad_full, "cols", split_axis=0, concat_axis=1, tiled=True
    )
    weight_term = lax.dot_general(
        full_inputs, grad_full, (((1,), (1,)), ((), ())), preferred_element_type=jnp.float32
    )
    grad_weight = lax.psum(weight_term, ("rows", "cols"))
    return (aggregated, grad_features, grad_weight)


def solution(mesh):
    placed = (
        P("cols", "rows"),
        P(),
        P("rows", None, None),
        P("rows"),
        P("rows"),
        P("rows"),
        P("cols", "rows"),
    )
    return jax.shard_map(
        on_device,
        mesh=mesh,
        in_specs=placed,
        out_specs=(P("cols", "rows"), P("cols", "rows"), P()),
        check_vma=False,
    )
```

profile of v0, /device:TPU:1, one launch (start us, length us, event | category | flops | bytes accessed | tf_op | source)
XLA Modules:
  0.0 927.2 jit_solution(11049642275321270350)
XLA Ops:
  7.2 0.0 copy-start
  7.2 0.0 copy-start.4
  7.2 0.0 copy-start.2
  7.2 1.7 copy.49
  8.9 6.6 all-to-all-start
  15.5 0.0 copy-done
  15.5 0.7 fusion.10
  16.9 9.9 %gather_fusion.1 = bf16[1024,32,128]{2,1,0:T(8,128)(2,1)} fusion(bf16[32,32,128]{2,0,1:T(8,128)(2,1)S(1)} %copy_bitcast_fusion.4, s32[1024]{0:T(1024)S(1)} %fusion.10), kind=kCustom, calls=%fused_computation.1 | custom fusion | bytes 16781312 | tf_op jit(solution)/shard_map/jit(_take)/gather | solution.py:28
  26.7 0.0 copy-done.4
  26.8 0.0 all-to-all-done
  26.8 0.0 copy-done.2
  26.8 1.0 convolution_convert_fusion.1
  27.7 4.8 all-to-all-start.1
  32.6 0.0 all-gather.2.cloned.1.call-start
  32.6 24.6 %convolution_multiply_fusion = f32[1024,32,128]{2,1,0:T(8,128)} fusion(bf16[1024,128,128]{2,1,0:T(8,128)(2,1)} %param.9, bf16[1024,32,128]{2,1,0:T(8,128)(2,1)} %gather_fusion.1, f32[1024]{0:T(1024)S(1)} %get-tuple-element.15, pred[1024]{0:T(1024)(128)(4,1)S(1)} %get-tuple-element.16), kind=kOutput, calls=%fused_computation.5 | convolution fusion | flops 1082130432 | bytes 58725376 | tf_op jit(solution)/shard_map/tij,fti->tfj/dot_general | solution.py:29
  57.1 0.0 copy-start.3
  57.1 7.9 broadcast_in_dim.41
  65.0 0.0 copy-done.3
  65.0 134.3 %scatter_fusion.1 = f32[1024,32,128]{2,1,0:T(8,128)} fusion(f32[1024,32,128]{2,1,0:T(8,128)} %broadcast_in_dim.41, s32[1024]{0:T(1024)S(1)} %copy-done.3, f32[1024,32,128]{2,1,0:T(8,128)} %convolution_multiply_fusion), kind=kCustom, calls=%fused_computation.3 | custom fusion | flops 4194304 | bytes 50335744 | tf_op jit(solution)/shard_map/scatter-add | solution.py:31
  199.3 0.0 all-to-all-done.1
  199.3 0.7 copy.38
  200.0 0.0 all-gather.2.cloned.1.call-update
  200.1 0.0 reduce-scatter.2.cloned.1.call-start
  200.1 11.3 %copy_bitcast_fusion = f32[32,131072]{1,0:T(8,128)} fusion(f32[1024,32,128]{2,1,0:T(8,128)} %scatter_fusion.1), kind=kLoop, calls=%fused_computation.4 | loop fusion | bytes 33554432 | tf_op jit(solution)/shard_map/reshape | solution.py:32
  211.5 0.0 reduce-scatter.2.cloned.1.call-update
  211.5 88.5 %all-gather.2.cloned.1.call-done = bf16[32,131072]{1,0:T(8,128)(2,1)} async-done(((bf16[32,4096]{1,0:T(8,128)(2,1)}), bf16[32,131072]{1,0:T(8,128)(2,1)}) %all-gather.2.cloned.1.call-update) | async-done | bytes 8388624 | tf_op jit(solution)/shard_map/all_gather | solution.py:20
  300.1 8.0 copy_bitcast_fusion.1
  308.1 13.2 %gather_fusion = bf16[1024,32,128]{2,1,0:T(8,128)(2,1)} fusion(bf16[32,1024,128]{2,0,1:T(8,128)(2,1)} %copy_bitcast_fusion.1, s32[1024]{0:T(1024)S(1)} %fusion.9), kind=kCustom, calls=%fused_computation | custom fusion | bytes 16781312 | tf_op jit(solution)/shard_map/jit(_take)/gather | solution.py:22
  321.4 220.9 %reduce-scatter.2.cloned.1.call-done = f32[32,4096]{1,0:T(8,128)} async-done(((f32[32,131072]{1,0:T(8,128)}), f32[32,4096]{1,0:T(8,128)}) %reduce-scatter.2.cloned.1.call-update) | async-done | bytes 524304 | tf_op jit(solution)/shard_map/reduce_scatter | solution.py:33
  542.2 1.1 convert_element_type.33
  543.3 0.7 copy.48
  544.0 9.1 all-to-all-start.2
  553.2 0.0 all-reduce.2.cloned.1.call-start
  553.2 27.1 %convolution_multiply_fusion.1 = f32[1024,32,128]{2,1,0:T(8,128)} fusion(bf16[1024,128,128]{2,1,0:T(8,128)(2,1)} %param.9, bf16[1024,32,128]{2,1,0:T(8,128)(2,1)} %gather_fusion, f32[1024]{0:T(1024)S(1)} %get-tuple-element.15, pred[1024]{0:T(1024)(128)(4,1)S(1)} %compare_and_fusion.1), kind=kOutput, calls=%fused_computation.6 | convolution fusion | flops 1082130432 | bytes 58725376 | tf_op jit(solution)/shard_map/tij,ftj->tfi/dot_general | solution.py:23
  580.3 0.0 copy-start.1
  580.3 88.9 %scatter_fusion = f32[32,32,128]{2,1,0:T(8,128)S(1)} fusion(f32[32,32,128]{2,1,0:T(8,128)S(1)} %broadcast_in_dim.36, s32[1024]{0:T(1024)S(1)} %copy-done.4, f32[1024,32,128]{2,1,0:T(8,128)} %convolution_multiply_fusion.1), kind=kCustom, calls=%fused_computation.2 | custom fusion | flops 4194304 | bytes 50335744 | tf_op jit(solution)/shard_map/scatter-add | solution.py:25
  669.2 0.0 all-to-all-done.2
  669.2 1.0 convolution_bitcast_fusion
  670.1 0.9 convolution_convert_fusion
  671.1 0.0 all-reduce.2.cloned.1.call-update
  671.1 4.8 all-to-all-start.3
  675.9 0.7 copy_bitcast_fusion.2
  676.7 241.5 %all-reduce.2.cloned.1.call-done = f32[256,256]{0,1:T(8,128)} async-done(((f32[256,256]{0,1:T(8,128)}), f32[256,256]{0,1:T(8,128)}) %all-reduce.2.cloned.1.call-update) | async-done | bytes 262160 | tf_op jit(solution)/shard_map/psum | solution.py:44
  918.1 1.8 copy.33
  919.9 0.0 all-to-all-done.3
  919.9 0.7 copy.41
  920.7 0.0 copy-done.1
  (5 shorter events, 0.1 us)
Async XLA Ops:
  7.2 8.3 copy-start
  7.2 19.6 %copy-start.4 = (s32[1024]{0:T(1024)S(1)}, s32[1024]{0:T(1024)}, u32[]{:S(2)}) copy-start(s32[1024]{0:T(1024)} %param.10) | copy-start | bytes 12292
  7.2 19.6 %copy-start.2 = (bf16[256,256]{1,0:T(8,128)(2,1)S(1)}, bf16[256,256]{1,0:T(8,128)(2,1)}, u32[]{:S(2)}) copy-start(bf16[256,256]{1,0:T(8,128)(2,1)} %param.8) | copy-start | bytes 393220
  8.9 17.8 %all-to-all-start = ((bf16[32,8,512]{2,0,1:T(8,128)(2,1)}), bf16[32,8,512]{2,0,1:T(8,128)(2,1)S(1)}, u32[]{:S(2)}, u32[]{:S(2)}) async-start(bf16[32,8,512]{2,0,1:T(8,128)(2,1)} %bitcast.62), calls=%async_computation | async-start | bytes 524288 | tf_op jit(solution)/shard_map/all_to_all | solution.py:15
  27.7 171.6 %all-to-all-start.1 = ((bf16[8,32,512]{2,1,0:T(8,128)(2,1)}), bf16[8,32,512]{2,1,0:T(8,128)(2,1)S(1)}, u32[]{:S(2)}, u32[]{:S(2)}) async-start(bf16[8,32,512]{2,1,0:T(8,128)(2,1)} %bitcast.2), calls=%async_computation.1 | async-start | bytes 524288 | tf_op jit(solution)/shard_map/all_to_all | solution.py:19
  32.6 267.5 %all-gather.2.cloned.1.call-start = ((), (), s32[]{:S(2)}) async-start(), calls=%async_computation.5 | async-start | bytes 8650752 | tf_op jit(solution)/shard_map/all_gather | solution.py:20
  57.1 7.9 copy-start.3
  200.1 342.2 %reduce-scatter.2.cloned.1.call-start = ((), (), s32[]{:S(2)}) async-start(), calls=%async_computation.6 | async-start | bytes 17301504 | tf_op jit(solution)/shard_map/reduce_scatter | solution.py:33
  544.0 125.1 %all-to-all-start.2 = ((bf16[32,8,512]{2,0,1:T(8,128)(2,1)}), bf16[32,8,512]{2,0,1:T(8,128)(2,1)S(1)}, u32[]{:S(2)}, u32[]{:S(2)}) async-start(bf16[32,8,512]{2,0,1:T(8,128)(2,1)} %bitcast.61), calls=%async_computation.3 | async-start | bytes 524288 | tf_op jit(solution)/shard_map/all_to_all | solution.py:34
  553.2 365.0 %all-reduce.2.cloned.1.call-start = ((), (), s32[]{:S(2)}) async-start(), calls=%async_computation.7 | async-start | bytes 524288 | tf_op jit(solution)/shard_map/psum | solution.py:44
  580.3 340.4 %copy-start.1 = (bf16[32,4096]{1,0:T(8,128)(2,1)S(1)}, bf16[32,4096]{1,0:T(8,128)(2,1)}, u32[]{:S(2)}) copy-start(bf16[32,4096]{1,0:T(8,128)(2,1)} %param.13) | copy-start | bytes 786436
  671.1 248.8 %all-to-all-start.3 = ((bf16[8,32,512]{2,1,0:T(8,128)(2,1)}), bf16[8,32,512]{2,1,0:T(8,128)(2,1)S(1)}, u32[]{:S(2)}, u32[]{:S(2)}) async-start(bf16[8,32,512]{2,1,0:T(8,128)(2,1)} %bitcast.12), calls=%async_computation.4 | async-start | bytes 524288 | tf_op jit(solution)/shard_map/all_to_all | solution.py:38
Sparse Core Ops, SparseCore 0:
  200.2 99.8 all-gather.1
  304.2 238.0 reduce-scatter.1
  671.2 246.8 all-reduce.1
where the time goes:
time: 932 us; the launch traced here: 927 us
  waiting for transfers between devices  551 us (59%)
  other arithmetic  226 us (24%)
  local copies, waits for them, and re-layouts  56.2 us (6%)
  matrix products  54.5 us (6%)
  starting transfers between devices  25.4 us (3%)
  between operations  14.5 us (2%)
    psum x1, waiting for transfers between devices, on_device(): grad_weight = lax.psum(weight_term, ('rows', 'cols'))  241 us
    reduce_scatter x1, waiting for transfers between devices, on_device(): lax.psum_scatter(spread, 'rows', scatter_dimension=1, tiled=True)  221 us
    scatter-add x1, other arithmetic, on_device(): spread = jax.ops.segment_sum(reverse, tile_cols, total_blocks)  134 us
    scatter-add x1, other arithmetic, on_device(): summed = jax.ops.segment_sum(terms, tile_rows, local_blocks)  88.9 us
    all_gather x1, waiting for transfers between devices, on_device(): whole_panel = lax.all_gather(hidden_panel, 'rows', axis=1, tiled=True)  88.5 us
    dot_general x1, matrix products, on_device(): jnp.einsum('tij,ftj->tfi', adj_tiles, picked, preferred_element_type=jnp....  27.1 us
    dot_general x1, matrix products, on_device(): jnp.einsum('tij,fti->tfj', adj_tiles, grad_picked, preferred_element_type...  24.6 us
  transfers between devices with their start and end apart: 7, of which 3 were waited for; matrix products, arithmetic and copies ran while one was open for 35% of the time, Pallas kernels for 0%

commit v1 on v0

v1 whole, which is shorter than its diff:
```python
import functools

import jax
import jax.numpy as jnp
from jax import lax
from jax.experimental import pallas as pl
from jax.experimental.pallas import tpu as pltpu
from jax.sharding import Mesh
from jax.sharding import PartitionSpec as P

TB = 128
MIB = 1024 * 1024


def zero(ref):
    @pl.loop(0, ref.shape[0] // 16)
    def _(i):
        ref[pl.ds(i * 16, 16)] = jnp.zeros((16,) + ref.shape[1:], ref.dtype)


def each_tile(count, tb, one):
    base = pl.program_id(0) * tb

    @pl.when(base + tb <= count)
    def _():
        for k in range(tb):
            one(base + k, k)

    @pl.when((base < count) & (base + tb > count))
    def _():
        @pl.loop(0, count - base)
        def _(k):
            one(base + k, k)


def reverse_body(rows_ref, places_ref, count_ref, grads_ref, tiles_ref, *rest, tb):
    outs, total = rest[:-1], rest[-1]

    @pl.when(pl.program_id(0) == 0)
    def _():
        zero(total)

    def one(slot, k):
        total[places_ref[slot]] += jnp.dot(
            grads_ref[rows_ref[slot]], tiles_ref[k], preferred_element_type=jnp.float32
        )

    each_tile(count_ref[0], tb, one)

    @pl.when(pl.program_id(0) == pl.num_programs(0) - 1)
    def _():
        for i, out in enumerate(outs):
            @pl.loop(0, out.shape[0] // 8)
            def _(j):
                out[pl.ds(j * 8, 8)] = total[pl.ds(i * out.shape[0] + j * 8, 8)].astype(out.dtype)


def forward_body(rows_ref, cols_ref, count_ref, panel_ref, tiles_ref, out_ref, total, *, tb):
    @pl.when(pl.program_id(0) == 0)
    def _():
        zero(total)

    def one(slot, k):
        total[rows_ref[slot]] += lax.dot_general(
            panel_ref[cols_ref[slot]], tiles_ref[k], (((1,), (1,)), ((), ())),
            preferred_element_type=jnp.float32,
        )

    each_tile(count_ref[0], tb, one)

    @pl.when(pl.program_id(0) == pl.num_programs(0) - 1)
    def _():
        out_ref[...] = total[...].astype(out_ref.dtype)


def tile_pass(body, rows, cols, count, resident, tiles, total, outs, name):
    slots, side, _ = tiles.shape
    narrow = resident.shape[1]

    def fetch(i, rows_ref, cols_ref, count_ref):
        return (jnp.minimum(i, jnp.maximum((count_ref[0] + TB - 1) // TB - 1, 0)), 0, 0)

    out = [jax.ShapeDtypeStruct((total // outs, narrow, side), jnp.bfloat16)] * outs
    return pl.pallas_call(
        functools.partial(body, tb=TB),
        out_shape=out,
        grid_spec=pltpu.PrefetchScalarGridSpec(
            num_scalar_prefetch=3,
            grid=(slots // TB,),
            in_specs=[
                pl.BlockSpec(memory_space=pltpu.VMEM),
                pl.BlockSpec((TB, side, side), fetch),
            ],
            out_specs=[pl.BlockSpec(memory_space=pltpu.VMEM)] * outs,
            scratch_shapes=[pltpu.VMEM((total, narrow, side), jnp.float32)],
        ),
        compiler_params=pltpu.CompilerParams(vmem_limit_bytes=40 * MIB),
        cost_estimate=pl.CostEstimate(
            flops=16 * slots * narrow * side * side,
            bytes_accessed=2 * slots * side * side + 6 * total * narrow * side,
            transcendentals=0,
        ),
        name=name,
    )(rows, cols, count, resident, tiles)


def exchange(parts, axis):
    return lax.all_to_all(parts, axis, split_axis=0, concat_axis=0, tiled=True)


def total_of_all(term):
    width = term.shape[1]
    n_cols, n_rows = lax.axis_size("cols"), lax.axis_size(("z", "x"))
    per_col = exchange(term, "cols").reshape(n_cols, term.shape[0] // n_cols, width).sum(0)
    per_row = exchange(per_col, ("z", "x")).reshape(n_rows, -1, width).sum(0)
    per_col = exchange(jnp.tile(per_row, (n_rows, 1)), ("z", "x"))
    return exchange(jnp.tile(per_col, (n_cols, 1)), "cols")


def on_device(features, weight, adj_tiles, tile_rows, tile_cols, tile_count, cotangent):
    side = adj_tiles.shape[1]
    narrow, local_nodes = features.shape
    blocks = local_nodes // side
    nz, nx, nc = lax.axis_size("z"), lax.axis_size("x"), lax.axis_size("cols")
    z, x, c = lax.axis_index("z"), lax.axis_index("x"), lax.axis_index("cols")

    def to_blocks(a):
        return jnp.transpose(a.reshape(narrow, blocks, side), (1, 0, 2))

    def from_blocks(a):
        return jnp.transpose(a, (1, 0, 2)).reshape(narrow, local_nodes)

    panel = lax.all_gather(to_blocks(features), ("z", "x"), axis=0, tiled=True)

    grad_full = lax.all_to_all(cotangent, "cols", split_axis=1, concat_axis=0, tiled=True)
    turned = jnp.dot(weight, grad_full, preferred_element_type=jnp.float32).astype(jnp.bfloat16)
    turned = lax.all_to_all(turned, "cols", split_axis=0, concat_axis=1, tiled=True)

    turn = 1 - 2 * (c % 2)
    owner = tile_cols // blocks
    far_x = (turn * (owner % nx - x)) % nx
    far_z = (turn * (owner // nx - z)) % nz
    early = nz // 2
    late_first = (far_z - (early - 1)) % nz
    place = ((late_first // early * nx + far_x) * early + late_first % early) * blocks + tile_cols % blocks
    terms = tile_pass(
        reverse_body, tile_rows, place, tile_count, to_blocks(turned), adj_tiles,
        nz * nx * blocks, 2 * nx, "reverse",
    )

    def ring(a, axis, n, ahead):
        moves = [(i * nc + j, (i + ahead * (1 - 2 * (j % 2))) % n * nc + j) for i in range(n) for j in range(nc)]
        return lax.ppermute(a, (axis, "cols"), moves)

    def add(*terms):
        return sum(t.astype(jnp.float32) for t in terms)

    held = {}
    for part in range(2):
        t0, t1, t2, t3 = terms[part * nx:(part + 1) * nx]
        m2 = ring(t2, "x", nx, 1)
        m3 = ring(t3, "x", nx, -1)
        m1 = ring(add(t1, m2).astype(jnp.bfloat16), "x", nx, 1)
        for i in range(early):
            cut = slice(i * blocks, (i + 1) * blocks)
            held[(part * early + i + early - 1) % nz] = (t0[cut], m1[cut], m3[cut])
    ahead, behind = (), ()
    for step in range(4):
        ahead = (ring(add(*held[4 - step], *ahead).astype(jnp.bfloat16), "z", nz, 1),)
        if step < 3:
            behind = (ring(add(*held[5 + step], *behind).astype(jnp.bfloat16), "z", nz, -1),)
    grad_features = from_blocks(add(*held[0], *ahead, *behind).astype(jnp.bfloat16))

    (mixed,) = tile_pass(
        forward_body, tile_rows, tile_cols, tile_count, panel, adj_tiles, blocks, 1, "forward"
    )
    mixed_full = lax.all_to_all(from_blocks(mixed), "cols", split_axis=1, concat_axis=0, tiled=True)
    aggregated = lax.dot_general(
        weight, mixed_full, (((0,), (0,)), ((), ())), preferred_element_type=jnp.float32
    ).astype(jnp.bfloat16)
    aggregated = lax.all_to_all(aggregated, "cols", split_axis=0, concat_axis=1, tiled=True)
    grad_weight = total_of_all(
        lax.dot_general(
            mixed_full, grad_full, (((1,), (1,)), ((), ())), preferred_element_type=jnp.float32
        )
    )
    return (aggregated, grad_features, grad_weight)


def solution(mesh):
    torus = Mesh(mesh.devices.reshape(8, 4, 8), ("z", "x", "cols"))
    rows = ("z", "x")
    placed = (
        P("cols", rows),
        P(),
        P(rows, None, None),
        P(rows),
        P(rows),
        P(rows),
        P("cols", rows),
    )
    return jax.shard_map(
        on_device,
        mesh=torus,
        in_specs=placed,
        out_specs=(P("cols", rows), P("cols", rows), P()),
        check_vma=False,
    )
```

time: 932 us -> 289 us (0.31)
  waiting for transfers between devices: 551 us -> 113 us
  other arithmetic: 226 us -> 7.45 us
  Pallas kernels: 0 us -> 72.8 us
  matrix products: 54.5 us -> 2.17 us
  local copies, waits for them, and re-layouts: 56.2 us -> 11.1 us
  blocking collectives: 0 us -> 22.2 us
  starting transfers between devices: 25.4 us -> 41.1 us
    psum x1 -> x0, waiting for transfers between devices: 241 us -> none  [on_device(): grad_weight = lax.psum(weight_term, ('rows', 'cols'))]
    scatter-add x2 -> x0, other arithmetic: 223 us -> none  [the longest x1 134 us: on_device(): spread = jax.ops.segment_sum(reverse, tile_cols, total_blocks)]
    reduce_scatter x1 -> x0, waiting for transfers between devices: 221 us -> none  [on_device(): lax.psum_scatter(spread, 'rows', scatter_dimension=1, tiled=True)]
    all_gather x1, waiting for transfers between devices: 88.5 us -> 0.01 us  [on_device(): panel = lax.all_gather(to_blocks(features), ('z', 'x'), axis=0, tiled=True)]
    ppermute x0 -> x13, waiting for transfers between devices: none -> 79.1 us  [ring(): return lax.ppermute(a, (axis, 'cols'), moves)]
    pallas_call x0 -> x2, Pallas kernels: none -> 72.8 us  [tile_pass(): pl.pallas_call(functools.partial(body, tb=TB), out_shape=out, grid_spec=p...]
    dot_general x4 -> x2, matrix products: 53.6 us -> 1.24 us  [the longest x1 0.98 us: on_device(): lax.dot_general(weight, mixed_full, (((0,), (0,)), ((), ())), preferred_e...]
    all_to_all x4 -> x6, waiting for transfers between devices: 0.01 us -> 33.6 us  [the longest x3 16.1 us: exchange(): return lax.all_to_all(parts, axis, split_axis=0, concat_axis=0, tiled=True)]
  transfers between devices with their start and end apart: 7 -> 20, of which waited for: 3 -> 11; matrix products, arithmetic and copies ran while one was open for 35% -> 5% of each run, Pallas kernels for 0% -> 26%
where the time goes in v1:
time: 289 us; the launch traced here: 284 us
  waiting for transfers between devices  113 us (39%)
  Pallas kernels  72.8 us (25%)
  starting transfers between devices  41.1 us (14%)
  blocking collectives  22.2 us (8%)
  between operations  14.9 us (5%)
  local copies, waits for them, and re-layouts  11.1 us (4%)
  other arithmetic  7.45 us (3%)
    ppermute x13, waiting for transfers between devices, ring(): return lax.ppermute(a, (axis, 'cols'), moves)  79.1 us
    pallas_call x2, Pallas kernels, tile_pass(): pl.pallas_call(functools.partial(body, tb=TB), out_shape=out, grid_spec=p...  72.8 us
    all_to_all x3, waiting for transfers between devices, exchange(): return lax.all_to_all(parts, axis, split_axis=0, concat_axis=0, tiled=True)  16.1 us
    all_to_all x3, starting transfers between devices, exchange(): return lax.all_to_all(parts, axis, split_axis=0, concat_axis=0, tiled=True)  13.2 us
    all_to_all x1, blocking collectives, on_device(): lax.all_to_all(cotangent, 'cols', split_axis=1, concat_axis=0, tiled=True)  12.3 us
    all_to_all x1, blocking collectives, exchange(): return lax.all_to_all(parts, axis, split_axis=0, concat_axis=0, tiled=True)  9.94 us
    ppermute x13, starting transfers between devices, ring(): return lax.ppermute(a, (axis, 'cols'), moves)  9.75 us
    all_to_all x1, starting transfers between devices, on_device(): lax.all_to_all(from_blocks(mixed), 'cols', split_axis=1, concat_axis=0, t...  7.74 us
  transfers between devices with their start and end apart: 20, of which 11 were waited for; matrix products, arithmetic and copies ran while one was open for 5% of the time, Pallas kernels for 26%

profile of v1, /device:TPU:1, one launch (start us, length us, event | category | flops | bytes accessed | tf_op | source)
XLA Modules:
  0.0 284.4 jit_solution(13471166513176590983)
XLA Ops:
  7.2 1.0 copy.32
  8.2 0.8 copy.20
  9.1 1.0 copy.37
  10.1 12.3 %all_to_all.103 = bf16[32,8,512]{2,0,1:T(8,128)(2,1)S(1)} all-to-all(bf16[32,8,512]{2,0,1:T(8,128)(2,1)S(1)} %bitcast.54), channel_id=1, replica_groups=mesh['z'=8,'x'=4,'cols'=8] {'cols'}, dimensions={1} | all-to-all | bytes 524288 | tf_op jit(solution)/shard_map/all_to_all | solution.py:135
  22.3 0.9 convolution_convert_fusion
  23.3 4.4 %all-to-all-start.3 = ((bf16[8,32,512]{2,1,0:T(8,128)(2,1)}), bf16[8,32,512]{2,1,0:T(8,128)(2,1)S(1)}, u32[]{:S(2)}, u32[]{:S(2)}) async-start(bf16[8,32,512]{2,1,0:T(8,128)(2,1)} %bitcast.9), calls=%async_computation.3 | async-start | bytes 524288 | tf_op jit(solution)/shard_map/all_to_all | solution.py:137
  28.3 5.8 %all-to-all-done.3 = bf16[8,32,512]{2,1,0:T(8,128)(2,1)S(1)} async-done(((bf16[8,32,512]{2,1,0:T(8,128)(2,1)}), bf16[8,32,512]{2,1,0:T(8,128)(2,1)S(1)}, u32[]{:S(2)}, u32[]{:S(2)}) %all-to-all-start.3) | async-done | bytes 262176 | tf_op jit(solution)/shard_map/all_to_all | solution.py:137
  34.6 34.5 %reverse.1 = (bf16[128,32,128]{2,1,0:T(8,128)(2,1)S(1)}, bf16[128,32,128]{2,1,0:T(8,128)(2,1)S(1)}, bf16[128,32,128]{2,1,0:T(8,128)(2,1)S(1)}, bf16[128,32,128]{...) custom-call(s32[1024]{0:T(1024)S(1)} %copy-done.2, ...), custom_call_target="tpu_custom_call" | custom-call | flops 8589934592 | bytes 58720256 | tf_op jit(solution)/shard_map/reverse/pallas_call | solution.py:84
  69.1 1.5 collective-permute-start.5
  70.6 45.7 %collective-permute-done.3 = bf16[128,32,128]{2,1,0:T(8,128)(2,1)S(1)} collective-permute-done((bf16[128,32,128]{2,1,0:T(8,128)(2,1)S(1)}, bf16[128,32,128]{2,1,0:T(8,128)(2,1)S(1)}, u32[]{:S(2)}, u32[]{:S(2)}) %collective-permute-start.3) | collective-permute-done | bytes 1048608 | tf_op jit(solution)/shard_map/ppermute | solution.py:153
  116.3 0.3 add_convert_fusion
  116.6 0.3 collective-permute-start.4
  117.0 0.7 collective-permute-done.5
  117.7 17.8 %collective-permute-done.4 = bf16[128,32,128]{2,1,0:T(8,128)(2,1)S(1)} collective-permute-done((bf16[128,32,128]{2,1,0:T(8,128)(2,1)S(1)}, bf16[128,32,128]{2,1,0:T(8,128)(2,1)S(1)}, u32[]{:S(2)}, u32[]{:S(2)}) %collective-permute-start.4) | collective-permute-done | bytes 1048608 | tf_op jit(solution)/shard_map/ppermute | solution.py:153
  135.6 1.4 collective-permute-start.6
  137.0 4.3 %collective-permute-done.6 = bf16[32,32,128]{2,1,0:T(8,128)(2,1)S(1)} collective-permute-done((bf16[32,32,128]{2,1,0:T(8,128)(2,1)S(1)}, bf16[32,32,128]{2,1,0:T(8,128)(2,1)S(1)}, u32[]{:S(2)}, u32[]{:S(2)}) %collective-permute-start.6) | collective-permute-done | bytes 262176 | tf_op jit(solution)/shard_map/ppermute | solution.py:153
  141.3 0.9 add_convert_fusion.8
  142.3 10.6 %collective-permute-done = bf16[128,32,128]{2,1,0:T(8,128)(2,1)S(1)} collective-permute-done((bf16[128,32,128]{2,1,0:T(8,128)(2,1)S(1)}, bf16[128,32,128]{2,1,0:T(8,128)(2,1)S(1)}, u32[]{:S(2)}, u32[]{:S(2)}) %collective-permute-start) | collective-permute-done | bytes 1048608 | tf_op jit(solution)/shard_map/ppermute | solution.py:153
  152.9 1.2 add_convert_fusion.1
  154.1 1.4 collective-permute-start.1
  155.7 2.2 collective-permute-start.11
  157.8 3.4 %copy-done.1 = bf16[1024,32,128]{2,1,0:T(8,128)(2,1)S(1)} copy-done((bf16[1024,32,128]{2,1,0:T(8,128)(2,1)S(1)}, bf16[1024,32,128]{2,1,0:T(8,128)(2,1)}, u32[]{:S(2)}) %copy-start.1) | copy-done | bytes 8388632
  161.2 38.4 %forward.1 = bf16[32,32,128]{2,1,0:T(8,128)(2,1)S(1)} custom-call(s32[1024]{0:T(1024)S(1)} %copy-done.2, s32[1024]{0:T(1024)S(1)} %copy-done.3, s32[1]{0:T(128)S(6)} %copy.41.count_ref, bf16[1024,32,128]{2,1,0:T(8,128)(2,1)S(1)} %copy-done.1, bf16[1024,128,128]{2,1,0:T(8,128)(2,1)} %tiles_ref.3), custom_call_target="tpu_custom_call" | custom-call | flops 8589934592 | bytes 34340864 | tf_op jit(solution)/shard_map/forward/pallas_call | solution.py:84
  199.7 0.2 all_to_all.74
  199.9 0.8 copy.22
  200.6 7.7 %all-to-all-start = ((bf16[32,8,512]{2,0,1:T(8,128)(2,1)}), bf16[32,8,512]{2,0,1:T(8,128)(2,1)S(1)}, u32[]{:S(2)}, u32[]{:S(2)}) async-start(bf16[32,8,512]{2,0,1:T(8,128)(2,1)} %copy.22), calls=%async_computation | async-start | bytes 524288 | tf_op jit(solution)/shard_map/all_to_all | solution.py:177
  208.4 1.3 add_convert_fusion.7
  209.7 5.1 %all-to-all-done = bf16[32,8,512]{2,0,1:T(8,128)(2,1)S(1)} async-done(((bf16[32,8,512]{2,0,1:T(8,128)(2,1)}), bf16[32,8,512]{2,0,1:T(8,128)(2,1)S(1)}, u32[]{:S(2)}, u32[]{:S(2)}) %all-to-all-start) | async-done | bytes 262176 | tf_op jit(solution)/shard_map/all_to_all | solution.py:177
  214.9 0.3 fusion.1
  215.2 9.9 %all_to_all.104 = f32[8,32,256]{2,1,0:T(8,128)S(1)} all-to-all(f32[8,32,256]{2,1,0:T(8,128)S(1)} %fusion.1), channel_id=1, replica_groups=mesh['z'=8,'x'=4,'cols'=8] {'cols'}, dimensions={0} | all-to-all | bytes 524288 | tf_op jit(solution)/shard_map/all_to_all | solution.py:108
  225.1 0.6 all_to_all.90
  225.8 4.1 %all-to-all-start.5 = ((f32[32,1,256]{2,1,0:T(1,128)}), f32[32,1,256]{2,1,0:T(1,128)S(1)}, u32[]{:S(2)}, u32[]{:S(2)}) async-start(f32[32,1,256]{2,1,0:T(1,128)} %all_to_all.90), calls=%async_computation.5 | async-start | bytes 65536 | tf_op jit(solution)/shard_map/all_to_all | solution.py:108
  229.9 1.5 add_convert_fusion.6
  231.4 1.3 collective-permute-start.12
  232.7 1.4 collective-permute-start.9
  234.1 4.5 %all-to-all-done.5 = f32[32,1,256]{2,1,0:T(1,128)S(1)} async-done(((f32[32,1,256]{2,1,0:T(1,128)}), f32[32,1,256]{2,1,0:T(1,128)S(1)}, u32[]{:S(2)}, u32[]{:S(2)}) %all-to-all-start.5) | async-done | bytes 32800 | tf_op jit(solution)/shard_map/all_to_all | solution.py:108
  238.7 0.6 tile.6
  239.3 4.7 %all-to-all-start.6 = ((f32[32,1,256]{2,1,0:T(1,128)}), f32[32,1,256]{2,1,0:T(1,128)S(1)}, u32[]{:S(2)}, u32[]{:S(2)}) async-start(f32[32,1,256]{2,1,0:T(1,128)} %tile.6), calls=%async_computation.6 | async-start | bytes 65536 | tf_op jit(solution)/shard_map/all_to_all | solution.py:108
  244.0 1.0 convolution_convert_fusion.1
  245.0 7.7 %all-to-all-done.6 = f32[32,1,256]{2,1,0:T(1,128)S(1)} async-done(((f32[32,1,256]{2,1,0:T(1,128)}), f32[32,1,256]{2,1,0:T(1,128)S(1)}, u32[]{:S(2)}, u32[]{:S(2)}) %all-to-all-start.6) | async-done | bytes 32800 | tf_op jit(solution)/shard_map/all_to_all | solution.py:108
  252.7 6.0 %all-to-all-start.1 = ((bf16[8,32,512]{2,1,0:T(8,128)(2,1)}), bf16[8,32,512]{2,1,0:T(8,128)(2,1)S(1)}, u32[]{:S(2)}, u32[]{:S(2)}) async-start(bf16[8,32,512]{2,1,0:T(8,128)(2,1)} %bitcast.5), calls=%async_computation.1 | async-start | bytes 524288 | tf_op jit(solution)/shard_map/all_to_all | solution.py:181
  258.7 6.5 %all-to-all-done.1 = bf16[8,32,512]{2,1,0:T(8,128)(2,1)S(1)} async-done(((bf16[8,32,512]{2,1,0:T(8,128)(2,1)}), bf16[8,32,512]{2,1,0:T(8,128)(2,1)S(1)}, u32[]{:S(2)}, u32[]{:S(2)}) %all-to-all-start.1) | async-done | bytes 262176 | tf_op jit(solution)/shard_map/all_to_all | solution.py:181
  265.3 0.7 tile.8
  266.0 4.4 %all-to-all-start.7 = ((f32[8,32,256]{2,1,0:T(8,128)}), f32[8,32,256]{2,1,0:T(8,128)S(1)}, u32[]{:S(2)}, u32[]{:S(2)}) async-start(f32[8,32,256]{2,1,0:T(8,128)} %tile.8), calls=%async_computation.7 | async-start | bytes 524288 | tf_op jit(solution)/shard_map/all_to_all | solution.py:108
  270.4 1.9 copy_bitcast_fusion
  272.2 0.7 copy.30
  273.0 3.9 %all-to-all-done.7 = f32[8,32,256]{2,1,0:T(8,128)S(1)} async-done(((f32[8,32,256]{2,1,0:T(8,128)}), f32[8,32,256]{2,1,0:T(8,128)S(1)}, u32[]{:S(2)}, u32[]{:S(2)}) %all-to-all-start.7) | async-done | bytes 262176 | tf_op jit(solution)/shard_map/all_to_all | solution.py:108
  276.9 0.7 copy.42
  (34 shorter events, 1.3 us)
Async XLA Ops:
  7.2 15.2 %copy-start = (bf16[256,256]{1,0:T(8,128)(2,1)S(1)}, bf16[256,256]{1,0:T(8,128)(2,1)}, u32[]{:S(2)}) copy-start(bf16[256,256]{1,0:T(8,128)(2,1)} %param.8) | copy-start | bytes 393220
  7.2 21.1 %copy-start.3 = (s32[1024]{0:T(1024)S(1)}, s32[1024]{0:T(1024)}, u32[]{:S(2)}) copy-start(s32[1024]{0:T(1024)} %cols_ref.1) | copy-start | bytes 12292
  7.2 150.6 %all-gather.2.cloned.1.call-start = ((), (), s32[]{:S(2)}) async-start(), calls=%async_computation.8 | async-start | bytes 8650752 | tf_op jit(solution)/shard_map/all_gather | solution.py:133
  9.1 25.5 %copy-start.2 = (s32[1024]{0:T(1024)S(1)}, s32[1024]{0:T(1024)}, u32[]{:S(2)}) copy-start(s32[1024]{0:T(1024)} %rows_ref.3) | copy-start | bytes 12292
  23.3 10.9 %all-to-all-start.3 = ((bf16[8,32,512]{2,1,0:T(8,128)(2,1)}), bf16[8,32,512]{2,1,0:T(8,128)(2,1)S(1)}, u32[]{:S(2)}, u32[]{:S(2)}) async-start(bf16[8,32,512]{2,1,0:T(8,128)(2,1)} %bitcast.9), calls=%async_computation.3 | async-start | bytes 524288 | tf_op jit(solution)/shard_map/all_to_all | solution.py:137
  69.1 47.3 %collective-permute-start.3 = (bf16[128,32,128]{2,1,0:T(8,128)(2,1)S(1)}, bf16[128,32,128]{2,1,0:T(8,128)(2,1)S(1)}, u32[]{:S(2)}, u32[]{:S(2)}) collective-permute-start(bf16[128,32,128]{2,1,0:T(8,128)(2,1)S(1)} %get-tuple-element.17), channel_id=1, source_target_pairs={{0,8},{1,25},{2,10},{3,27},{4,12},{5,29},{6,14},{7,31},{8,16},{9,1... | collective-permute-start | bytes 3145736 | tf_op jit(solution)/shard_map/ppermute | solution.py:153
  69.1 48.5 %collective-permute-start.5 = (bf16[128,32,128]{2,1,0:T(8,128)(2,1)S(1)}, bf16[128,32,128]{2,1,0:T(8,128)(2,1)S(1)}, u32[]{:S(2)}, u32[]{:S(2)}) collective-permute-start(bf16[128,32,128]{2,1,0:T(8,128)(2,1)S(1)} %get-tuple-element.18), channel_id=1, source_target_pairs={{0,24},{1,9},{2,26},{3,11},{4,28},{5,13},{6,30},{7,15},{8,0},{9,17... | collective-permute-start | bytes 3145736 | tf_op jit(solution)/shard_map/ppermute | solution.py:153
  116.6 18.9 %collective-permute-start.4 = (bf16[128,32,128]{2,1,0:T(8,128)(2,1)S(1)}, bf16[128,32,128]{2,1,0:T(8,128)(2,1)S(1)}, u32[]{:S(2)}, u32[]{:S(2)}) collective-permute-start(bf16[128,32,128]{2,1,0:T(8,128)(2,1)S(1)} %add_convert_fusion), channel_id=1, source_target_pairs={{0,8},{1,25},{2,10},{3,27},{4,12},{5,29},{6,14},{7,31},{8,16},{9,1... | collective-permute-start | bytes 3145736 | tf_op jit(solution)/shard_map/ppermute | solution.py:153
  116.9 35.9 %collective-permute-start = (bf16[128,32,128]{2,1,0:T(8,128)(2,1)S(1)}, bf16[128,32,128]{2,1,0:T(8,128)(2,1)S(1)}, u32[]{:S(2)}, u32[]{:S(2)}) collective-permute-start(bf16[128,32,128]{2,1,0:T(8,128)(2,1)S(1)} %get-tuple-element.13), channel_id=1, source_target_pairs={{0,8},{1,25},{2,10},{3,27},{4,12},{5,29},{6,14},{7,31},{8,16},{9,1... | collective-permute-start | bytes 3145736 | tf_op jit(solution)/shard_map/ppermute | solution.py:153
  135.6 5.7 %collective-permute-start.6 = (bf16[32,32,128]{2,1,0:T(8,128)(2,1)S(1)}, bf16[32,32,128]{2,1,0:T(8,128)(2,1)S(1)}, u32[]{:S(2)}, u32[]{:S(2)}) collective-permute-start(bf16[32,32,128]{2,1,0:T(8,128)(2,1)S(1)} %add_convert_fusion.9), channel_id=1, source_target_pairs={{0,32},{1,225},{2,34},{3,227},{4,36},{5,229},{6,38},{7,231},{32,64... | collective-permute-start | bytes 786440 | tf_op jit(solution)/shard_map/ppermute | solution.py:153
  137.0 71.4 %collective-permute-start.2 = (bf16[128,32,128]{2,1,0:T(8,128)(2,1)S(1)}, bf16[128,32,128]{2,1,0:T(8,128)(2,1)}, u32[]{:S(2)}, u32[]{:S(2)}) collective-permute-start(bf16[128,32,128]{2,1,0:T(8,128)(2,1)S(1)} %get-tuple-element.14), channel_id=1, source_target_pairs={{0,24},{1,9},{2,26},{3,11},{4,28},{5,13},{6,30},{7,15},{8,0},{9,17... | collective-permute-start | bytes 3145736 | tf_op jit(solution)/shard_map/ppermute | solution.py:153
  142.3 13.2 %collective-permute-start.10 = (bf16[32,32,128]{2,1,0:T(8,128)(2,1)S(1)}, bf16[32,32,128]{2,1,0:T(8,128)(2,1)S(1)}, u32[]{:S(2)}, u32[]{:S(2)}) collective-permute-start(bf16[32,32,128]{2,1,0:T(8,128)(2,1)S(1)} %get-tuple-element.22), channel_id=1, source_target_pairs={{0,224},{1,33},{2,226},{3,35},{4,228},{5,37},{6,230},{7,39},{32,0}... | collective-permute-start | bytes 786440 | tf_op jit(solution)/shard_map/ppermute | solution.py:153
  154.1 54.3 %collective-permute-start.1 = (bf16[128,32,128]{2,1,0:T(8,128)(2,1)}, bf16[128,32,128]{2,1,0:T(8,128)(2,1)}, u32[]{:S(2)}, u32[]{:S(2)}) collective-permute-start(bf16[128,32,128]{2,1,0:T(8,128)(2,1)} %add_convert_fusion.1), channel_id=1, source_target_pairs={{0,8},{1,25},{2,10},{3,27},{4,12},{5,29},{6,14},{7,31},{8,16},{9,1... | collective-permute-start | bytes 3145736 | tf_op jit(solution)/shard_map/ppermute | solution.py:153
  155.5 52.9 %collective-permute-start.7 = (bf16[32,32,128]{2,1,0:T(8,128)(2,1)}, bf16[32,32,128]{2,1,0:T(8,128)(2,1)}, u32[]{:S(2)}, u32[]{:S(2)}) collective-permute-start(bf16[32,32,128]{2,1,0:T(8,128)(2,1)} %get-tuple-element.21), channel_id=1, source_target_pairs={{0,32},{1,225},{2,34},{3,227},{4,36},{5,229},{6,38},{7,231},{32,64... | collective-permute-start | bytes 786440 | tf_op jit(solution)/shard_map/ppermute | solution.py:153
  155.7 74.2 %collective-permute-start.11 = (bf16[32,32,128]{2,1,0:T(8,128)(2,1)S(1)}, bf16[32,32,128]{2,1,0:T(8,128)(2,1)S(1)}, u32[]{:S(2)}, u32[]{:S(2)}) collective-permute-start(bf16[32,32,128]{2,1,0:T(8,128)(2,1)S(1)} %add_convert_fusion.4), channel_id=1, source_target_pairs={{0,224},{1,33},{2,226},{3,35},{4,228},{5,37},{6,230},{7,39},{32,0}... | collective-permute-start | bytes 786440 | tf_op jit(solution)/shard_map/ppermute | solution.py:153
  157.8 3.4 %copy-start.1 = (bf16[1024,32,128]{2,1,0:T(8,128)(2,1)S(1)}, bf16[1024,32,128]{2,1,0:T(8,128)(2,1)}, u32[]{:S(2)}) copy-start(bf16[1024,32,128]{2,1,0:T(8,128)(2,1)} %all-gather.2.cloned.1.call-done.panel_ref) | copy-start | bytes 25165828
  200.6 14.2 %all-to-all-start = ((bf16[32,8,512]{2,0,1:T(8,128)(2,1)}), bf16[32,8,512]{2,0,1:T(8,128)(2,1)S(1)}, u32[]{:S(2)}, u32[]{:S(2)}) async-start(bf16[32,8,512]{2,0,1:T(8,128)(2,1)} %copy.22), calls=%async_computation | async-start | bytes 524288 | tf_op jit(solution)/shard_map/all_to_all | solution.py:177
  209.7 20.2 %collective-permute-start.8 = (bf16[32,32,128]{2,1,0:T(8,128)(2,1)S(1)}, bf16[32,32,128]{2,1,0:T(8,128)(2,1)S(1)}, u32[]{:S(2)}, u32[]{:S(2)}) collective-permute-start(bf16[32,32,128]{2,1,0:T(8,128)(2,1)S(1)} %add_convert_fusion.7), channel_id=1, source_target_pairs={{0,32},{1,225},{2,34},{3,227},{4,36},{5,229},{6,38},{7,231},{32,64... | collective-permute-start | bytes 786440 | tf_op jit(solution)/shard_map/ppermute | solution.py:153
  225.8 12.9 %all-to-all-start.5 = ((f32[32,1,256]{2,1,0:T(1,128)}), f32[32,1,256]{2,1,0:T(1,128)S(1)}, u32[]{:S(2)}, u32[]{:S(2)}) async-start(f32[32,1,256]{2,1,0:T(1,128)} %all_to_all.90), calls=%async_computation.5 | async-start | bytes 65536 | tf_op jit(solution)/shard_map/all_to_all | solution.py:108
  231.4 39.0 %collective-permute-start.12 = (bf16[32,32,128]{2,1,0:T(8,128)(2,1)S(1)}, bf16[32,32,128]{2,1,0:T(8,128)(2,1)S(1)}, u32[]{:S(2)}, u32[]{:S(2)}) collective-permute-start(bf16[32,32,128]{2,1,0:T(8,128)(2,1)S(1)} %get-tuple-element.20), channel_id=1, source_target_pairs={{0,224},{1,33},{2,226},{3,35},{4,228},{5,37},{6,230},{7,39},{32,0}... | collective-permute-start | bytes 786440 | tf_op jit(solution)/shard_map/ppermute | solution.py:153
  232.7 37.7 %collective-permute-start.9 = (bf16[32,32,128]{2,1,0:T(8,128)(2,1)S(1)}, bf16[32,32,128]{2,1,0:T(8,128)(2,1)S(1)}, u32[]{:S(2)}, u32[]{:S(2)}) collective-permute-start(bf16[32,32,128]{2,1,0:T(8,128)(2,1)S(1)} %get-tuple-element.19), channel_id=1, source_target_pairs={{0,32},{1,225},{2,34},{3,227},{4,36},{5,229},{6,38},{7,231},{32,64... | collective-permute-start | bytes 786440 | tf_op jit(solution)/shard_map/ppermute | solution.py:153
  239.3 13.4 %all-to-all-start.6 = ((f32[32,1,256]{2,1,0:T(1,128)}), f32[32,1,256]{2,1,0:T(1,128)S(1)}, u32[]{:S(2)}, u32[]{:S(2)}) async-start(f32[32,1,256]{2,1,0:T(1,128)} %tile.6), calls=%async_computation.6 | async-start | bytes 65536 | tf_op jit(solution)/shard_map/all_to_all | solution.py:108
  252.7 12.5 %all-to-all-start.1 = ((bf16[8,32,512]{2,1,0:T(8,128)(2,1)}), bf16[8,32,512]{2,1,0:T(8,128)(2,1)S(1)}, u32[]{:S(2)}, u32[]{:S(2)}) async-start(bf16[8,32,512]{2,1,0:T(8,128)(2,1)} %bitcast.5), calls=%async_computation.1 | async-start | bytes 524288 | tf_op jit(solution)/shard_map/all_to_all | solution.py:181
  266.0 10.9 %all-to-all-start.7 = ((f32[8,32,256]{2,1,0:T(8,128)}), f32[8,32,256]{2,1,0:T(8,128)S(1)}, u32[]{:S(2)}, u32[]{:S(2)}) async-start(f32[8,32,256]{2,1,0:T(8,128)} %tile.8), calls=%async_computation.7 | async-start | bytes 524288 | tf_op jit(solution)/shard_map/all_to_all | solution.py:108
Sparse Core Ops, SparseCore 0:
  11.2 128.2 all-gather.1

commit v2 on v1

v2 whole, which is shorter than its diff:
```python
import functools

import jax
import jax.numpy as jnp
from jax import lax
from jax.experimental import pallas as pl
from jax.experimental.pallas import tpu as pltpu
from jax.sharding import Mesh
from jax.sharding import PartitionSpec as P

TB = 128
STRIP = 16
MIB = 1024 * 1024


def zero(ref):
    @pl.loop(0, ref.shape[0] // 16)
    def _(i):
        ref[pl.ds(i * 16, 16)] = jnp.zeros((16,) + ref.shape[1:], ref.dtype)


def each_tile(count, tb, one):
    base = pl.program_id(0) * tb

    @pl.when(base + tb <= count)
    def _():
        for k in range(tb):
            one(base + k, k, None)

    @pl.when((base < count) & (base + tb > count))
    def _():
        @pl.loop(0, (count - base + STRIP - 1) // STRIP)
        def _(strip):
            for i in range(STRIP):
                k = strip * STRIP + i
                one(base + k, k, base + k < count)


def kept(term, used):
    return term if used is None else jnp.where(used, term, 0.0)


def reverse_body(rows_ref, places_ref, count_ref, grads_ref, tiles_ref, *rest, tb):
    outs, total = rest[:-1], rest[-1]

    @pl.when(pl.program_id(0) == 0)
    def _():
        zero(total)

    def one(slot, k, used):
        term = jnp.dot(grads_ref[rows_ref[slot]], tiles_ref[k], preferred_element_type=jnp.float32)
        total[places_ref[slot]] += kept(term, used)

    each_tile(count_ref[0], tb, one)

    @pl.when(pl.program_id(0) == pl.num_programs(0) - 1)
    def _():
        base = 0
        for out in outs:
            @pl.loop(0, out.shape[0] // 8)
            def _(j):
                out[pl.ds(j * 8, 8)] = total[pl.ds(base + j * 8, 8)].astype(out.dtype)

            base += out.shape[0]


def forward_body(rows_ref, cols_ref, count_ref, panel_ref, tiles_ref, out_ref, total, *, tb):
    @pl.when(pl.program_id(0) == 0)
    def _():
        zero(total)

    def one(slot, k, used):
        term = lax.dot_general(
            panel_ref[cols_ref[slot]], tiles_ref[k], (((1,), (1,)), ((), ())),
            preferred_element_type=jnp.float32,
        )
        total[rows_ref[slot]] += kept(term, used)

    each_tile(count_ref[0], tb, one)

    @pl.when(pl.program_id(0) == pl.num_programs(0) - 1)
    def _():
        out_ref[...] = total[...].astype(out_ref.dtype)


def tile_pass(body, rows, places, count, resident, tiles, outs, name):
    slots, side, _ = tiles.shape
    narrow = resident.shape[1]

    def fetch(i, rows_ref, places_ref, count_ref):
        return (jnp.minimum(i, jnp.maximum((count_ref[0] + TB - 1) // TB - 1, 0)), 0, 0)

    total = sum(outs)
    return pl.pallas_call(
        functools.partial(body, tb=TB),
        out_shape=[jax.ShapeDtypeStruct((n, narrow, side), jnp.bfloat16) for n in outs],
        grid_spec=pltpu.PrefetchScalarGridSpec(
            num_scalar_prefetch=3,
            grid=(slots // TB,),
            in_specs=[pl.BlockSpec(memory_space=pltpu.VMEM), pl.BlockSpec((TB, side, side), fetch)],
            out_specs=[pl.BlockSpec(memory_space=pltpu.VMEM)] * len(outs),
            scratch_shapes=[pltpu.VMEM((total, narrow, side), jnp.float32)],
        ),
        compiler_params=pltpu.CompilerParams(vmem_limit_bytes=40 * MIB),
        cost_estimate=pl.CostEstimate(
            flops=16 * slots * narrow * side * side,
            bytes_accessed=2 * slots * side * side + 2 * (total + resident.shape[0]) * narrow * side,
            transcendentals=0,
        ),
        name=name,
    )(rows, places, count, resident, tiles)


def exchange(parts, axis):
    return lax.all_to_all(parts, axis, split_axis=0, concat_axis=0, tiled=True)


def together(*arrays):
    return lax.optimization_barrier(arrays)


def to_all(a, axis):
    return exchange(jnp.tile(a, (lax.axis_size(axis),) + (1,) * (a.ndim - 1)), axis)


def on_device(features, weight, adj_tiles, tile_rows, tile_cols, tile_count, cotangent):
    side = adj_tiles.shape[1]
    narrow, local_nodes = features.shape
    blocks = local_nodes // side
    nz, nx, nc = lax.axis_size("z"), lax.axis_size("x"), lax.axis_size("cols")
    z, x, c = lax.axis_index("z"), lax.axis_index("x"), lax.axis_index("cols")

    def to_blocks(a):
        return jnp.transpose(a.reshape(narrow, blocks, side), (1, 0, 2))

    def from_blocks(a):
        return jnp.transpose(a, (1, 0, 2)).reshape(narrow, local_nodes)

    turn = 1 - 2 * (c % 2)
    owner = tile_cols // blocks
    far_x = (turn * (owner % nx - x)) % nx
    far_z = (turn * (owner // nx - z)) % nz
    x_first = blocks // 2
    z_first = blocks - x_first
    inner = tile_cols % blocks
    place = jnp.where(
        inner < x_first,
        (far_x * nz + far_z) * x_first + inner,
        nx * nz * x_first + (far_z * nx + far_x) * z_first + inner - x_first,
    )
    def ring(a, axis, n, ahead):
        moves = [(i * nc + j, (i + ahead * (1 - 2 * (j % 2))) % n * nc + j) for i in range(n) for j in range(nc)]
        return lax.ppermute(a, (axis, "cols"), moves)

    panel = lax.all_gather(to_blocks(features), ("z", "x"), axis=0, tiled=True)

    per_col = weight.reshape(nc, narrow, nc, narrow)
    split = (nc, blocks // nc, narrow, side)
    whole = (blocks, narrow, side)
    turned = exchange(to_blocks(cotangent), "cols").reshape(split)
    turned = jnp.einsum("dgcf,cbfn->dbgn", per_col, turned, preferred_element_type=jnp.float32)
    turned = exchange(turned.astype(jnp.bfloat16).reshape(whole), "cols")
    turned, spread = together(turned, cotangent)
    grad_full = to_all(spread, "cols")
    terms = tile_pass(
        reverse_body, tile_rows, place, tile_count, turned, adj_tiles,
        (nz * x_first,) * nx + (nx * z_first,) * nz, "reverse",
    )

    def add(*terms):
        return sum(t.astype(jnp.float32) for t in terms)

    def narrowed(*terms):
        return add(*terms).astype(jnp.bfloat16)

    *terms, grad_full = together(*terms, grad_full)
    by_x, by_z = terms[:nx], terms[nx:]
    m2 = ring(by_x[2], "x", nx, 1)
    m3 = ring(by_x[3], "x", nx, -1)
    ahead, behind = ring(by_z[4], "z", nz, 1), ring(by_z[5], "z", nz, -1)
    ahead, behind = together(narrowed(by_z[3], ahead), narrowed(by_z[6], behind))
    ahead, behind = ring(ahead, "z", nz, 1), ring(behind, "z", nz, -1)
    m2, m3, ahead, behind = together(m2, m3, ahead, behind)

    m1 = ring(narrowed(by_x[1], m2), "x", nx, 1)
    ahead = ring(narrowed(by_z[2], ahead), "z", nz, 1)
    behind = ring(narrowed(by_z[7], behind), "z", nz, -1)
    m1, ahead, behind, count = together(m1, ahead, behind, tile_count)

    def held(*far):
        cut = slice(far[0] * x_first, (far[-1] + 1) * x_first)
        return by_x[0][cut], m1[cut], m3[cut]

    n34 = ring(narrowed(*held(3, 4)), "z", nz, 2)
    n56 = ring(narrowed(*held(5, 6)), "z", nz, -2)
    ahead = ring(narrowed(by_z[1], ahead), "z", nz, 1)
    (mixed,) = tile_pass(
        forward_body, tile_rows, tile_cols, count, panel, adj_tiles, (blocks,), "forward"
    )
    n34, n56, ahead, mixed = together(n34, n56, ahead, mixed)

    mixed_full = exchange(mixed, "cols").reshape(split)
    term = lax.dot_general(
        from_blocks(mixed), grad_full, (((1,), (1,)), ((), ())), preferred_element_type=jnp.float32
    )
    shares = to_all(term.astype(jnp.bfloat16)[None], ("z", "x"))
    n2 = ring(narrowed(*held(2), n34[x_first:]), "z", nz, 2)
    n1 = ring(narrowed(*held(1), n34[:x_first]), "z", nz, 1)
    n7 = ring(narrowed(*held(7), n56[:x_first]), "z", nz, -1)
    line = add(by_z[0], ahead, behind).reshape(nx, z_first, narrow, side)
    late = add(line[0], *(ring(narrowed(line[i]), "x", nx, (0, 1, 2, -1)[i]) for i in (1, 2, 3)))

    aggregated = jnp.einsum(
        "cfdg,cbfn->dbgn", per_col, mixed_full, preferred_element_type=jnp.float32
    ).astype(jnp.bfloat16)
    whole_term = shares.astype(jnp.float32).sum(0).reshape(narrow, -1, side).transpose(1, 0, 2)
    top = whole_term.astype(jnp.bfloat16)
    rest = (whole_term - top.astype(jnp.float32)).astype(jnp.bfloat16)
    for_all = jnp.broadcast_to(jnp.concatenate([top, rest], 0), (nc, 2 * top.shape[0], narrow, side))
    back = exchange(jnp.concatenate([aggregated, for_all], 1), "cols")
    n_own, n_top = split[1], top.shape[0]
    aggregated = from_blocks(back[:, :n_own].reshape(whole))
    top, rest = back[:, n_own:n_own + n_top], back[:, n_own + n_top:]
    grad_weight = add(top, rest).transpose(0, 2, 1, 3).reshape(nc * narrow, -1)

    soon = add(*held(0), n56[x_first:], n2, n1, n7)
    grad_features = from_blocks(jnp.concatenate([soon, late], 0).astype(jnp.bfloat16))
    return (aggregated, grad_features, grad_weight)


def solution(mesh):
    torus = Mesh(mesh.devices.reshape(8, 4, 8), ("z", "x", "cols"))
    rows = ("z", "x")
    placed = (
        P("cols", rows),
        P(),
        P(rows, None, None),
        P(rows),
        P(rows),
        P(rows),
        P("cols", rows),
    )
    return jax.shard_map(
        on_device,
        mesh=torus,
        in_specs=placed,
        out_specs=(P("cols", rows), P("cols", rows), P()),
        check_vma=False,
    )
```

time: 289 us -> 241 us (0.83); the launches traced: 284 us -> 240 us
  Pallas kernels: 72.8 us -> 30.1 us
  waiting for transfers between devices: 113 us -> 83.7 us
  starting transfers between devices: 41.1 us -> 62.8 us
  blocking collectives: 22.2 us -> 9.94 us
  local copies, waits for them, and re-layouts: 11.1 us -> 21.1 us
  other arithmetic: 7.45 us -> 14.2 us
    pallas_call x2, Pallas kernels: 72.8 us -> 30.1 us  [tile_pass(): pl.pallas_call(functools.partial(body, tb=TB), out_shape=[jax.ShapeDtypeS...]
    ppermute x13 -> x18, starting transfers between devices: 9.75 us -> 31.6 us  [ring(): return lax.ppermute(a, (axis, 'cols'), moves)]
    ppermute x13 -> x18, waiting for transfers between devices: 79.1 us -> 57.5 us  [ring(): return lax.ppermute(a, (axis, 'cols'), moves)]
    all_to_all x3 -> x0, starting transfers between devices: 18.1 us -> none  [the longest x1 7.74 us: on_device(): lax.all_to_all(from_blocks(mixed), 'cols', split_axis=1, concat_axis=0, t...]
    all_to_all x3 -> x5, starting transfers between devices: 13.2 us -> 31.2 us  [exchange(): return lax.all_to_all(parts, axis, split_axis=0, concat_axis=0, tiled=True)]
    all_to_all x3 -> x0, waiting for transfers between devices: 17.5 us -> none  [the longest x1 6.52 us: on_device(): lax.all_to_all(aggregated, 'cols', split_axis=0, concat_axis=1, tiled=True)]
    all_to_all x1 -> x0, blocking collectives: 12.3 us -> none  [on_device(): lax.all_to_all(cotangent, 'cols', split_axis=1, concat_axis=0, tiled=True)]
    all_to_all x3 -> x5, waiting for transfers between devices: 16.1 us -> 26.1 us  [exchange(): return lax.all_to_all(parts, axis, split_axis=0, concat_axis=0, tiled=True)]
  transfers between devices with their start and end apart: 20 -> 24, of which waited for: 11 -> 11; matrix products, arithmetic and copies ran while one was open for 5% -> 10% of each run, Pallas kernels for 26% -> 13%
where the time goes in v2:
time: 241 us; the launch traced here: 240 us
  waiting for transfers between devices  83.7 us (35%)
  starting transfers between devices  62.8 us (26%)
  Pallas kernels  30.1 us (12%)
  local copies, waits for them, and re-layouts  21.1 us (9%)
  between operations  15 us (6%)
  other arithmetic  14.2 us (6%)
  blocking collectives  9.94 us (4%)
  matrix products  3.01 us (1%)
    ppermute x18, waiting for transfers between devices, ring(): return lax.ppermute(a, (axis, 'cols'), moves)  57.5 us
    ppermute x18, starting transfers between devices, ring(): return lax.ppermute(a, (axis, 'cols'), moves)  31.6 us
    all_to_all x5, starting transfers between devices, exchange(): return lax.all_to_all(parts, axis, split_axis=0, concat_axis=0, tiled=True)  31.2 us
    pallas_call x2, Pallas kernels, tile_pass(): pl.pallas_call(functools.partial(body, tb=TB), out_shape=[jax.ShapeDtypeS...  30.1 us
    all_to_all x5, waiting for transfers between devices, exchange(): return lax.all_to_all(parts, axis, split_axis=0, concat_axis=0, tiled=True)  26.1 us
    unnamed x43, local copies, waits for them, and re-layouts  12.9 us
    all_to_all x1, blocking collectives, exchange(): return lax.all_to_all(parts, axis, split_axis=0, concat_axis=0, tiled=True)  9.94 us
    convert_element_type x8, other arithmetic, narrowed(): return add(*terms).astype(jnp.bfloat16)  9.38 us
  transfers between devices with their start and end apart: 24, of which 11 were waited for; matrix products, arithmetic and copies ran while one was open for 10% of the time, Pallas kernels for 13%

profile of v2, /device:TPU:1, one launch (start us, length us, event | category | flops | bytes accessed | tf_op | source)
XLA Modules:
  0.0 239.9 jit_solution(2310751994293505571)
XLA Ops:
  7.2 1.0 copy.76
  9.1 1.0 copy.75
  10.9 6.7 %all-to-all-start = ((bf16[32,32,128]{2,1,0:T(8,128)(2,1)}), bf16[32,32,128]{2,1,0:T(8,128)(2,1)S(1)}, u32[]{:S(2)}, u32[]{:S(2)}) async-start(bf16[32,32,128]{2,1,0:T(8,128)(2,1)} %copy.51), calls=%async_computation | async-start | bytes 524288 | tf_op jit(solution)/shard_map/all_to_all | solution.py:115
  17.8 6.3 %all-to-all-done = bf16[32,32,128]{2,1,0:T(8,128)(2,1)S(1)} async-done(((bf16[32,32,128]{2,1,0:T(8,128)(2,1)}), bf16[32,32,128]{2,1,0:T(8,128)(2,1)S(1)}, u32[]{:S(2)}, u32[]{:S(2)}) %all-to-all-start) | async-done | bytes 262176 | tf_op jit(solution)/shard_map/all_to_all | solution.py:115
  24.4 9.9 %all_to_all.34.grads_ref = bf16[32,32,128]{2,1,0:T(8,128)(2,1)S(1)} all-to-all(bf16[32,32,128]{2,1,0:T(8,128)(2,1)S(1)} %bitcast.76), channel_id=1, replica_groups=mesh['z'=8,'x'=4,'cols'=8] {'cols'}, dimensions={0} | all-to-all | bytes 524288 | tf_op jit(solution)/shard_map/all_to_all | solution.py:115
  34.4 1.7 tile.4
  36.0 5.4 %all-to-all-start.2 = ((bf16[8,32,4096]{2,1,0:T(8,128)(2,1)}), bf16[8,32,4096]{2,1,0:T(8,128)(2,1)}, u32[]{:S(2)}, u32[]{:S(2)}) async-start(bf16[8,32,4096]{2,1,0:T(8,128)(2,1)} %tile.4), calls=%async_computation.2 | async-start | bytes 4194304 | tf_op jit(solution)/shard_map/all_to_all | solution.py:115
  42.2 14.3 %reverse.1 = (bf16[128,32,128]{2,1,0:T(8,128)(2,1)S(1)}, bf16[128,32,128]{2,1,0:T(8,128)(2,1)S(1)}, bf16[128,32,128]{2,1,0:T(8,128)(2,1)S(1)}, bf16[128,32,128]{...) custom-call(s32[1024]{0:T(1024)S(1)} %copy-done.7, ...), custom_call_target="tpu_custom_call" | custom-call | flops 8589934592 | bytes 42205184 | tf_op jit(solution)/shard_map/reverse/pallas_call | solution.py:94
  59.7 1.0 copy-done.9
  60.7 1.0 copy-done.10
  63.2 4.7 %all-to-all-done.2 = bf16[8,32,4096]{2,1,0:T(8,128)(2,1)} async-done(((bf16[8,32,4096]{2,1,0:T(8,128)(2,1)}), bf16[8,32,4096]{2,1,0:T(8,128)(2,1)}, u32[]{:S(2)}, u32[]{:S(2)}) %all-to-all-start.2) | async-done | bytes 2097184 | tf_op jit(solution)/shard_map/all_to_all | solution.py:115
  67.9 5.5 %collective-permute-start.2 = (bf16[64,32,128]{2,1,0:T(8,128)(2,1)}, bf16[64,32,128]{2,1,0:T(8,128)(2,1)S(1)}, u32[]{:S(2)}, u32[]{:S(2)}) collective-permute-start(bf16[64,32,128]{2,1,0:T(8,128)(2,1)} %copy-done.12), channel_id=1, source_target_pairs={{0,32},{1,225},{2,34},{3,227},{4,36},{5,229},{6,38},{7,231},{32,64... | collective-permute-start | bytes 1572872 | tf_op jit(solution)/shard_map/ppermute | solution.py:153
  73.4 2.2 collective-permute-start
  75.7 18.9 %collective-permute-done.2 = bf16[64,32,128]{2,1,0:T(8,128)(2,1)S(1)} collective-permute-done((bf16[64,32,128]{2,1,0:T(8,128)(2,1)}, bf16[64,32,128]{2,1,0:T(8,128)(2,1)S(1)}, u32[]{:S(2)}, u32[]{:S(2)}) %collective-permute-start.2) | collective-permute-done | bytes 524320 | tf_op jit(solution)/shard_map/ppermute | solution.py:153
  94.6 1.2 add_convert_fusion.5
  95.8 2.0 collective-permute-done.3
  97.8 1.2 add_convert_fusion.4
  99.0 1.6 collective-permute-start.4
  100.5 17.6 %collective-permute-done.4 = bf16[64,32,128]{2,1,0:T(8,128)(2,1)S(1)} collective-permute-done((bf16[64,32,128]{2,1,0:T(8,128)(2,1)S(1)}, bf16[64,32,128]{2,1,0:T(8,128)(2,1)S(1)}, u32[]{:S(2)}, u32[]{:S(2)}) %collective-permute-start.4) | collective-permute-done | bytes 524320 | tf_op jit(solution)/shard_map/ppermute | solution.py:153
  118.2 4.3 %collective-permute-done.5 = bf16[64,32,128]{2,1,0:T(8,128)(2,1)S(1)} collective-permute-done((bf16[64,32,128]{2,1,0:T(8,128)(2,1)S(1)}, bf16[64,32,128]{2,1,0:T(8,128)(2,1)S(1)}, u32[]{:S(2)}, u32[]{:S(2)}) %collective-permute-start.5) | collective-permute-done | bytes 524320 | tf_op jit(solution)/shard_map/ppermute | solution.py:153
  122.4 2.0 collective-permute-done.1
  124.4 1.2 add_convert_fusion
  125.7 3.2 %collective-permute-start.6 = (bf16[128,32,128]{2,1,0:T(8,128)(2,1)}, bf16[128,32,128]{2,1,0:T(8,128)(2,1)}, u32[]{:S(2)}, u32[]{:S(2)}) collective-permute-start(bf16[128,32,128]{2,1,0:T(8,128)(2,1)} %add_convert_fusion), channel_id=1, source_target_pairs={{0,8},{1,25},{2,10},{3,27},{4,12},{5,29},{6,14},{7,31},{8,16},{9,1... | collective-permute-start | bytes 3145736 | tf_op jit(solution)/shard_map/ppermute | solution.py:153
  128.9 0.9 add_convert_fusion.3
  129.8 1.2 collective-permute-start.7
  131.0 0.9 add_convert_fusion.2
  132.3 1.2 copy.57
  133.5 11.3 %collective-permute-done.7 = bf16[64,32,128]{2,1,0:T(8,128)(2,1)S(1)} collective-permute-done((bf16[64,32,128]{2,1,0:T(8,128)(2,1)}, bf16[64,32,128]{2,1,0:T(8,128)(2,1)S(1)}, u32[]{:S(2)}, u32[]{:S(2)}) %collective-permute-start.7) | collective-permute-done | bytes 524320 | tf_op jit(solution)/shard_map/ppermute | solution.py:153
  144.7 1.4 collective-permute-done.8
  146.2 1.6 add_convert_fusion.6
  148.0 3.6 %collective-permute-start.9 = (bf16[32,32,128]{2,1,0:T(8,128)(2,1)S(1)}, bf16[32,32,128]{2,1,0:T(8,128)(2,1)S(1)}, u32[]{:S(2)}, u32[]{:S(2)}) collective-permute-start(bf16[32,32,128]{2,1,0:T(8,128)(2,1)S(1)} %get-tuple-element.93), channel_id=1, source_target_pairs={{0,64},{1,193},{2,66},{3,195},{4,68},{5,197},{6,70},{7,199},{32,96... | collective-permute-start | bytes 786440 | tf_op jit(solution)/shard_map/ppermute | solution.py:153
  151.9 3.4 %copy-done = bf16[1024,32,128]{2,1,0:T(8,128)(2,1)S(1)} copy-done((bf16[1024,32,128]{2,1,0:T(8,128)(2,1)S(1)}, bf16[1024,32,128]{2,1,0:T(8,128)(2,1)}, u32[]{:S(2)}) %copy-start) | copy-done | bytes 8388632
  155.2 15.8 %forward.1 = bf16[32,32,128]{2,1,0:T(8,128)(2,1)} custom-call(s32[1024]{0:T(1024)S(1)} %copy-done.7, s32[1024]{0:T(1024)S(1)} %copy-done.8, s32[1]{0:T(128)S(6)} %copy.95.count_ref, bf16[1024,32,128]{2,1,0:T(8,128)(2,1)S(1)} %copy-done, bf16[1024,128,128]{2,1,0:T(8,128)(2,1)} %tiles_ref.3), custom_call_target="tpu_custom_call" | custom-call | flops 8589934592 | bytes 42205184 | tf_op jit(solution)/shard_map/forward/pallas_call | solution.py:94
  171.1 5.0 %all-to-all-start.3 = ((bf16[32,32,128]{2,1,0:T(8,128)(2,1)}), bf16[32,32,128]{2,1,0:T(8,128)(2,1)S(1)}, u32[]{:S(2)}, u32[]{:S(2)}) async-start(bf16[32,32,128]{2,1,0:T(8,128)(2,1)} %forward.1), calls=%async_computation.3 | async-start | bytes 524288 | tf_op jit(solution)/shard_map/all_to_all | solution.py:115
  176.1 2.2 add_convert_fusion.11
  178.3 1.6 collective-permute-start.12
  179.9 6.8 %collective-permute-start.13 = (bf16[16,32,128]{2,1,0:T(8,128)(2,1)}, bf16[16,32,128]{2,1,0:T(8,128)(2,1)}, u32[]{:S(2)}, u32[]{:S(2)}) collective-permute-start(bf16[16,32,128]{2,1,0:T(8,128)(2,1)} %get-tuple-element.90), channel_id=1, source_target_pairs={{0,32},{1,225},{2,34},{3,227},{4,36},{5,229},{6,38},{7,231},{32,64... | collective-permute-start | bytes 393224 | tf_op jit(solution)/shard_map/ppermute | solution.py:153
  186.7 1.1 collective-permute-start.14
  187.8 2.4 %convolution_convert_fusion = bf16[32,256]{1,0:T(8,128)(2,1)S(1)} fusion(bf16[256,4096]{1,0:T(8,128)(2,1)} %bitcast.8, bf16[32,32,128]{2,1,0:T(8,128)(2,1)} %forward.1), kind=kOutput, calls=%fused_computation.7 | convolution fusion | flops 67117056 | bytes 2375680 | tf_op jit(solution)/shard_map/dot_general | solution.py:203
  191.1 6.3 %all-to-all-start.4 = ((bf16[32,32,256]{2,1,0:T(8,128)(2,1)}), bf16[32,32,256]{2,1,0:T(8,128)(2,1)S(1)}, u32[]{:S(2)}, u32[]{:S(2)}) async-start(bf16[32,32,256]{2,1,0:T(8,128)(2,1)} %tile.5), calls=%async_computation.4 | async-start | bytes 1048576 | tf_op jit(solution)/shard_map/all_to_all | solution.py:115
  197.5 1.5 fusion.25
  199.7 2.4 %collective-permute-start.15 = (bf16[16,32,128]{2,1,0:T(8,128)(2,1)}, bf16[16,32,128]{2,1,0:T(8,128)(2,1)S(1)}, u32[]{:S(2)}, u32[]{:S(2)}) collective-permute-start(bf16[16,32,128]{2,1,0:T(8,128)(2,1)} %get-tuple-element.94), channel_id=1, source_target_pairs={{0,8},{1,25},{2,10},{3,27},{4,12},{5,29},{6,14},{7,31},{8,16},{9,1... | collective-permute-start | bytes 393224 | tf_op jit(solution)/shard_map/ppermute | solution.py:153
  202.1 1.8 collective-permute-start.16
  203.9 1.3 add_convert_fusion.8
  205.6 7.4 %all-to-all-done.4 = bf16[32,32,256]{2,1,0:T(8,128)(2,1)S(1)} async-done(((bf16[32,32,256]{2,1,0:T(8,128)(2,1)}), bf16[32,32,256]{2,1,0:T(8,128)(2,1)S(1)}, u32[]{:S(2)}, u32[]{:S(2)}) %all-to-all-start.4) | async-done | bytes 524320 | tf_op jit(solution)/shard_map/all_to_all | solution.py:115
  214.1 7.7 %all-to-all-start.5 = ((bf16[8,8,32,128]{3,2,1,0:T(8,128)(2,1)}), bf16[8,8,32,128]{3,2,1,0:T(8,128)(2,1)S(1)}, u32[]{:S(2)}, u32[]{:S(2)}) async-start(bf16[8,8,32,128]{3,2,1,0:T(8,128)(2,1)} %copy.60), calls=%async_computation.5 | async-start | bytes 1048576 | tf_op jit(solution)/shard_map/all_to_all | solution.py:115
  221.9 1.0 fusion.11
  223.6 7.7 %all-to-all-done.5 = bf16[8,8,32,128]{3,2,1,0:T(8,128)(2,1)S(1)} async-done(((bf16[8,8,32,128]{3,2,1,0:T(8,128)(2,1)}), bf16[8,8,32,128]{3,2,1,0:T(8,128)(2,1)S(1)}, u32[]{:S(2)}, u32[]{:S(2)}) %all-to-all-start.5) | async-done | bytes 524320 | tf_op jit(solution)/shard_map/all_to_all | solution.py:115
  (83 shorter events, 13.4 us)
Async XLA Ops:
  7.2 10.4 %copy-start.19 = (bf16[256,256]{1,0:T(8,128)(2,1)S(1)}, bf16[256,256]{1,0:T(8,128)(2,1)}, u32[]{:S(2)}) copy-start(bf16[256,256]{1,0:T(8,128)(2,1)} %param.8) | copy-start | bytes 393220
  7.2 144.7 %all-gather.2.cloned.1.call-start = ((), (), s32[]{:S(2)}) async-start(), calls=%async_computation.6 | async-start | bytes 8650752 | tf_op jit(solution)/shard_map/all_gather | solution.py:155
  10.9 23.5 %copy-start.15 = (bf16[32,4096]{1,0:T(8,128)(2,1)S(1)}, bf16[32,4096]{1,0:T(8,128)(2,1)}, u32[]{:S(2)}) copy-start(bf16[32,4096]{1,0:T(8,128)(2,1)} %param.13) | copy-start | bytes 786436
  10.9 13.2 %all-to-all-start = ((bf16[32,32,128]{2,1,0:T(8,128)(2,1)}), bf16[32,32,128]{2,1,0:T(8,128)(2,1)S(1)}, u32[]{:S(2)}, u32[]{:S(2)}) async-start(bf16[32,32,128]{2,1,0:T(8,128)(2,1)} %copy.51), calls=%async_computation | async-start | bytes 524288 | tf_op jit(solution)/shard_map/all_to_all | solution.py:115
  17.8 18.2 %copy-start.13 = (bf16[8,32,8,32]{3,2,1,0:T(8,128)(2,1)}, bf16[8,32,8,32]{3,2,1,0:T(8,128)(2,1)S(1)}, u32[]{:S(2)}) copy-start(bf16[8,32,8,32]{3,2,1,0:T(8,128)(2,1)S(1)} %reshape.63) | copy-start | bytes 393220
  36.0 6.1 %copy-start.8 = (s32[1024]{0:T(1024)S(1)}, s32[1024]{0:T(1024)}, u32[]{:S(2)}) copy-start(s32[1024]{0:T(1024)} %cols_ref.1) | copy-start | bytes 12292
  36.0 6.1 %copy-start.7 = (s32[1024]{0:T(1024)S(1)}, s32[1024]{0:T(1024)}, u32[]{:S(2)}) copy-start(s32[1024]{0:T(1024)} %rows_ref.3) | copy-start | bytes 12292
  36.0 31.9 %all-to-all-start.2 = ((bf16[8,32,4096]{2,1,0:T(8,128)(2,1)}), bf16[8,32,4096]{2,1,0:T(8,128)(2,1)}, u32[]{:S(2)}, u32[]{:S(2)}) async-start(bf16[8,32,4096]{2,1,0:T(8,128)(2,1)} %tile.4), calls=%async_computation.2 | async-start | bytes 4194304 | tf_op jit(solution)/shard_map/all_to_all | solution.py:115
  56.5 0.8 copy-start.1
  57.3 0.8 copy-start.3
  58.1 0.8 copy-start.4
  58.9 0.8 copy-start.5
  59.7 1.0 copy-start.9
  60.7 1.0 copy-start.10
  61.6 0.8 copy-start.11
  62.4 0.8 copy-start.12
  67.9 26.7 %collective-permute-start.2 = (bf16[64,32,128]{2,1,0:T(8,128)(2,1)}, bf16[64,32,128]{2,1,0:T(8,128)(2,1)S(1)}, u32[]{:S(2)}, u32[]{:S(2)}) collective-permute-start(bf16[64,32,128]{2,1,0:T(8,128)(2,1)} %copy-done.12), channel_id=1, source_target_pairs={{0,32},{1,225},{2,34},{3,227},{4,36},{5,229},{6,38},{7,231},{32,64... | collective-permute-start | bytes 1572872 | tf_op jit(solution)/shard_map/ppermute | solution.py:153
  73.4 24.3 %collective-permute-start.3 = (bf16[64,32,128]{2,1,0:T(8,128)(2,1)}, bf16[64,32,128]{2,1,0:T(8,128)(2,1)S(1)}, u32[]{:S(2)}, u32[]{:S(2)}) collective-permute-start(bf16[64,32,128]{2,1,0:T(8,128)(2,1)} %copy-done.11), channel_id=1, source_target_pairs={{0,224},{1,33},{2,226},{3,35},{4,228},{5,37},{6,230},{7,39},{32,0}... | collective-permute-start | bytes 1572872 | tf_op jit(solution)/shard_map/ppermute | solution.py:153
  73.4 49.0 %collective-permute-start = (bf16[128,32,128]{2,1,0:T(8,128)(2,1)}, bf16[128,32,128]{2,1,0:T(8,128)(2,1)S(1)}, u32[]{:S(2)}, u32[]{:S(2)}) collective-permute-start(bf16[128,32,128]{2,1,0:T(8,128)(2,1)} %copy-done.10), channel_id=1, source_target_pairs={{0,8},{1,25},{2,10},{3,27},{4,12},{5,29},{6,14},{7,31},{8,16},{9,1... | collective-permute-start | bytes 3145736 | tf_op jit(solution)/shard_map/ppermute | solution.py:153
  75.7 48.8 %collective-permute-start.1 = (bf16[128,32,128]{2,1,0:T(8,128)(2,1)}, bf16[128,32,128]{2,1,0:T(8,128)(2,1)}, u32[]{:S(2)}, u32[]{:S(2)}) collective-permute-start(bf16[128,32,128]{2,1,0:T(8,128)(2,1)} %copy-done.9), channel_id=1, source_target_pairs={{0,24},{1,9},{2,26},{3,11},{4,28},{5,13},{6,30},{7,15},{8,0},{9,17... | collective-permute-start | bytes 3145736 | tf_op jit(solution)/shard_map/ppermute | solution.py:153
  95.8 33.1 %copy-start.2 = (bf16[64,32,128]{2,1,0:T(8,128)(2,1)S(1)}, bf16[64,32,128]{2,1,0:T(8,128)(2,1)}, u32[]{:S(2)}) copy-start(bf16[64,32,128]{2,1,0:T(8,128)(2,1)} %copy-done.1) | copy-start | bytes 1572868
  99.0 19.2 %collective-permute-start.4 = (bf16[64,32,128]{2,1,0:T(8,128)(2,1)S(1)}, bf16[64,32,128]{2,1,0:T(8,128)(2,1)S(1)}, u32[]{:S(2)}, u32[]{:S(2)}) collective-permute-start(bf16[64,32,128]{2,1,0:T(8,128)(2,1)S(1)} %add_convert_fusion.5), channel_id=1, source_target_pairs={{0,32},{1,225},{2,34},{3,227},{4,36},{5,229},{6,38},{7,231},{32,64... | collective-permute-start | bytes 1572872 | tf_op jit(solution)/shard_map/ppermute | solution.py:153
  100.5 21.9 %collective-permute-start.5 = (bf16[64,32,128]{2,1,0:T(8,128)(2,1)S(1)}, bf16[64,32,128]{2,1,0:T(8,128)(2,1)S(1)}, u32[]{:S(2)}, u32[]{:S(2)}) collective-permute-start(bf16[64,32,128]{2,1,0:T(8,128)(2,1)S(1)} %add_convert_fusion.4), channel_id=1, source_target_pairs={{0,224},{1,33},{2,226},{3,35},{4,228},{5,37},{6,230},{7,39},{32,0}... | collective-permute-start | bytes 1572872 | tf_op jit(solution)/shard_map/ppermute | solution.py:153
  125.7 6.6 %copy-start.14 = (bf16[8,32,8,32]{3,2,1,0:T(8,128)(2,1)S(1)}, bf16[8,32,8,32]{3,2,1,0:T(8,128)(2,1)}, u32[]{:S(2)}) copy-start(bf16[8,32,8,32]{3,2,1,0:T(8,128)(2,1)} %copy-done.13) | copy-start | bytes 393220
  125.7 20.5 %collective-permute-start.6 = (bf16[128,32,128]{2,1,0:T(8,128)(2,1)}, bf16[128,32,128]{2,1,0:T(8,128)(2,1)}, u32[]{:S(2)}, u32[]{:S(2)}) collective-permute-start(bf16[128,32,128]{2,1,0:T(8,128)(2,1)} %add_convert_fusion), channel_id=1, source_target_pairs={{0,8},{1,25},{2,10},{3,27},{4,12},{5,29},{6,14},{7,31},{8,16},{9,1... | collective-permute-start | bytes 3145736 | tf_op jit(solution)/shard_map/ppermute | solution.py:153
  129.8 14.9 %collective-permute-start.7 = (bf16[64,32,128]{2,1,0:T(8,128)(2,1)}, bf16[64,32,128]{2,1,0:T(8,128)(2,1)S(1)}, u32[]{:S(2)}, u32[]{:S(2)}) collective-permute-start(bf16[64,32,128]{2,1,0:T(8,128)(2,1)} %add_convert_fusion.3), channel_id=1, source_target_pairs={{0,32},{1,225},{2,34},{3,227},{4,36},{5,229},{6,38},{7,231},{32,64... | collective-permute-start | bytes 1572872 | tf_op jit(solution)/shard_map/ppermute | solution.py:153
  132.0 14.2 %collective-permute-start.8 = (bf16[64,32,128]{2,1,0:T(8,128)(2,1)}, bf16[64,32,128]{2,1,0:T(8,128)(2,1)S(1)}, u32[]{:S(2)}, u32[]{:S(2)}) collective-permute-start(bf16[64,32,128]{2,1,0:T(8,128)(2,1)} %add_convert_fusion.2), channel_id=1, source_target_pairs={{0,224},{1,33},{2,226},{3,35},{4,228},{5,37},{6,230},{7,39},{32,0}... | collective-permute-start | bytes 1572872 | tf_op jit(solution)/shard_map/ppermute | solution.py:153
  146.2 1.9 copy-start.17
  147.8 23.3 %collective-permute-start.10 = (bf16[32,32,128]{2,1,0:T(8,128)(2,1)S(1)}, bf16[32,32,128]{2,1,0:T(8,128)(2,1)}, u32[]{:S(2)}, u32[]{:S(2)}) collective-permute-start(bf16[32,32,128]{2,1,0:T(8,128)(2,1)S(1)} %get-tuple-element.92), channel_id=1, source_target_pairs={{0,192},{1,65},{2,194},{3,67},{4,196},{5,69},{6,198},{7,71},{32,22... | collective-permute-start | bytes 786440 | tf_op jit(solution)/shard_map/ppermute | solution.py:153
  148.0 23.0 %collective-permute-start.9 = (bf16[32,32,128]{2,1,0:T(8,128)(2,1)S(1)}, bf16[32,32,128]{2,1,0:T(8,128)(2,1)S(1)}, u32[]{:S(2)}, u32[]{:S(2)}) collective-permute-start(bf16[32,32,128]{2,1,0:T(8,128)(2,1)S(1)} %get-tuple-element.93), channel_id=1, source_target_pairs={{0,64},{1,193},{2,66},{3,195},{4,68},{5,197},{6,70},{7,199},{32,96... | collective-permute-start | bytes 786440 | tf_op jit(solution)/shard_map/ppermute | solution.py:153
  151.7 19.3 %collective-permute-start.11 = (bf16[64,32,128]{2,1,0:T(8,128)(2,1)S(1)}, bf16[64,32,128]{2,1,0:T(8,128)(2,1)S(1)}, u32[]{:S(2)}, u32[]{:S(2)}) collective-permute-start(bf16[64,32,128]{2,1,0:T(8,128)(2,1)S(1)} %add_convert_fusion.1), channel_id=1, source_target_pairs={{0,32},{1,225},{2,34},{3,227},{4,36},{5,229},{6,38},{7,231},{32,64... | collective-permute-start | bytes 1572872 | tf_op jit(solution)/shard_map/ppermute | solution.py:153
  151.9 3.4 %copy-start = (bf16[1024,32,128]{2,1,0:T(8,128)(2,1)S(1)}, bf16[1024,32,128]{2,1,0:T(8,128)(2,1)}, u32[]{:S(2)}) copy-start(bf16[1024,32,128]{2,1,0:T(8,128)(2,1)} %all-gather.2.cloned.1.call-done.panel_ref) | copy-start | bytes 25165828
  171.1 5.0 %copy-start.18 = (bf16[64,32,128]{2,1,0:T(8,128)(2,1)}, bf16[64,32,128]{2,1,0:T(8,128)(2,1)S(1)}, u32[]{:S(2)}) copy-start(bf16[64,32,128]{2,1,0:T(8,128)(2,1)S(1)} %collective-permute-done.11) | copy-start | bytes 1572868
  171.1 19.2 %all-to-all-start.3 = ((bf16[32,32,128]{2,1,0:T(8,128)(2,1)}), bf16[32,32,128]{2,1,0:T(8,128)(2,1)S(1)}, u32[]{:S(2)}, u32[]{:S(2)}) async-start(bf16[32,32,128]{2,1,0:T(8,128)(2,1)} %forward.1), calls=%async_computation.3 | async-start | bytes 524288 | tf_op jit(solution)/shard_map/all_to_all | solution.py:115
  178.3 19.1 %copy-start.6 = (bf16[64,32,128]{2,1,0:T(8,128)(2,1)S(1)}, bf16[64,32,128]{2,1,0:T(8,128)(2,1)}, u32[]{:S(2)}) copy-start(bf16[64,32,128]{2,1,0:T(8,128)(2,1)} %copy-done.5) | copy-start | bytes 1572868
  178.3 23.9 %collective-permute-start.12 = (bf16[16,32,128]{2,1,0:T(8,128)(2,1)}, bf16[16,32,128]{2,1,0:T(8,128)(2,1)}, u32[]{:S(2)}, u32[]{:S(2)}) collective-permute-start(bf16[16,32,128]{2,1,0:T(8,128)(2,1)} %get-tuple-element.89), channel_id=1, source_target_pairs={{0,64},{1,193},{2,66},{3,195},{4,68},{5,197},{6,70},{7,199},{32,96... | collective-permute-start | bytes 393224 | tf_op jit(solution)/shard_map/ppermute | solution.py:153
  179.9 24.0 %collective-permute-start.13 = (bf16[16,32,128]{2,1,0:T(8,128)(2,1)}, bf16[16,32,128]{2,1,0:T(8,128)(2,1)}, u32[]{:S(2)}, u32[]{:S(2)}) collective-permute-start(bf16[16,32,128]{2,1,0:T(8,128)(2,1)} %get-tuple-element.90), channel_id=1, source_target_pairs={{0,32},{1,225},{2,34},{3,227},{4,36},{5,229},{6,38},{7,231},{32,64... | collective-permute-start | bytes 393224 | tf_op jit(solution)/shard_map/ppermute | solution.py:153
  186.7 17.2 %collective-permute-start.14 = (bf16[16,32,128]{2,1,0:T(8,128)(2,1)}, bf16[16,32,128]{2,1,0:T(8,128)(2,1)}, u32[]{:S(2)}, u32[]{:S(2)}) collective-permute-start(bf16[16,32,128]{2,1,0:T(8,128)(2,1)} %get-tuple-element.91), channel_id=1, source_target_pairs={{0,224},{1,33},{2,226},{3,35},{4,228},{5,37},{6,230},{7,39},{32,0}... | collective-permute-start | bytes 393224 | tf_op jit(solution)/shard_map/ppermute | solution.py:153
  191.1 21.9 %all-to-all-start.4 = ((bf16[32,32,256]{2,1,0:T(8,128)(2,1)}), bf16[32,32,256]{2,1,0:T(8,128)(2,1)S(1)}, u32[]{:S(2)}, u32[]{:S(2)}) async-start(bf16[32,32,256]{2,1,0:T(8,128)(2,1)} %tile.5), calls=%async_computation.4 | async-start | bytes 1048576 | tf_op jit(solution)/shard_map/all_to_all | solution.py:115
  197.4 7.8 %copy-start.16 = (bf16[8,32,8,32]{1,3,0,2:T(8,128)(2,1)S(1)}, bf16[8,32,8,32]{1,3,0,2:T(8,128)(2,1)}, u32[]{:S(2)}) copy-start(bf16[8,32,8,32]{1,3,0,2:T(8,128)(2,1)} %copy.57) | copy-start | bytes 393220
  199.7 22.1 %collective-permute-start.15 = (bf16[16,32,128]{2,1,0:T(8,128)(2,1)}, bf16[16,32,128]{2,1,0:T(8,128)(2,1)S(1)}, u32[]{:S(2)}, u32[]{:S(2)}) collective-permute-start(bf16[16,32,128]{2,1,0:T(8,128)(2,1)} %get-tuple-element.94), channel_id=1, source_target_pairs={{0,8},{1,25},{2,10},{3,27},{4,12},{5,29},{6,14},{7,31},{8,16},{9,1... | collective-permute-start | bytes 393224 | tf_op jit(solution)/shard_map/ppermute | solution.py:153
  202.1 19.7 %collective-permute-start.17 = (bf16[16,32,128]{2,1,0:T(8,128)(2,1)}, bf16[16,32,128]{2,1,0:T(8,128)(2,1)}, u32[]{:S(2)}, u32[]{:S(2)}) collective-permute-start(bf16[16,32,128]{2,1,0:T(8,128)(2,1)} %get-tuple-element.95), channel_id=1, source_target_pairs={{0,24},{1,9},{2,26},{3,11},{4,28},{5,13},{6,30},{7,15},{8,0},{9,17... | collective-permute-start | bytes 393224 | tf_op jit(solution)/shard_map/ppermute | solution.py:153
  202.1 19.7 %collective-permute-start.16 = (bf16[16,32,128]{2,1,0:T(8,128)(2,1)}, bf16[16,32,128]{2,1,0:T(8,128)(2,1)}, u32[]{:S(2)}, u32[]{:S(2)}) collective-permute-start(bf16[16,32,128]{2,1,0:T(8,128)(2,1)} %get-tuple-element.96), channel_id=1, source_target_pairs={{0,16},{1,17},{2,18},{3,19},{4,20},{5,21},{6,22},{7,23},{8,24},{9,... | collective-permute-start | bytes 393224 | tf_op jit(solution)/shard_map/ppermute | solution.py:153
  214.1 17.2 %all-to-all-start.5 = ((bf16[8,8,32,128]{3,2,1,0:T(8,128)(2,1)}), bf16[8,8,32,128]{3,2,1,0:T(8,128)(2,1)S(1)}, u32[]{:S(2)}, u32[]{:S(2)}) async-start(bf16[8,8,32,128]{3,2,1,0:T(8,128)(2,1)} %copy.60), calls=%async_computation.5 | async-start | bytes 1048576 | tf_op jit(solution)/shard_map/all_to_all | solution.py:115
Sparse Core Ops, SparseCore 0:
  11.2 125.7 all-gather.1

commit v3 on v2

--- a/solution.py
+++ b/solution.py
@@ -64,14 +64,24 @@
             base += out.shape[0]
 
 
-def forward_body(rows_ref, cols_ref, count_ref, panel_ref, tiles_ref, out_ref, total, *, tb):
+def forward_body(rows_ref, places_ref, count_ref, *rest, tb, pieces):
+    parts, (tiles_ref, out_ref, total, panel, sems) = rest[:pieces], rest[pieces:]
+
     @pl.when(pl.program_id(0) == 0)
     def _():
+        base, copies = 0, []
+        for i, part in enumerate(parts):
+            copies.append(pltpu.make_async_copy(part, panel.at[pl.ds(base, part.shape[0])], sems.at[i]))
+            base += part.shape[0]
+        for copy in copies:
+            copy.start()
         zero(total)
+        for copy in copies:
+            copy.wait()
 
     def one(slot, k, used):
         term = lax.dot_general(
-            panel_ref[cols_ref[slot]], tiles_ref[k], (((1,), (1,)), ((), ())),
+            panel[places_ref[slot]], tiles_ref[k], (((1,), (1,)), ((), ())),
             preferred_element_type=jnp.float32,
         )
         total[rows_ref[slot]] += kept(term, used)
@@ -83,32 +93,31 @@
         out_ref[...] = total[...].astype(out_ref.dtype)
 
 
-def tile_pass(body, rows, places, count, resident, tiles, outs, name):
+def tile_pass(body, rows, places, count, resident, resident_spec, tiles, outs, scratch, room, name):
     slots, side, _ = tiles.shape
-    narrow = resident.shape[1]
+    narrow = resident[0].shape[1]
 
     def fetch(i, rows_ref, places_ref, count_ref):
         return (jnp.minimum(i, jnp.maximum((count_ref[0] + TB - 1) // TB - 1, 0)), 0, 0)
 
     total = sum(outs)
+    moved = 2 * (slots * side * side + (total + sum(r.shape[0] for r in resident)) * narrow * side)
     return pl.pallas_call(
-        functools.partial(body, tb=TB),
+        body,
         out_shape=[jax.ShapeDtypeStruct((n, narrow, side), jnp.bfloat16) for n in outs],
         grid_spec=pltpu.PrefetchScalarGridSpec(
             num_scalar_prefetch=3,
             grid=(slots // TB,),
-            in_specs=[pl.BlockSpec(memory_space=pltpu.VMEM), pl.BlockSpec((TB, side, side), fetch)],
+            in_specs=[resident_spec] * len(resident) + [pl.BlockSpec((TB, side, side), fetch)],
             out_specs=[pl.BlockSpec(memory_space=pltpu.VMEM)] * len(outs),
-            scratch_shapes=[pltpu.VMEM((total, narrow, side), jnp.float32)],
+            scratch_shapes=[pltpu.VMEM((total, narrow, side), jnp.float32)] + scratch,
         ),
-        compiler_params=pltpu.CompilerParams(vmem_limit_bytes=40 * MIB),
+        compiler_params=pltpu.CompilerParams(vmem_limit_bytes=room * MIB),
         cost_estimate=pl.CostEstimate(
-            flops=16 * slots * narrow * side * side,
-            bytes_accessed=2 * slots * side * side + 2 * (total + resident.shape[0]) * narrow * side,
-            transcendentals=0,
+            flops=16 * slots * narrow * side * side, bytes_accessed=moved, transcendentals=0
         ),
         name=name,
-    )(rows, places, count, resident, tiles)
+    )(rows, places, count, *resident, tiles)
 
 
 def exchange(parts, axis):
@@ -136,56 +145,90 @@
     def from_blocks(a):
         return jnp.transpose(a, (1, 0, 2)).reshape(narrow, local_nodes)
 
+    def ring(a, axis, n, ahead):
+        moves = [(i * nc + j, (i + ahead * (1 - 2 * (j % 2))) % n * nc + j) for i in range(n) for j in range(nc)]
+        return lax.ppermute(a, (axis, "cols"), moves)
+
+    def add(*terms):
+        return sum(t.astype(jnp.float32) for t in terms)
+
+    def narrowed(*terms):
+        return add(*terms).astype(jnp.bfloat16)
+
     turn = 1 - 2 * (c % 2)
     owner = tile_cols // blocks
     far_x = (turn * (owner % nx - x)) % nx
     far_z = (turn * (owner // nx - z)) % nz
+    inner = tile_cols % blocks
+    most = blocks * 5 // 8
+    few = blocks - most
+    source = jnp.where(
+        inner < most, owner * most + inner, nz * nx * most + (far_z * nx + far_x) * few + inner - most
+    )
     x_first = blocks // 2
     z_first = blocks - x_first
-    inner = tile_cols % blocks
     place = jnp.where(
         inner < x_first,
         (far_x * nz + far_z) * x_first + inner,
         nx * nz * x_first + (far_z * nx + far_x) * z_first + inner - x_first,
     )
-    def ring(a, axis, n, ahead):
-        moves = [(i * nc + j, (i + ahead * (1 - 2 * (j % 2))) % n * nc + j) for i in range(n) for j in range(nc)]
-        return lax.ppermute(a, (axis, "cols"), moves)
-
-    panel = lax.all_gather(to_blocks(features), ("z", "x"), axis=0, tiled=True)
+
+    mine = to_blocks(features)
+    gathered = lax.all_gather(mine[:most], ("z", "x"), axis=0, tiled=True)
+    s1, s2, s3 = (ring(mine[most:], "x", nx, step) for step in (1, 2, -1))
 
     per_col = weight.reshape(nc, narrow, nc, narrow)
     split = (nc, blocks // nc, narrow, side)
     whole = (blocks, narrow, side)
     turned = exchange(to_blocks(cotangent), "cols").reshape(split)
+    s1, s2, s3, turned = together(s1, s2, s3, turned)
+    start = jnp.concatenate([mine[most:], s3, s2, s1], 0)
+    before, after = [ring(start, "z", nz, 1)], [start, ring(start, "z", nz, -1)]
     turned = jnp.einsum("dgcf,cbfn->dbgn", per_col, turned, preferred_element_type=jnp.float32)
     turned = exchange(turned.astype(jnp.bfloat16).reshape(whole), "cols")
-    turned, spread = together(turned, cotangent)
+    turned, before[0], after[1] = together(turned, before[0], after[1])
+    before.append(ring(before[0], "z", nz, 1))
+    after.append(ring(after[1], "z", nz, -1))
+    turned, before[1], after[2] = together(turned, before[1], after[2])
+    before.append(ring(before[1], "z", nz, 1))
+    after.append(ring(after[2], "z", nz, -1))
+    in_vmem = pl.BlockSpec(memory_space=pltpu.VMEM)
+    terms = tile_pass(
+        functools.partial(reverse_body, tb=TB), tile_rows, place, tile_count, [turned], in_vmem, adj_tiles,
+        (nz * x_first,) * nx + (nx * z_first,) * nz, [], 40, "reverse",
+    )
+    *terms, spread, before[2], after[3] = together(*terms, cotangent, before[2], after[3])
     grad_full = to_all(spread, "cols")
-    terms = tile_pass(
-        reverse_body, tile_rows, place, tile_count, turned, adj_tiles,
-        (nz * x_first,) * nx + (nx * z_first,) * nz, "reverse",
-    )
-
-    def add(*terms):
-        return sum(t.astype(jnp.float32) for t in terms)
-
-    def narrowed(*terms):
-        return add(*terms).astype(jnp.bfloat16)
-
-    *terms, grad_full = together(*terms, grad_full)
+
     by_x, by_z = terms[:nx], terms[nx:]
+    before.append(ring(before[2], "z", nz, 1))
     m2 = ring(by_x[2], "x", nx, 1)
     m3 = ring(by_x[3], "x", nx, -1)
     ahead, behind = ring(by_z[4], "z", nz, 1), ring(by_z[5], "z", nz, -1)
-    ahead, behind = together(narrowed(by_z[3], ahead), narrowed(by_z[6], behind))
+    ahead, behind, before[3], count = together(
+        narrowed(by_z[3], ahead), narrowed(by_z[6], behind), before[3], tile_count
+    )
     ahead, behind = ring(ahead, "z", nz, 1), ring(behind, "z", nz, -1)
-    m2, m3, ahead, behind = together(m2, m3, ahead, behind)
+    panel = [gathered, *after, *before[::-1]]
+    (mixed,) = tile_pass(
+        functools.partial(forward_body, tb=TB, pieces=len(panel)), tile_rows, source, count, panel,
+        pl.BlockSpec(memory_space=pl.ANY), adj_tiles, (blocks,),
+        [
+            pltpu.VMEM((nz * nx * blocks, narrow, side), jnp.bfloat16),
+            pltpu.SemaphoreType.DMA((len(panel),)),
+        ],
+        56, "forward",
+    )
+    m2, m3, ahead, behind, grad_full, mixed = together(m2, m3, ahead, behind, grad_full, mixed)
 
     m1 = ring(narrowed(by_x[1], m2), "x", nx, 1)
     ahead = ring(narrowed(by_z[2], ahead), "z", nz, 1)
     behind = ring(narrowed(by_z[7], behind), "z", nz, -1)
-    m1, ahead, behind, count = together(m1, ahead, behind, tile_count)
+    mixed_full = exchange(mixed, "cols").reshape(split)
+    term = lax.dot_general(
+        from_blocks(mixed), grad_full, (((1,), (1,)), ((), ())), preferred_element_type=jnp.float32
+    ).astype(jnp.bfloat16)
+    m1, ahead, behind, mixed_full, term = together(m1, ahead, behind, mixed_full, term)
 
     def held(*far):
         cut = slice(far[0] * x_first, (far[-1] + 1) * x_first)
@@ -194,25 +237,16 @@
     n34 = ring(narrowed(*held(3, 4)), "z", nz, 2)
     n56 = ring(narrowed(*held(5, 6)), "z", nz, -2)
     ahead = ring(narrowed(by_z[1], ahead), "z", nz, 1)
-    (mixed,) = tile_pass(
-        forward_body, tile_rows, tile_cols, count, panel, adj_tiles, (blocks,), "forward"
-    )
-    n34, n56, ahead, mixed = together(n34, n56, ahead, mixed)
-
-    mixed_full = exchange(mixed, "cols").reshape(split)
-    term = lax.dot_general(
-        from_blocks(mixed), grad_full, (((1,), (1,)), ((), ())), preferred_element_type=jnp.float32
-    )
-    shares = to_all(term.astype(jnp.bfloat16)[None], ("z", "x"))
+    n34, n56, term, mixed_full = together(n34, n56, term, mixed_full)
+    shares = to_all(term[None], ("z", "x"))
+    aggregated = jnp.einsum(
+        "cfdg,cbfn->dbgn", per_col, mixed_full, preferred_element_type=jnp.float32
+    ).astype(jnp.bfloat16)
     n2 = ring(narrowed(*held(2), n34[x_first:]), "z", nz, 2)
     n1 = ring(narrowed(*held(1), n34[:x_first]), "z", nz, 1)
     n7 = ring(narrowed(*held(7), n56[:x_first]), "z", nz, -1)
     line = add(by_z[0], ahead, behind).reshape(nx, z_first, narrow, side)
     late = add(line[0], *(ring(narrowed(line[i]), "x", nx, (0, 1, 2, -1)[i]) for i in (1, 2, 3)))
-
-    aggregated = jnp.einsum(
-        "cfdg,cbfn->dbgn", per_col, mixed_full, preferred_element_type=jnp.float32
-    ).astype(jnp.bfloat16)
     whole_term = shares.astype(jnp.float32).sum(0).reshape(narrow, -1, side).transpose(1, 0, 2)
     top = whole_term.astype(jnp.bfloat16)
     rest = (whole_term - top.astype(jnp.float32)).astype(jnp.bfloat16)

time: 241 us -> 237 us (0.983)
  waiting for transfers between devices: 83.7 us -> 56.3 us
  starting transfers between devices: 62.8 us -> 76.6 us
  Pallas kernels: 30.1 us -> 36.3 us
  other arithmetic: 14.2 us -> 18.1 us
  local copies, waits for them, and re-layouts: 21.1 us -> 18.2 us
    ppermute x18 -> x28, waiting for transfers between devices: 57.5 us -> 38.8 us  [ring(): return lax.ppermute(a, (axis, 'cols'), moves)]
    ppermute x18 -> x28, starting transfers between devices: 31.6 us -> 43.1 us  [ring(): return lax.ppermute(a, (axis, 'cols'), moves)]
    all_to_all x5, waiting for transfers between devices: 26.1 us -> 17.4 us  [exchange(): return lax.all_to_all(parts, axis, split_axis=0, concat_axis=0, tiled=True)]
    pallas_call x2, Pallas kernels: 30.1 us -> 36.3 us  [tile_pass(): pl.pallas_call(body, out_shape=[jax.ShapeDtypeStruct((n, narrow, side), j...]
    convert_element_type x8, other arithmetic: 9.38 us -> 13.6 us  [narrowed(): return add(*terms).astype(jnp.bfloat16)]
    unnamed x43 -> x58, local copies, waits for them, and re-layouts: 12.9 us -> 10.9 us
  transfers between devices with their start and end apart: 24 -> 34, of which waited for: 11 -> 14; matrix products, arithmetic and copies ran while one was open for 10% -> 11% of each run, Pallas kernels for 13% -> 15%
where the time goes in v3:
time: 237 us
  starting transfers between devices  76.6 us (32%)
  waiting for transfers between devices  56.3 us (24%)
  Pallas kernels  36.3 us (15%)
  local copies, waits for them, and re-layouts  18.2 us (8%)
  other arithmetic  18.1 us (8%)
  between operations  15.1 us (6%)
  blocking collectives  11.3 us (5%)
  matrix products  4.66 us (2%)
    ppermute x28, starting transfers between devices, ring(): return lax.ppermute(a, (axis, 'cols'), moves)  43.1 us
    ppermute x28, waiting for transfers between devices, ring(): return lax.ppermute(a, (axis, 'cols'), moves)  38.8 us
    pallas_call x2, Pallas kernels, tile_pass(): pl.pallas_call(body, out_shape=[jax.ShapeDtypeStruct((n, narrow, side), j...  36.3 us
    all_to_all x5, starting transfers between devices, exchange(): return lax.all_to_all(parts, axis, split_axis=0, concat_axis=0, tiled=True)  33.5 us
    all_to_all x5, waiting for transfers between devices, exchange(): return lax.all_to_all(parts, axis, split_axis=0, concat_axis=0, tiled=True)  17.4 us
    convert_element_type x8, other arithmetic, narrowed(): return add(*terms).astype(jnp.bfloat16)  13.6 us
    all_to_all x1, blocking collectives, exchange(): return lax.all_to_all(parts, axis, split_axis=0, concat_axis=0, tiled=True)  11.3 us
    unnamed x58, local copies, waits for them, and re-layouts  10.9 us
  transfers between devices with their start and end apart: 34, of which 14 were waited for; matrix products, arithmetic and copies ran while one was open for 11% of the time, Pallas kernels for 15%

profile of v3, /device:TPU:1, one launch (start us, length us, event | category | flops | bytes accessed | tf_op | source)
XLA Modules:
  0.0 236.6 jit_solution(2037071587294140742)
XLA Ops:
  10.7 6.6 %all-to-all-start = ((bf16[32,32,128]{2,1,0:T(8,128)(2,1)}), bf16[32,32,128]{2,1,0:T(8,128)(2,1)S(1)}, u32[]{:S(2)}, u32[]{:S(2)}) async-start(bf16[32,32,128]{2,1,0:T(8,128)(2,1)} %copy.52), calls=%async_computation | async-start | bytes 524288 | tf_op jit(solution)/shard_map/all_to_all | solution.py:124
  17.3 2.0 collective-permute-start
  21.1 4.0 %collective-permute-done.1 = bf16[12,32,128]{2,1,0:T(8,128)(2,1)S(1)} collective-permute-done((bf16[12,32,128]{2,1,0:T(8,128)(2,1)S(1)}, bf16[12,32,128]{2,1,0:T(8,128)(2,1)S(1)}, u32[]{:S(2)}, u32[]{:S(2)}) %collective-permute-start.1) | collective-permute-done | bytes 98336 | tf_op jit(solution)/shard_map/ppermute | solution.py:150
  26.1 5.7 %collective-permute-start.3 = (bf16[48,32,128]{2,1,0:T(8,128)(2,1)S(1)}, bf16[48,32,128]{2,1,0:T(8,128)(2,1)S(1)}, u32[]{:S(2)}, u32[]{:S(2)}) collective-permute-start(bf16[48,32,128]{2,1,0:T(8,128)(2,1)S(1)} %pad_maximum_fusion.1.rest_1_), channel_id=1, source_target_pairs={{0,32},{1,225},{2,34},{3,227},{4,36},{5,229},{6,38},{7,231},{32,64... | collective-permute-start | bytes 1179656 | tf_op jit(solution)/shard_map/ppermute | solution.py:150
  32.1 11.3 %all_to_all.34.grads_ref = bf16[32,32,128]{2,1,0:T(8,128)(2,1)S(1)} all-to-all(bf16[32,32,128]{2,1,0:T(8,128)(2,1)S(1)} %bitcast.83), channel_id=1, replica_groups=mesh['z'=8,'x'=4,'cols'=8] {'cols'}, dimensions={0} | all-to-all | bytes 524288 | tf_op jit(solution)/shard_map/all_to_all | solution.py:124
  43.8 2.7 %collective-permute-start.5 = (bf16[48,32,128]{2,1,0:T(8,128)(2,1)S(1)}, bf16[48,32,128]{2,1,0:T(8,128)(2,1)}, u32[]{:S(2)}, u32[]{:S(2)}) collective-permute-start(bf16[48,32,128]{2,1,0:T(8,128)(2,1)S(1)} %collective-permute-done.3.rest_8_), channel_id=1, source_target_pairs={{0,32},{1,225},{2,34},{3,227},{4,36},{5,229},{6,38},{7,231},{32,64... | collective-permute-start | bytes 1179656 | tf_op jit(solution)/shard_map/ppermute | solution.py:150
  47.8 8.6 %collective-permute-done.5.rest_7_ = bf16[48,32,128]{2,1,0:T(8,128)(2,1)} collective-permute-done((bf16[48,32,128]{2,1,0:T(8,128)(2,1)S(1)}, bf16[48,32,128]{2,1,0:T(8,128)(2,1)}, u32[]{:S(2)}, u32[]{:S(2)}) %collective-permute-start.5) | collective-permute-done | bytes 393248 | tf_op jit(solution)/shard_map/ppermute | solution.py:150
  56.4 2.4 collective-permute-done.6.rest_3_
  58.7 1.2 collective-permute-start.7
  60.2 15.8 %reverse.1 = (bf16[128,32,128]{2,1,0:T(8,128)(2,1)S(1)}, bf16[128,32,128]{2,1,0:T(8,128)(2,1)S(1)}, bf16[128,32,128]{2,1,0:T(8,128)(2,1)S(1)}, bf16[128,32,128]{...) custom-call(s32[1024]{0:T(1024)S(1)} %copy-done.8, ...), custom_call_target="tpu_custom_call" | custom-call | flops 8589934592 | bytes 42205184 | tf_op jit(solution)/shard_map/reverse/pallas_call | solution.py:105
  79.3 1.0 copy-done.9
  81.1 1.0 copy-done.10
  84.2 1.6 tile.4
  85.8 6.6 %all-to-all-start.2 = ((bf16[8,32,4096]{2,1,0:T(8,128)(2,1)}), bf16[8,32,4096]{2,1,0:T(8,128)(2,1)}, u32[]{:S(2)}, u32[]{:S(2)}) async-start(bf16[8,32,4096]{2,1,0:T(8,128)(2,1)} %tile.4), calls=%async_computation.2 | async-start | bytes 4194304 | tf_op jit(solution)/shard_map/all_to_all | solution.py:124
  92.4 3.7 %collective-permute-start.11 = (bf16[64,32,128]{2,1,0:T(8,128)(2,1)}, bf16[64,32,128]{2,1,0:T(8,128)(2,1)S(1)}, u32[]{:S(2)}, u32[]{:S(2)}) collective-permute-start(bf16[64,32,128]{2,1,0:T(8,128)(2,1)} %copy-done.11), channel_id=1, source_target_pairs={{0,32},{1,225},{2,34},{3,227},{4,36},{5,229},{6,38},{7,231},{32,64... | collective-permute-start | bytes 1572872 | tf_op jit(solution)/shard_map/ppermute | solution.py:150
  96.1 2.7 %collective-permute-start.9 = (bf16[128,32,128]{2,1,0:T(8,128)(2,1)}, bf16[128,32,128]{2,1,0:T(8,128)(2,1)}, u32[]{:S(2)}, u32[]{:S(2)}) collective-permute-start(bf16[128,32,128]{2,1,0:T(8,128)(2,1)} %copy-done.9), channel_id=1, source_target_pairs={{0,8},{1,25},{2,10},{3,27},{4,12},{5,29},{6,14},{7,31},{8,16},{9,1... | collective-permute-start | bytes 3145736 | tf_op jit(solution)/shard_map/ppermute | solution.py:150
  98.8 7.4 %collective-permute-done.12 = bf16[64,32,128]{2,1,0:T(8,128)(2,1)} collective-permute-done((bf16[64,32,128]{2,1,0:T(8,128)(2,1)}, bf16[64,32,128]{2,1,0:T(8,128)(2,1)}, u32[]{:S(2)}, u32[]{:S(2)}) %collective-permute-start.12) | collective-permute-done | bytes 524320 | tf_op jit(solution)/shard_map/ppermute | solution.py:150
  106.2 2.1 add_convert_fusion.4
  108.8 2.0 add_convert_fusion.5
  110.8 2.2 collective-permute-done.13.rest_5_
  113.0 2.6 %collective-permute-start.14 = (bf16[64,32,128]{2,1,0:T(8,128)(2,1)}, bf16[64,32,128]{2,1,0:T(8,128)(2,1)}, u32[]{:S(2)}, u32[]{:S(2)}) collective-permute-start(bf16[64,32,128]{2,1,0:T(8,128)(2,1)} %add_convert_fusion.5), channel_id=1, source_target_pairs={{0,32},{1,225},{2,34},{3,227},{4,36},{5,229},{6,38},{7,231},{32,64... | collective-permute-start | bytes 1572872 | tf_op jit(solution)/shard_map/ppermute | solution.py:150
  115.6 20.5 %forward.1 = bf16[32,32,128]{2,1,0:T(8,128)(2,1)} custom-call(s32[1024]{0:T(1024)} %rows_ref.3, s32[1024]{0:T(1024)} %get-tuple-element.127.places_ref, s32[1]{0:T(128)S(6)} %copy.96.count_ref, bf16[640,32,128]{2,1,0:T(8,128)(2,1)} %all-gather.2.cloned.1.call-done.rest_0_, bf16[48,32,128]{2,1,0:T(8,128)(2,1)} %copy-done.14, bf16[48,32,128]{2,1,0:T(8,128)(2,1)} %copy-done.18, ...), custom_call_target="tpu_custom_call" | custom-call | flops 8589934592 | bytes 42205184 | tf_op jit(solution)/shard_map/forward/pallas_call | solution.py:105
  136.2 2.5 %add_convert_fusion = bf16[128,32,128]{2,1,0:T(8,128)(2,1)} fusion(bf16[128,32,128]{2,1,0:T(8,128)(2,1)} %collective-permute-done.9, bf16[128,32,128]{2,1,0:T(8,128)(2,1)S(1)} %get-tuple-element.82), kind=kLoop, calls=%fused_computation | loop fusion | flops 2097152 | bytes 3145728 | tf_op jit(solution)/shard_map/convert_element_type | solution.py:156
  138.7 6.0 %collective-permute-start.16 = (bf16[128,32,128]{2,1,0:T(8,128)(2,1)}, bf16[128,32,128]{2,1,0:T(8,128)(2,1)}, u32[]{:S(2)}, u32[]{:S(2)}) collective-permute-start(bf16[128,32,128]{2,1,0:T(8,128)(2,1)} %add_convert_fusion), channel_id=1, source_target_pairs={{0,8},{1,25},{2,10},{3,27},{4,12},{5,29},{6,14},{7,31},{8,16},{9,1... | collective-permute-start | bytes 3145736 | tf_op jit(solution)/shard_map/ppermute | solution.py:150
  144.7 1.2 add_convert_fusion.2
  146.0 2.0 add_convert_fusion.3
  148.0 2.7 %collective-permute-start.17 = (bf16[64,32,128]{2,1,0:T(8,128)(2,1)}, bf16[64,32,128]{2,1,0:T(8,128)(2,1)S(1)}, u32[]{:S(2)}, u32[]{:S(2)}) collective-permute-start(bf16[64,32,128]{2,1,0:T(8,128)(2,1)} %add_convert_fusion.3), channel_id=1, source_target_pairs={{0,32},{1,225},{2,34},{3,227},{4,36},{5,229},{6,38},{7,231},{32,64... | collective-permute-start | bytes 1572872 | tf_op jit(solution)/shard_map/ppermute | solution.py:150
  150.6 1.2 copy.58
  151.8 4.3 %all-to-all-start.3 = ((bf16[32,32,128]{2,1,0:T(8,128)(2,1)}), bf16[32,32,128]{2,1,0:T(8,128)(2,1)S(1)}, u32[]{:S(2)}, u32[]{:S(2)}) async-start(bf16[32,32,128]{2,1,0:T(8,128)(2,1)} %forward.1), calls=%async_computation.3 | async-start | bytes 524288 | tf_op jit(solution)/shard_map/all_to_all | solution.py:124
  156.1 2.4 %convolution_convert_fusion = bf16[32,256]{1,0:T(8,128)(2,1)S(1)} fusion(bf16[256,4096]{1,0:T(8,128)(2,1)} %bitcast.9, bf16[32,32,128]{2,1,0:T(8,128)(2,1)} %forward.1), kind=kOutput, calls=%fused_computation.7 | convolution fusion | flops 67117056 | bytes 2375680 | tf_op jit(solution)/shard_map/dot_general | solution.py:228
  158.5 4.1 %all-to-all-done.3 = bf16[32,32,128]{2,1,0:T(8,128)(2,1)S(1)} async-done(((bf16[32,32,128]{2,1,0:T(8,128)(2,1)}), bf16[32,32,128]{2,1,0:T(8,128)(2,1)S(1)}, u32[]{:S(2)}, u32[]{:S(2)}) %all-to-all-start.3) | async-done | bytes 262176 | tf_op jit(solution)/shard_map/all_to_all | solution.py:124
  162.6 1.5 add_convert_fusion.6
  164.1 1.2 collective-permute-start.19
  165.3 1.2 collective-permute-start.20
  166.7 1.5 collective-permute-start.24
  168.2 7.7 %collective-permute-done.19 = bf16[32,32,128]{2,1,0:T(8,128)(2,1)S(1)} collective-permute-done((bf16[32,32,128]{2,1,0:T(8,128)(2,1)S(1)}, bf16[32,32,128]{2,1,0:T(8,128)(2,1)S(1)}, u32[]{:S(2)}, u32[]{:S(2)}) %collective-permute-start.19) | collective-permute-done | bytes 262176 | tf_op jit(solution)/shard_map/ppermute | solution.py:150
  175.9 4.2 %collective-permute-done.20 = bf16[32,32,128]{2,1,0:T(8,128)(2,1)S(1)} collective-permute-done((bf16[32,32,128]{2,1,0:T(8,128)(2,1)S(1)}, bf16[32,32,128]{2,1,0:T(8,128)(2,1)S(1)}, u32[]{:S(2)}, u32[]{:S(2)}) %collective-permute-start.20) | collective-permute-done | bytes 262176 | tf_op jit(solution)/shard_map/ppermute | solution.py:150
  180.1 2.2 add_convert_fusion.11
  182.3 1.0 collective-permute-start.21
  183.3 3.3 %collective-permute-start.22 = (bf16[16,32,128]{2,1,0:T(8,128)(2,1)}, bf16[16,32,128]{2,1,0:T(8,128)(2,1)}, u32[]{:S(2)}, u32[]{:S(2)}) collective-permute-start(bf16[16,32,128]{2,1,0:T(8,128)(2,1)} %get-tuple-element.120), channel_id=1, source_target_pairs={{0,32},{1,225},{2,34},{3,227},{4,36},{5,229},{6,38},{7,231},{32,64... | collective-permute-start | bytes 393224 | tf_op jit(solution)/shard_map/ppermute | solution.py:150
  187.5 7.3 %all-to-all-start.4 = ((bf16[32,32,256]{2,1,0:T(8,128)(2,1)}), bf16[32,32,256]{2,1,0:T(8,128)(2,1)S(1)}, u32[]{:S(2)}, u32[]{:S(2)}) async-start(bf16[32,32,256]{2,1,0:T(8,128)(2,1)} %tile.5), calls=%async_computation.4 | async-start | bytes 1048576 | tf_op jit(solution)/shard_map/all_to_all | solution.py:124
  194.8 2.0 fusion.2
  197.4 1.3 add_convert_fusion.8
  198.8 1.5 fusion.25
  200.3 2.5 %collective-permute-start.25 = (bf16[16,32,128]{2,1,0:T(8,128)(2,1)S(1)}, bf16[16,32,128]{2,1,0:T(8,128)(2,1)S(1)}, u32[]{:S(2)}, u32[]{:S(2)}) collective-permute-start(bf16[16,32,128]{2,1,0:T(8,128)(2,1)S(1)} %get-tuple-element.124), channel_id=1, source_target_pairs={{0,8},{1,25},{2,10},{3,27},{4,12},{5,29},{6,14},{7,31},{8,16},{9,1... | collective-permute-start | bytes 393224 | tf_op jit(solution)/shard_map/ppermute | solution.py:150
  203.9 4.6 %all-to-all-done.4 = bf16[32,32,256]{2,1,0:T(8,128)(2,1)S(1)} async-done(((bf16[32,32,256]{2,1,0:T(8,128)(2,1)}), bf16[32,32,256]{2,1,0:T(8,128)(2,1)S(1)}, u32[]{:S(2)}, u32[]{:S(2)}) %all-to-all-start.4) | async-done | bytes 524320 | tf_op jit(solution)/shard_map/all_to_all | solution.py:124
  209.8 8.8 %all-to-all-start.5 = ((bf16[8,8,32,128]{3,2,1,0:T(8,128)(2,1)}), bf16[8,8,32,128]{3,2,1,0:T(8,128)(2,1)S(1)}, u32[]{:S(2)}, u32[]{:S(2)}) async-start(bf16[8,8,32,128]{3,2,1,0:T(8,128)(2,1)} %copy.60), calls=%async_computation.5 | async-start | bytes 1048576 | tf_op jit(solution)/shard_map/all_to_all | solution.py:124
  219.3 8.7 %all-to-all-done.5 = bf16[8,8,32,128]{3,2,1,0:T(8,128)(2,1)S(1)} async-done(((bf16[8,8,32,128]{3,2,1,0:T(8,128)(2,1)}), bf16[8,8,32,128]{3,2,1,0:T(8,128)(2,1)S(1)}, u32[]{:S(2)}, u32[]{:S(2)}) %all-to-all-start.5) | async-done | bytes 524320 | tf_op jit(solution)/shard_map/all_to_all | solution.py:124
  (121 shorter events, 21.2 us)
Async XLA Ops:
  7.2 13.2 %copy-start.25 = (bf16[256,256]{1,0:T(8,128)(2,1)S(1)}, bf16[256,256]{1,0:T(8,128)(2,1)}, u32[]{:S(2)}) copy-start(bf16[256,256]{1,0:T(8,128)(2,1)} %param.8) | copy-start | bytes 393220
  7.2 108.4 %all-gather.2.cloned.1.call-start = ((), (), s32[]{:S(2)}) async-start(), calls=%async_computation.6 | async-start | bytes 5406720 | tf_op jit(solution)/shard_map/all_gather | solution.py:177
  10.7 15.4 %all-to-all-start = ((bf16[32,32,128]{2,1,0:T(8,128)(2,1)}), bf16[32,32,128]{2,1,0:T(8,128)(2,1)S(1)}, u32[]{:S(2)}, u32[]{:S(2)}) async-start(bf16[32,32,128]{2,1,0:T(8,128)(2,1)} %copy.52), calls=%async_computation | async-start | bytes 524288 | tf_op jit(solution)/shard_map/all_to_all | solution.py:124
  17.2 29.9 %copy-start.27 = (s32[1024]{0:T(1024)S(1)}, s32[1024]{0:T(1024)}, u32[]{:S(2)}) copy-start(s32[1024]{0:T(1024)} %param.11) | copy-start | bytes 12292
  17.3 43.0 %copy-start.8 = (s32[1024]{0:T(1024)S(1)}, s32[1024]{0:T(1024)}, u32[]{:S(2)}) copy-start(s32[1024]{0:T(1024)} %rows_ref.3) | copy-start | bytes 12292
  17.3 3.8 %collective-permute-start = (bf16[12,32,128]{2,1,0:T(8,128)(2,1)S(1)}, bf16[12,32,128]{2,1,0:T(8,128)(2,1)S(1)}, u32[]{:S(2)}, u32[]{:S(2)}) collective-permute-start(bf16[12,32,128]{2,1,0:T(8,128)(2,1)S(1)} %slice.134), channel_id=1, source_target_pairs={{0,8},{1,25},{2,10},{3,27},{4,12},{5,29},{6,14},{7,31},{8,16},{9,1... | collective-permute-start | bytes 294920 | tf_op jit(solution)/shard_map/ppermute | solution.py:150
  19.2 5.9 %collective-permute-start.1 = (bf16[12,32,128]{2,1,0:T(8,128)(2,1)S(1)}, bf16[12,32,128]{2,1,0:T(8,128)(2,1)S(1)}, u32[]{:S(2)}, u32[]{:S(2)}) collective-permute-start(bf16[12,32,128]{2,1,0:T(8,128)(2,1)S(1)} %slice.134), channel_id=1, source_target_pairs={{0,16},{1,17},{2,18},{3,19},{4,20},{5,21},{6,22},{7,23},{8,24},{9,... | collective-permute-start | bytes 294920 | tf_op jit(solution)/shard_map/ppermute | solution.py:150
  19.8 6.3 %collective-permute-start.2 = (bf16[12,32,128]{2,1,0:T(8,128)(2,1)S(1)}, bf16[12,32,128]{2,1,0:T(8,128)(2,1)S(1)}, u32[]{:S(2)}, u32[]{:S(2)}) collective-permute-start(bf16[12,32,128]{2,1,0:T(8,128)(2,1)S(1)} %slice.134), channel_id=1, source_target_pairs={{0,24},{1,9},{2,26},{3,11},{4,28},{5,13},{6,30},{7,15},{8,0},{9,17... | collective-permute-start | bytes 294920 | tf_op jit(solution)/shard_map/ppermute | solution.py:150
  20.6 39.6 %copy-start.12 = (bf16[8,32,8,32]{3,2,1,0:T(8,128)(2,1)}, bf16[8,32,8,32]{3,2,1,0:T(8,128)(2,1)S(1)}, u32[]{:S(2)}) copy-start(bf16[8,32,8,32]{3,2,1,0:T(8,128)(2,1)S(1)} %reshape.64) | copy-start | bytes 393220
  26.1 34.1 %copy-start.14 = (bf16[48,32,128]{2,1,0:T(8,128)(2,1)}, bf16[48,32,128]{2,1,0:T(8,128)(2,1)S(1)}, u32[]{:S(2)}) copy-start(bf16[48,32,128]{2,1,0:T(8,128)(2,1)S(1)} %pad_maximum_fusion.1.rest_1_) | copy-start | bytes 1179652
  26.1 17.2 %collective-permute-start.3 = (bf16[48,32,128]{2,1,0:T(8,128)(2,1)S(1)}, bf16[48,32,128]{2,1,0:T(8,128)(2,1)S(1)}, u32[]{:S(2)}, u32[]{:S(2)}) collective-permute-start(bf16[48,32,128]{2,1,0:T(8,128)(2,1)S(1)} %pad_maximum_fusion.1.rest_1_), channel_id=1, source_target_pairs={{0,32},{1,225},{2,34},{3,227},{4,36},{5,229},{6,38},{7,231},{32,64... | collective-permute-start | bytes 1179656 | tf_op jit(solution)/shard_map/ppermute | solution.py:150
  31.8 12.0 %collective-permute-start.4 = (bf16[48,32,128]{2,1,0:T(8,128)(2,1)S(1)}, bf16[48,32,128]{2,1,0:T(8,128)(2,1)S(1)}, u32[]{:S(2)}, u32[]{:S(2)}) collective-permute-start(bf16[48,32,128]{2,1,0:T(8,128)(2,1)S(1)} %pad_maximum_fusion.1.rest_1_), channel_id=1, source_target_pairs={{0,224},{1,33},{2,226},{3,35},{4,228},{5,37},{6,230},{7,39},{32,0}... | collective-permute-start | bytes 1179656 | tf_op jit(solution)/shard_map/ppermute | solution.py:150
  43.4 16.9 %copy-start.17 = (bf16[48,32,128]{2,1,0:T(8,128)(2,1)}, bf16[48,32,128]{2,1,0:T(8,128)(2,1)S(1)}, u32[]{:S(2)}) copy-start(bf16[48,32,128]{2,1,0:T(8,128)(2,1)S(1)} %collective-permute-done.3.rest_8_) | copy-start | bytes 1179652
  43.8 16.5 %copy-start.18 = (bf16[48,32,128]{2,1,0:T(8,128)(2,1)}, bf16[48,32,128]{2,1,0:T(8,128)(2,1)S(1)}, u32[]{:S(2)}) copy-start(bf16[48,32,128]{2,1,0:T(8,128)(2,1)S(1)} %collective-permute-done.4.rest_2_) | copy-start | bytes 1179652
  43.8 12.6 %collective-permute-start.5 = (bf16[48,32,128]{2,1,0:T(8,128)(2,1)S(1)}, bf16[48,32,128]{2,1,0:T(8,128)(2,1)}, u32[]{:S(2)}, u32[]{:S(2)}) collective-permute-start(bf16[48,32,128]{2,1,0:T(8,128)(2,1)S(1)} %collective-permute-done.3.rest_8_), channel_id=1, source_target_pairs={{0,32},{1,225},{2,34},{3,227},{4,36},{5,229},{6,38},{7,231},{32,64... | collective-permute-start | bytes 1179656 | tf_op jit(solution)/shard_map/ppermute | solution.py:150
  46.5 12.3 %collective-permute-start.6 = (bf16[48,32,128]{2,1,0:T(8,128)(2,1)S(1)}, bf16[48,32,128]{2,1,0:T(8,128)(2,1)}, u32[]{:S(2)}, u32[]{:S(2)}) collective-permute-start(bf16[48,32,128]{2,1,0:T(8,128)(2,1)S(1)} %collective-permute-done.4.rest_2_), channel_id=1, source_target_pairs={{0,224},{1,33},{2,226},{3,35},{4,228},{5,37},{6,230},{7,39},{32,0}... | collective-permute-start | bytes 1179656 | tf_op jit(solution)/shard_map/ppermute | solution.py:150
  58.7 22.4 %collective-permute-start.7 = (bf16[48,32,128]{2,1,0:T(8,128)(2,1)}, bf16[48,32,128]{2,1,0:T(8,128)(2,1)S(1)}, u32[]{:S(2)}, u32[]{:S(2)}) collective-permute-start(bf16[48,32,128]{2,1,0:T(8,128)(2,1)} %collective-permute-done.5.rest_7_), channel_id=1, source_target_pairs={{0,32},{1,225},{2,34},{3,227},{4,36},{5,229},{6,38},{7,231},{32,64... | collective-permute-start | bytes 1179656 | tf_op jit(solution)/shard_map/ppermute | solution.py:150
  59.9 22.3 %collective-permute-start.8 = (bf16[48,32,128]{2,1,0:T(8,128)(2,1)}, bf16[48,32,128]{2,1,0:T(8,128)(2,1)S(1)}, u32[]{:S(2)}, u32[]{:S(2)}) collective-permute-start(bf16[48,32,128]{2,1,0:T(8,128)(2,1)} %collective-permute-done.6.rest_3_), channel_id=1, source_target_pairs={{0,224},{1,33},{2,226},{3,35},{4,228},{5,37},{6,230},{7,39},{32,0}... | collective-permute-start | bytes 1179656 | tf_op jit(solution)/shard_map/ppermute | solution.py:150
  60.2 23.9 %copy-start.15 = (bf16[32,4096]{1,0:T(8,128)(2,1)S(1)}, bf16[32,4096]{1,0:T(8,128)(2,1)}, u32[]{:S(2)}) copy-start(bf16[32,4096]{1,0:T(8,128)(2,1)} %param.13) | copy-start | bytes 786436
  83.7 22.6 %collective-permute-start.12 = (bf16[64,32,128]{2,1,0:T(8,128)(2,1)}, bf16[64,32,128]{2,1,0:T(8,128)(2,1)}, u32[]{:S(2)}, u32[]{:S(2)}) collective-permute-start(bf16[64,32,128]{2,1,0:T(8,128)(2,1)} %get-tuple-element.88), channel_id=1, source_target_pairs={{0,224},{1,33},{2,226},{3,35},{4,228},{5,37},{6,230},{7,39},{32,0}... | collective-permute-start | bytes 1572872 | tf_op jit(solution)/shard_map/ppermute | solution.py:150
  85.8 50.4 %all-to-all-start.2 = ((bf16[8,32,4096]{2,1,0:T(8,128)(2,1)}), bf16[8,32,4096]{2,1,0:T(8,128)(2,1)}, u32[]{:S(2)}, u32[]{:S(2)}) async-start(bf16[8,32,4096]{2,1,0:T(8,128)(2,1)} %tile.4), calls=%async_computation.2 | async-start | bytes 4194304 | tf_op jit(solution)/shard_map/all_to_all | solution.py:124
  92.4 16.4 %collective-permute-start.11 = (bf16[64,32,128]{2,1,0:T(8,128)(2,1)}, bf16[64,32,128]{2,1,0:T(8,128)(2,1)S(1)}, u32[]{:S(2)}, u32[]{:S(2)}) collective-permute-start(bf16[64,32,128]{2,1,0:T(8,128)(2,1)} %copy-done.11), channel_id=1, source_target_pairs={{0,32},{1,225},{2,34},{3,227},{4,36},{5,229},{6,38},{7,231},{32,64... | collective-permute-start | bytes 1572872 | tf_op jit(solution)/shard_map/ppermute | solution.py:150
  96.1 16.9 %collective-permute-start.13 = (bf16[48,32,128]{2,1,0:T(8,128)(2,1)}, bf16[48,32,128]{2,1,0:T(8,128)(2,1)}, u32[]{:S(2)}, u32[]{:S(2)}) collective-permute-start(bf16[48,32,128]{2,1,0:T(8,128)(2,1)} %copy-done.19), channel_id=1, source_target_pairs={{0,32},{1,225},{2,34},{3,227},{4,36},{5,229},{6,38},{7,231},{32,64... | collective-permute-start | bytes 1179656 | tf_op jit(solution)/shard_map/ppermute | solution.py:150
  96.1 40.0 %collective-permute-start.10 = (bf16[128,32,128]{2,1,0:T(8,128)(2,1)}, bf16[128,32,128]{2,1,0:T(8,128)(2,1)}, u32[]{:S(2)}, u32[]{:S(2)}) collective-permute-start(bf16[128,32,128]{2,1,0:T(8,128)(2,1)} %copy-done.10), channel_id=1, source_target_pairs={{0,24},{1,9},{2,26},{3,11},{4,28},{5,13},{6,30},{7,15},{8,0},{9,17... | collective-permute-start | bytes 3145736 | tf_op jit(solution)/shard_map/ppermute | solution.py:150
  96.1 40.0 %collective-permute-start.9 = (bf16[128,32,128]{2,1,0:T(8,128)(2,1)}, bf16[128,32,128]{2,1,0:T(8,128)(2,1)}, u32[]{:S(2)}, u32[]{:S(2)}) collective-permute-start(bf16[128,32,128]{2,1,0:T(8,128)(2,1)} %copy-done.9), channel_id=1, source_target_pairs={{0,8},{1,25},{2,10},{3,27},{4,12},{5,29},{6,14},{7,31},{8,16},{9,1... | collective-permute-start | bytes 3145736 | tf_op jit(solution)/shard_map/ppermute | solution.py:150
  113.0 23.1 %collective-permute-start.14 = (bf16[64,32,128]{2,1,0:T(8,128)(2,1)}, bf16[64,32,128]{2,1,0:T(8,128)(2,1)}, u32[]{:S(2)}, u32[]{:S(2)}) collective-permute-start(bf16[64,32,128]{2,1,0:T(8,128)(2,1)} %add_convert_fusion.5), channel_id=1, source_target_pairs={{0,32},{1,225},{2,34},{3,227},{4,36},{5,229},{6,38},{7,231},{32,64... | collective-permute-start | bytes 1572872 | tf_op jit(solution)/shard_map/ppermute | solution.py:150
  115.6 20.5 %collective-permute-start.15 = (bf16[64,32,128]{2,1,0:T(8,128)(2,1)}, bf16[64,32,128]{2,1,0:T(8,128)(2,1)}, u32[]{:S(2)}, u32[]{:S(2)}) collective-permute-start(bf16[64,32,128]{2,1,0:T(8,128)(2,1)} %add_convert_fusion.4), channel_id=1, source_target_pairs={{0,224},{1,33},{2,226},{3,35},{4,228},{5,37},{6,230},{7,39},{32,0}... | collective-permute-start | bytes 1572872 | tf_op jit(solution)/shard_map/ppermute | solution.py:150
  138.7 11.9 %copy-start.13 = (bf16[8,32,8,32]{3,2,1,0:T(8,128)(2,1)S(1)}, bf16[8,32,8,32]{3,2,1,0:T(8,128)(2,1)}, u32[]{:S(2)}) copy-start(bf16[8,32,8,32]{3,2,1,0:T(8,128)(2,1)} %copy-done.12) | copy-start | bytes 393220
  138.7 23.9 %collective-permute-start.16 = (bf16[128,32,128]{2,1,0:T(8,128)(2,1)}, bf16[128,32,128]{2,1,0:T(8,128)(2,1)}, u32[]{:S(2)}, u32[]{:S(2)}) collective-permute-start(bf16[128,32,128]{2,1,0:T(8,128)(2,1)} %add_convert_fusion), channel_id=1, source_target_pairs={{0,8},{1,25},{2,10},{3,27},{4,12},{5,29},{6,14},{7,31},{8,16},{9,1... | collective-permute-start | bytes 3145736 | tf_op jit(solution)/shard_map/ppermute | solution.py:150
  145.9 16.7 %collective-permute-start.18 = (bf16[64,32,128]{2,1,0:T(8,128)(2,1)S(1)}, bf16[64,32,128]{2,1,0:T(8,128)(2,1)}, u32[]{:S(2)}, u32[]{:S(2)}) collective-permute-start(bf16[64,32,128]{2,1,0:T(8,128)(2,1)S(1)} %add_convert_fusion.2), channel_id=1, source_target_pairs={{0,224},{1,33},{2,226},{3,35},{4,228},{5,37},{6,230},{7,39},{32,0}... | collective-permute-start | bytes 1572872 | tf_op jit(solution)/shard_map/ppermute | solution.py:150
  148.0 14.6 %collective-permute-start.17 = (bf16[64,32,128]{2,1,0:T(8,128)(2,1)}, bf16[64,32,128]{2,1,0:T(8,128)(2,1)S(1)}, u32[]{:S(2)}, u32[]{:S(2)}) collective-permute-start(bf16[64,32,128]{2,1,0:T(8,128)(2,1)} %add_convert_fusion.3), channel_id=1, source_target_pairs={{0,32},{1,225},{2,34},{3,227},{4,36},{5,229},{6,38},{7,231},{32,64... | collective-permute-start | bytes 1572872 | tf_op jit(solution)/shard_map/ppermute | solution.py:150
  151.8 10.8 %all-to-all-start.3 = ((bf16[32,32,128]{2,1,0:T(8,128)(2,1)}), bf16[32,32,128]{2,1,0:T(8,128)(2,1)S(1)}, u32[]{:S(2)}, u32[]{:S(2)}) async-start(bf16[32,32,128]{2,1,0:T(8,128)(2,1)} %forward.1), calls=%async_computation.3 | async-start | bytes 524288 | tf_op jit(solution)/shard_map/all_to_all | solution.py:124
  164.1 11.8 %collective-permute-start.19 = (bf16[32,32,128]{2,1,0:T(8,128)(2,1)S(1)}, bf16[32,32,128]{2,1,0:T(8,128)(2,1)S(1)}, u32[]{:S(2)}, u32[]{:S(2)}) collective-permute-start(bf16[32,32,128]{2,1,0:T(8,128)(2,1)S(1)} %get-tuple-element.123), channel_id=1, source_target_pairs={{0,64},{1,193},{2,66},{3,195},{4,68},{5,197},{6,70},{7,199},{32,96... | collective-permute-start | bytes 786440 | tf_op jit(solution)/shard_map/ppermute | solution.py:150
  165.3 14.8 %collective-permute-start.20 = (bf16[32,32,128]{2,1,0:T(8,128)(2,1)S(1)}, bf16[32,32,128]{2,1,0:T(8,128)(2,1)S(1)}, u32[]{:S(2)}, u32[]{:S(2)}) collective-permute-start(bf16[32,32,128]{2,1,0:T(8,128)(2,1)S(1)} %get-tuple-element.122), channel_id=1, source_target_pairs={{0,192},{1,65},{2,194},{3,67},{4,196},{5,69},{6,198},{7,71},{32,22... | collective-permute-start | bytes 786440 | tf_op jit(solution)/shard_map/ppermute | solution.py:150
  166.7 28.1 %copy-start.16 = (bf16[8,32,8,32]{1,3,0,2:T(8,128)(2,1)S(1)}, bf16[8,32,8,32]{1,3,0,2:T(8,128)(2,1)}, u32[]{:S(2)}) copy-start(bf16[8,32,8,32]{1,3,0,2:T(8,128)(2,1)} %copy.58) | copy-start | bytes 393220
  166.7 32.0 %collective-permute-start.24 = (bf16[64,32,128]{2,1,0:T(8,128)(2,1)S(1)}, bf16[64,32,128]{2,1,0:T(8,128)(2,1)}, u32[]{:S(2)}, u32[]{:S(2)}) collective-permute-start(bf16[64,32,128]{2,1,0:T(8,128)(2,1)S(1)} %add_convert_fusion.1), channel_id=1, source_target_pairs={{0,32},{1,225},{2,34},{3,227},{4,36},{5,229},{6,38},{7,231},{32,64... | collective-permute-start | bytes 1572872 | tf_op jit(solution)/shard_map/ppermute | solution.py:150
  182.3 14.4 %collective-permute-start.21 = (bf16[16,32,128]{2,1,0:T(8,128)(2,1)}, bf16[16,32,128]{2,1,0:T(8,128)(2,1)S(1)}, u32[]{:S(2)}, u32[]{:S(2)}) collective-permute-start(bf16[16,32,128]{2,1,0:T(8,128)(2,1)} %get-tuple-element.119), channel_id=1, source_target_pairs={{0,64},{1,193},{2,66},{3,195},{4,68},{5,197},{6,70},{7,199},{32,96... | collective-permute-start | bytes 393224 | tf_op jit(solution)/shard_map/ppermute | solution.py:150
  183.3 13.4 %collective-permute-start.22 = (bf16[16,32,128]{2,1,0:T(8,128)(2,1)}, bf16[16,32,128]{2,1,0:T(8,128)(2,1)}, u32[]{:S(2)}, u32[]{:S(2)}) collective-permute-start(bf16[16,32,128]{2,1,0:T(8,128)(2,1)} %get-tuple-element.120), channel_id=1, source_target_pairs={{0,32},{1,225},{2,34},{3,227},{4,36},{5,229},{6,38},{7,231},{32,64... | collective-permute-start | bytes 393224 | tf_op jit(solution)/shard_map/ppermute | solution.py:150
  186.6 10.8 %copy-start.24 = (bf16[32,32,128]{2,1,0:T(8,128)(2,1)S(1)}, bf16[32,32,128]{2,1,0:T(8,128)(2,1)}, u32[]{:S(2)}) copy-start(bf16[32,32,128]{2,1,0:T(8,128)(2,1)} %copy-done.23) | copy-start | bytes 786436
  186.6 12.1 %copy-start.7 = (bf16[64,32,128]{2,1,0:T(8,128)(2,1)S(1)}, bf16[64,32,128]{2,1,0:T(8,128)(2,1)}, u32[]{:S(2)}) copy-start(bf16[64,32,128]{2,1,0:T(8,128)(2,1)} %copy-done.6) | copy-start | bytes 1572868
  186.6 10.8 %collective-permute-start.23 = (bf16[16,32,128]{2,1,0:T(8,128)(2,1)}, bf16[16,32,128]{2,1,0:T(8,128)(2,1)}, u32[]{:S(2)}, u32[]{:S(2)}) collective-permute-start(bf16[16,32,128]{2,1,0:T(8,128)(2,1)} %get-tuple-element.121), channel_id=1, source_target_pairs={{0,224},{1,33},{2,226},{3,35},{4,228},{5,37},{6,230},{7,39},{32,0}... | collective-permute-start | bytes 393224 | tf_op jit(solution)/shard_map/ppermute | solution.py:150
  187.5 21.1 %all-to-all-start.4 = ((bf16[32,32,256]{2,1,0:T(8,128)(2,1)}), bf16[32,32,256]{2,1,0:T(8,128)(2,1)S(1)}, u32[]{:S(2)}, u32[]{:S(2)}) async-start(bf16[32,32,256]{2,1,0:T(8,128)(2,1)} %tile.5), calls=%async_computation.4 | async-start | bytes 1048576 | tf_op jit(solution)/shard_map/all_to_all | solution.py:124
  198.7 10.1 %copy-start.22 = (bf16[8,4,32,128]{3,2,0,1:T(8,128)(2,1)S(1)}, bf16[8,4,32,128]{3,2,0,1:T(8,128)(2,1)}, u32[]{:S(2)}) copy-start(bf16[8,4,32,128]{3,2,0,1:T(8,128)(2,1)} %fusion.2) | copy-start | bytes 786436
  200.3 18.2 %collective-permute-start.25 = (bf16[16,32,128]{2,1,0:T(8,128)(2,1)S(1)}, bf16[16,32,128]{2,1,0:T(8,128)(2,1)S(1)}, u32[]{:S(2)}, u32[]{:S(2)}) collective-permute-start(bf16[16,32,128]{2,1,0:T(8,128)(2,1)S(1)} %get-tuple-element.124), channel_id=1, source_target_pairs={{0,8},{1,25},{2,10},{3,27},{4,12},{5,29},{6,14},{7,31},{8,16},{9,1... | collective-permute-start | bytes 393224 | tf_op jit(solution)/shard_map/ppermute | solution.py:150
  202.8 15.7 %collective-permute-start.26 = (bf16[16,32,128]{2,1,0:T(8,128)(2,1)S(1)}, bf16[16,32,128]{2,1,0:T(8,128)(2,1)S(1)}, u32[]{:S(2)}, u32[]{:S(2)}) collective-permute-start(bf16[16,32,128]{2,1,0:T(8,128)(2,1)S(1)} %get-tuple-element.126), channel_id=1, source_target_pairs={{0,16},{1,17},{2,18},{3,19},{4,20},{5,21},{6,22},{7,23},{8,24},{9,... | collective-permute-start | bytes 393224 | tf_op jit(solution)/shard_map/ppermute | solution.py:150
  203.4 15.2 %collective-permute-start.27 = (bf16[16,32,128]{2,1,0:T(8,128)(2,1)S(1)}, bf16[16,32,128]{2,1,0:T(8,128)(2,1)S(1)}, u32[]{:S(2)}, u32[]{:S(2)}) collective-permute-start(bf16[16,32,128]{2,1,0:T(8,128)(2,1)S(1)} %get-tuple-element.125), channel_id=1, source_target_pairs={{0,24},{1,9},{2,26},{3,11},{4,28},{5,13},{6,30},{7,15},{8,0},{9,17... | collective-permute-start | bytes 393224 | tf_op jit(solution)/shard_map/ppermute | solution.py:150
  209.8 18.3 %all-to-all-start.5 = ((bf16[8,8,32,128]{3,2,1,0:T(8,128)(2,1)}), bf16[8,8,32,128]{3,2,1,0:T(8,128)(2,1)S(1)}, u32[]{:S(2)}, u32[]{:S(2)}) async-start(bf16[8,8,32,128]{3,2,1,0:T(8,128)(2,1)} %copy.60), calls=%async_computation.5 | async-start | bytes 1048576 | tf_op jit(solution)/shard_map/all_to_all | solution.py:124
  218.5 11.2 %copy-start.1 = (bf16[32,4096]{1,0:T(8,128)(2,1)S(1)}, bf16[32,4096]{1,0:T(8,128)(2,1)}, u32[]{:S(2)}) copy-start(bf16[32,4096]{1,0:T(8,128)(2,1)} %param.7) | copy-start | bytes 786436
  (14 other events, 25.7 us)
Sparse Core Ops, SparseCore 0:
  11.2 94.5 all-gather.1

commit v4 on v3

--- a/solution.py
+++ b/solution.py
@@ -237,8 +237,9 @@
     n34 = ring(narrowed(*held(3, 4)), "z", nz, 2)
     n56 = ring(narrowed(*held(5, 6)), "z", nz, -2)
     ahead = ring(narrowed(by_z[1], ahead), "z", nz, 1)
-    n34, n56, term, mixed_full = together(n34, n56, term, mixed_full)
+    ahead, term = together(ahead, term)
     shares = to_all(term[None], ("z", "x"))
+    n34, n56, mixed_full = together(n34, n56, mixed_full)
     aggregated = jnp.einsum(
         "cfdg,cbfn->dbgn", per_col, mixed_full, preferred_element_type=jnp.float32
     ).astype(jnp.bfloat16)

time: 237 us -> 242 us (1.021)
  Pallas kernels: 36.3 us -> 43.2 us
  starting transfers between devices: 76.6 us -> 69.7 us
  waiting for transfers between devices: 56.3 us -> 59.3 us
    ppermute x28, starting transfers between devices: 43.1 us -> 36.2 us  [ring(): return lax.ppermute(a, (axis, 'cols'), moves)]
    pallas_call x2, Pallas kernels: 36.3 us -> 43.2 us  [tile_pass(): pl.pallas_call(body, out_shape=[jax.ShapeDtypeStruct((n, narrow, side), j...]
    ppermute x28, waiting for transfers between devices: 38.8 us -> 41.3 us  [ring(): return lax.ppermute(a, (axis, 'cols'), moves)]
    unnamed x58 -> x50, local copies, waits for them, and re-layouts: 10.9 us -> 10.2 us
  transfers between devices with their start and end apart: 34 -> 34, of which waited for: 14 -> 14; matrix products, arithmetic and copies ran while one was open for 11% -> 11% of each run, Pallas kernels for 15% -> 18%
where the time goes in v4:
time: 242 us; the launch traced here: 241 us
  starting transfers between devices  69.7 us (29%)
  waiting for transfers between devices  59.3 us (25%)
  Pallas kernels  43.2 us (18%)
  other arithmetic  20.2 us (8%)
  local copies, waits for them, and re-layouts  17.5 us (7%)
  between operations  15.1 us (6%)
  blocking collectives  11.3 us (5%)
  matrix products  4.83 us (2%)
    pallas_call x2, Pallas kernels, tile_pass(): pl.pallas_call(body, out_shape=[jax.ShapeDtypeStruct((n, narrow, side), j...  43.2 us
    ppermute x28, waiting for transfers between devices, ring(): return lax.ppermute(a, (axis, 'cols'), moves)  41.3 us
    ppermute x28, starting transfers between devices, ring(): return lax.ppermute(a, (axis, 'cols'), moves)  36.2 us
    all_to_all x5, starting transfers between devices, exchange(): return lax.all_to_all(parts, axis, split_axis=0, concat_axis=0, tiled=True)  33.5 us
    all_to_all x5, waiting for transfers between devices, exchange(): return lax.all_to_all(parts, axis, split_axis=0, concat_axis=0, tiled=True)  17.9 us
    convert_element_type x8, other arithmetic, narrowed(): return add(*terms).astype(jnp.bfloat16)  15.9 us
    all_to_all x1, blocking collectives, exchange(): return lax.all_to_all(parts, axis, split_axis=0, concat_axis=0, tiled=True)  11.3 us
    unnamed x50, local copies, waits for them, and re-layouts  10.2 us
  transfers between devices with their start and end apart: 34, of which 14 were waited for; matrix products, arithmetic and copies ran while one was open for 11% of the time, Pallas kernels for 18%

profile of v4, /device:TPU:1, one launch (start us, length us, event | category | flops | bytes accessed | tf_op | source)
XLA Modules:
  0.0 241.1 jit_solution(15106058155068745284)
XLA Ops:
  8.9 1.0 copy.76
  10.7 6.6 %all-to-all-start = ((bf16[32,32,128]{2,1,0:T(8,128)(2,1)}), bf16[32,32,128]{2,1,0:T(8,128)(2,1)S(1)}, u32[]{:S(2)}, u32[]{:S(2)}) async-start(bf16[32,32,128]{2,1,0:T(8,128)(2,1)} %copy.52), calls=%async_computation | async-start | bytes 524288 | tf_op jit(solution)/shard_map/all_to_all | solution.py:124
  17.3 2.0 collective-permute-start
  21.1 4.0 %collective-permute-done.1 = bf16[12,32,128]{2,1,0:T(8,128)(2,1)S(1)} collective-permute-done((bf16[12,32,128]{2,1,0:T(8,128)(2,1)S(1)}, bf16[12,32,128]{2,1,0:T(8,128)(2,1)S(1)}, u32[]{:S(2)}, u32[]{:S(2)}) %collective-permute-start.1) | collective-permute-done | bytes 98336 | tf_op jit(solution)/shard_map/ppermute | solution.py:150
  26.1 5.7 %collective-permute-start.3 = (bf16[48,32,128]{2,1,0:T(8,128)(2,1)S(1)}, bf16[48,32,128]{2,1,0:T(8,128)(2,1)S(1)}, u32[]{:S(2)}, u32[]{:S(2)}) collective-permute-start(bf16[48,32,128]{2,1,0:T(8,128)(2,1)S(1)} %pad_maximum_fusion.1.rest_1_), channel_id=1, source_target_pairs={{0,32},{1,225},{2,34},{3,227},{4,36},{5,229},{6,38},{7,231},{32,64... | collective-permute-start | bytes 1179656 | tf_op jit(solution)/shard_map/ppermute | solution.py:150
  32.1 11.3 %all_to_all.34.grads_ref = bf16[32,32,128]{2,1,0:T(8,128)(2,1)S(1)} all-to-all(bf16[32,32,128]{2,1,0:T(8,128)(2,1)S(1)} %bitcast.83), channel_id=1, replica_groups=mesh['z'=8,'x'=4,'cols'=8] {'cols'}, dimensions={0} | all-to-all | bytes 524288 | tf_op jit(solution)/shard_map/all_to_all | solution.py:124
  43.8 2.7 %collective-permute-start.5 = (bf16[48,32,128]{2,1,0:T(8,128)(2,1)S(1)}, bf16[48,32,128]{2,1,0:T(8,128)(2,1)}, u32[]{:S(2)}, u32[]{:S(2)}) collective-permute-start(bf16[48,32,128]{2,1,0:T(8,128)(2,1)S(1)} %collective-permute-done.3.rest_8_), channel_id=1, source_target_pairs={{0,32},{1,225},{2,34},{3,227},{4,36},{5,229},{6,38},{7,231},{32,64... | collective-permute-start | bytes 1179656 | tf_op jit(solution)/shard_map/ppermute | solution.py:150
  47.8 8.6 %collective-permute-done.5.rest_7_ = bf16[48,32,128]{2,1,0:T(8,128)(2,1)} collective-permute-done((bf16[48,32,128]{2,1,0:T(8,128)(2,1)S(1)}, bf16[48,32,128]{2,1,0:T(8,128)(2,1)}, u32[]{:S(2)}, u32[]{:S(2)}) %collective-permute-start.5) | collective-permute-done | bytes 393248 | tf_op jit(solution)/shard_map/ppermute | solution.py:150
  56.4 2.4 collective-permute-done.6.rest_3_
  58.7 1.2 collective-permute-start.7
  60.2 18.9 %reverse.1 = (bf16[128,32,128]{2,1,0:T(8,128)(2,1)S(1)}, bf16[128,32,128]{2,1,0:T(8,128)(2,1)S(1)}, bf16[128,32,128]{2,1,0:T(8,128)(2,1)S(1)}, bf16[128,32,128]{...) custom-call(s32[1024]{0:T(1024)S(1)} %copy-done.8, ...), custom_call_target="tpu_custom_call" | custom-call | flops 8589934592 | bytes 42205184 | tf_op jit(solution)/shard_map/reverse/pallas_call | solution.py:105
  82.4 1.0 copy-done.9
  84.1 1.0 copy-done.10
  86.7 1.6 tile.4
  88.3 5.4 %all-to-all-start.2 = ((bf16[8,32,4096]{2,1,0:T(8,128)(2,1)}), bf16[8,32,4096]{2,1,0:T(8,128)(2,1)}, u32[]{:S(2)}, u32[]{:S(2)}) async-start(bf16[8,32,4096]{2,1,0:T(8,128)(2,1)} %tile.4), calls=%async_computation.2 | async-start | bytes 4194304 | tf_op jit(solution)/shard_map/all_to_all | solution.py:124
  93.7 1.9 collective-permute-start.11
  96.2 2.7 %collective-permute-start.9 = (bf16[128,32,128]{2,1,0:T(8,128)(2,1)}, bf16[128,32,128]{2,1,0:T(8,128)(2,1)}, u32[]{:S(2)}, u32[]{:S(2)}) collective-permute-start(bf16[128,32,128]{2,1,0:T(8,128)(2,1)} %copy-done.9), channel_id=1, source_target_pairs={{0,8},{1,25},{2,10},{3,27},{4,12},{5,29},{6,14},{7,31},{8,16},{9,1... | collective-permute-start | bytes 3145736 | tf_op jit(solution)/shard_map/ppermute | solution.py:150
  98.9 8.5 %collective-permute-done.12 = bf16[64,32,128]{2,1,0:T(8,128)(2,1)} collective-permute-done((bf16[64,32,128]{2,1,0:T(8,128)(2,1)}, bf16[64,32,128]{2,1,0:T(8,128)(2,1)}, u32[]{:S(2)}, u32[]{:S(2)}) %collective-permute-start.12) | collective-permute-done | bytes 524320 | tf_op jit(solution)/shard_map/ppermute | solution.py:150
  107.4 2.1 add_convert_fusion.4
  109.9 2.0 add_convert_fusion.5
  111.9 2.2 collective-permute-done.13.rest_5_
  114.2 1.6 collective-permute-start.14
  115.8 24.3 %forward.1 = bf16[32,32,128]{2,1,0:T(8,128)(2,1)} custom-call(s32[1024]{0:T(1024)} %rows_ref.3, s32[1024]{0:T(1024)} %get-tuple-element.129.places_ref, s32[1]{0:T(128)S(6)} %copy.96.count_ref, bf16[640,32,128]{2,1,0:T(8,128)(2,1)} %all-gather.2.cloned.1.call-done.rest_0_, bf16[48,32,128]{2,1,0:T(8,128)(2,1)} %copy-done.14, bf16[48,32,128]{2,1,0:T(8,128)(2,1)} %copy-done.17, ...), custom_call_target="tpu_custom_call" | custom-call | flops 8589934592 | bytes 42205184 | tf_op jit(solution)/shard_map/forward/pallas_call | solution.py:105
  140.1 2.6 %add_convert_fusion = bf16[128,32,128]{2,1,0:T(8,128)(2,1)} fusion(bf16[128,32,128]{2,1,0:T(8,128)(2,1)} %collective-permute-done.9, bf16[128,32,128]{2,1,0:T(8,128)(2,1)S(1)} %get-tuple-element.83), kind=kLoop, calls=%fused_computation | loop fusion | flops 2097152 | bytes 3145728 | tf_op jit(solution)/shard_map/convert_element_type | solution.py:156
  142.7 2.8 %collective-permute-start.16 = (bf16[128,32,128]{2,1,0:T(8,128)(2,1)}, bf16[128,32,128]{2,1,0:T(8,128)(2,1)S(1)}, u32[]{:S(2)}, u32[]{:S(2)}) collective-permute-start(bf16[128,32,128]{2,1,0:T(8,128)(2,1)} %add_convert_fusion), channel_id=1, source_target_pairs={{0,8},{1,25},{2,10},{3,27},{4,12},{5,29},{6,14},{7,31},{8,16},{9,1... | collective-permute-start | bytes 3145736 | tf_op jit(solution)/shard_map/ppermute | solution.py:150
  145.5 2.0 add_convert_fusion.2
  147.5 2.0 add_convert_fusion.3
  149.5 2.7 %collective-permute-start.17 = (bf16[64,32,128]{2,1,0:T(8,128)(2,1)}, bf16[64,32,128]{2,1,0:T(8,128)(2,1)}, u32[]{:S(2)}, u32[]{:S(2)}) collective-permute-start(bf16[64,32,128]{2,1,0:T(8,128)(2,1)} %add_convert_fusion.3), channel_id=1, source_target_pairs={{0,32},{1,225},{2,34},{3,227},{4,36},{5,229},{6,38},{7,231},{32,64... | collective-permute-start | bytes 1572872 | tf_op jit(solution)/shard_map/ppermute | solution.py:150
  152.1 4.3 %all-to-all-start.3 = ((bf16[32,32,128]{2,1,0:T(8,128)(2,1)}), bf16[32,32,128]{2,1,0:T(8,128)(2,1)S(1)}, u32[]{:S(2)}, u32[]{:S(2)}) async-start(bf16[32,32,128]{2,1,0:T(8,128)(2,1)} %forward.1), calls=%async_computation.3 | async-start | bytes 524288 | tf_op jit(solution)/shard_map/all_to_all | solution.py:124
  156.4 2.4 convolution_convert_fusion
  158.9 4.1 %all-to-all-done.3 = bf16[32,32,128]{2,1,0:T(8,128)(2,1)S(1)} async-done(((bf16[32,32,128]{2,1,0:T(8,128)(2,1)}), bf16[32,32,128]{2,1,0:T(8,128)(2,1)S(1)}, u32[]{:S(2)}, u32[]{:S(2)}) %all-to-all-start.3) | async-done | bytes 262176 | tf_op jit(solution)/shard_map/all_to_all | solution.py:124
  163.0 2.0 add_convert_fusion.1
  165.7 1.2 add_convert_fusion.6
  166.9 2.9 %collective-permute-start.19 = (bf16[32,32,128]{2,1,0:T(8,128)(2,1)S(1)}, bf16[32,32,128]{2,1,0:T(8,128)(2,1)S(1)}, u32[]{:S(2)}, u32[]{:S(2)}) collective-permute-start(bf16[32,32,128]{2,1,0:T(8,128)(2,1)S(1)} %get-tuple-element.125), channel_id=1, source_target_pairs={{0,64},{1,193},{2,66},{3,195},{4,68},{5,197},{6,70},{7,199},{32,96... | collective-permute-start | bytes 786440 | tf_op jit(solution)/shard_map/ppermute | solution.py:150
  169.8 1.2 copy.58
  171.0 9.6 %collective-permute-done.19 = bf16[32,32,128]{2,1,0:T(8,128)(2,1)S(1)} collective-permute-done((bf16[32,32,128]{2,1,0:T(8,128)(2,1)S(1)}, bf16[32,32,128]{2,1,0:T(8,128)(2,1)S(1)}, u32[]{:S(2)}, u32[]{:S(2)}) %collective-permute-start.19) | collective-permute-done | bytes 262176 | tf_op jit(solution)/shard_map/ppermute | solution.py:150
  180.6 3.8 %collective-permute-done.20 = bf16[32,32,128]{2,1,0:T(8,128)(2,1)} collective-permute-done((bf16[32,32,128]{2,1,0:T(8,128)(2,1)S(1)}, bf16[32,32,128]{2,1,0:T(8,128)(2,1)}, u32[]{:S(2)}, u32[]{:S(2)}) %collective-permute-start.20) | collective-permute-done | bytes 262176 | tf_op jit(solution)/shard_map/ppermute | solution.py:150
  184.4 2.0 add_convert_fusion.11
  186.4 1.7 collective-permute-start.22
  188.1 1.7 collective-permute-start.23
  190.9 8.3 %all-to-all-start.4 = ((bf16[32,32,256]{2,1,0:T(8,128)(2,1)}), bf16[32,32,256]{2,1,0:T(8,128)(2,1)S(1)}, u32[]{:S(2)}, u32[]{:S(2)}) async-start(bf16[32,32,256]{2,1,0:T(8,128)(2,1)} %tile.5), calls=%async_computation.4 | async-start | bytes 1048576 | tf_op jit(solution)/shard_map/all_to_all | solution.py:124
  199.2 2.1 fusion.2
  201.3 1.2 add_convert_fusion.8
  202.5 1.5 fusion.25
  204.0 2.5 %collective-permute-start.25 = (bf16[16,32,128]{2,1,0:T(8,128)(2,1)S(1)}, bf16[16,32,128]{2,1,0:T(8,128)(2,1)S(1)}, u32[]{:S(2)}, u32[]{:S(2)}) collective-permute-start(bf16[16,32,128]{2,1,0:T(8,128)(2,1)S(1)} %get-tuple-element.126), channel_id=1, source_target_pairs={{0,8},{1,25},{2,10},{3,27},{4,12},{5,29},{6,14},{7,31},{8,16},{9,1... | collective-permute-start | bytes 393224 | tf_op jit(solution)/shard_map/ppermute | solution.py:150
  207.7 5.2 %all-to-all-done.4 = bf16[32,32,256]{2,1,0:T(8,128)(2,1)S(1)} async-done(((bf16[32,32,256]{2,1,0:T(8,128)(2,1)}), bf16[32,32,256]{2,1,0:T(8,128)(2,1)S(1)}, u32[]{:S(2)}, u32[]{:S(2)}) %all-to-all-start.4) | async-done | bytes 524320 | tf_op jit(solution)/shard_map/all_to_all | solution.py:124
  214.1 8.9 %all-to-all-start.5 = ((bf16[8,8,32,128]{3,2,1,0:T(8,128)(2,1)}), bf16[8,8,32,128]{3,2,1,0:T(8,128)(2,1)S(1)}, u32[]{:S(2)}, u32[]{:S(2)}) async-start(bf16[8,8,32,128]{3,2,1,0:T(8,128)(2,1)} %copy.60), calls=%async_computation.5 | async-start | bytes 1048576 | tf_op jit(solution)/shard_map/all_to_all | solution.py:124
  223.9 8.7 %all-to-all-done.5 = bf16[8,8,32,128]{3,2,1,0:T(8,128)(2,1)S(1)} async-done(((bf16[8,8,32,128]{3,2,1,0:T(8,128)(2,1)}), bf16[8,8,32,128]{3,2,1,0:T(8,128)(2,1)S(1)}, u32[]{:S(2)}, u32[]{:S(2)}) %all-to-all-start.5) | async-done | bytes 524320 | tf_op jit(solution)/shard_map/all_to_all | solution.py:124
  (113 shorter events, 20.2 us)
Async XLA Ops:
  7.2 13.2 %copy-start.22 = (bf16[256,256]{1,0:T(8,128)(2,1)S(1)}, bf16[256,256]{1,0:T(8,128)(2,1)}, u32[]{:S(2)}) copy-start(bf16[256,256]{1,0:T(8,128)(2,1)} %param.8) | copy-start | bytes 393220
  7.2 108.6 %all-gather.2.cloned.1.call-start = ((), (), s32[]{:S(2)}) async-start(), calls=%async_computation.6 | async-start | bytes 5406720 | tf_op jit(solution)/shard_map/all_gather | solution.py:177
  10.7 15.4 %all-to-all-start = ((bf16[32,32,128]{2,1,0:T(8,128)(2,1)}), bf16[32,32,128]{2,1,0:T(8,128)(2,1)S(1)}, u32[]{:S(2)}, u32[]{:S(2)}) async-start(bf16[32,32,128]{2,1,0:T(8,128)(2,1)} %copy.52), calls=%async_computation | async-start | bytes 524288 | tf_op jit(solution)/shard_map/all_to_all | solution.py:124
  17.2 29.9 %copy-start.23 = (s32[1024]{0:T(1024)S(1)}, s32[1024]{0:T(1024)}, u32[]{:S(2)}) copy-start(s32[1024]{0:T(1024)} %param.11) | copy-start | bytes 12292
  17.3 43.0 %copy-start.8 = (s32[1024]{0:T(1024)S(1)}, s32[1024]{0:T(1024)}, u32[]{:S(2)}) copy-start(s32[1024]{0:T(1024)} %rows_ref.3) | copy-start | bytes 12292
  17.3 3.8 %collective-permute-start = (bf16[12,32,128]{2,1,0:T(8,128)(2,1)S(1)}, bf16[12,32,128]{2,1,0:T(8,128)(2,1)S(1)}, u32[]{:S(2)}, u32[]{:S(2)}) collective-permute-start(bf16[12,32,128]{2,1,0:T(8,128)(2,1)S(1)} %slice.134), channel_id=1, source_target_pairs={{0,8},{1,25},{2,10},{3,27},{4,12},{5,29},{6,14},{7,31},{8,16},{9,1... | collective-permute-start | bytes 294920 | tf_op jit(solution)/shard_map/ppermute | solution.py:150
  19.2 5.9 %collective-permute-start.1 = (bf16[12,32,128]{2,1,0:T(8,128)(2,1)S(1)}, bf16[12,32,128]{2,1,0:T(8,128)(2,1)S(1)}, u32[]{:S(2)}, u32[]{:S(2)}) collective-permute-start(bf16[12,32,128]{2,1,0:T(8,128)(2,1)S(1)} %slice.134), channel_id=1, source_target_pairs={{0,16},{1,17},{2,18},{3,19},{4,20},{5,21},{6,22},{7,23},{8,24},{9,... | collective-permute-start | bytes 294920 | tf_op jit(solution)/shard_map/ppermute | solution.py:150
  19.8 6.3 %collective-permute-start.2 = (bf16[12,32,128]{2,1,0:T(8,128)(2,1)S(1)}, bf16[12,32,128]{2,1,0:T(8,128)(2,1)S(1)}, u32[]{:S(2)}, u32[]{:S(2)}) collective-permute-start(bf16[12,32,128]{2,1,0:T(8,128)(2,1)S(1)} %slice.134), channel_id=1, source_target_pairs={{0,24},{1,9},{2,26},{3,11},{4,28},{5,13},{6,30},{7,15},{8,0},{9,17... | collective-permute-start | bytes 294920 | tf_op jit(solution)/shard_map/ppermute | solution.py:150
  20.6 39.6 %copy-start.12 = (bf16[8,32,8,32]{3,2,1,0:T(8,128)(2,1)}, bf16[8,32,8,32]{3,2,1,0:T(8,128)(2,1)S(1)}, u32[]{:S(2)}) copy-start(bf16[8,32,8,32]{3,2,1,0:T(8,128)(2,1)S(1)} %reshape.64) | copy-start | bytes 393220
  26.1 34.1 %copy-start.14 = (bf16[48,32,128]{2,1,0:T(8,128)(2,1)}, bf16[48,32,128]{2,1,0:T(8,128)(2,1)S(1)}, u32[]{:S(2)}) copy-start(bf16[48,32,128]{2,1,0:T(8,128)(2,1)S(1)} %pad_maximum_fusion.1.rest_1_) | copy-start | bytes 1179652
  26.1 17.2 %collective-permute-start.3 = (bf16[48,32,128]{2,1,0:T(8,128)(2,1)S(1)}, bf16[48,32,128]{2,1,0:T(8,128)(2,1)S(1)}, u32[]{:S(2)}, u32[]{:S(2)}) collective-permute-start(bf16[48,32,128]{2,1,0:T(8,128)(2,1)S(1)} %pad_maximum_fusion.1.rest_1_), channel_id=1, source_target_pairs={{0,32},{1,225},{2,34},{3,227},{4,36},{5,229},{6,38},{7,231},{32,64... | collective-permute-start | bytes 1179656 | tf_op jit(solution)/shard_map/ppermute | solution.py:150
  31.8 12.0 %collective-permute-start.4 = (bf16[48,32,128]{2,1,0:T(8,128)(2,1)S(1)}, bf16[48,32,128]{2,1,0:T(8,128)(2,1)S(1)}, u32[]{:S(2)}, u32[]{:S(2)}) collective-permute-start(bf16[48,32,128]{2,1,0:T(8,128)(2,1)S(1)} %pad_maximum_fusion.1.rest_1_), channel_id=1, source_target_pairs={{0,224},{1,33},{2,226},{3,35},{4,228},{5,37},{6,230},{7,39},{32,0}... | collective-permute-start | bytes 1179656 | tf_op jit(solution)/shard_map/ppermute | solution.py:150
  43.4 16.9 %copy-start.16 = (bf16[48,32,128]{2,1,0:T(8,128)(2,1)}, bf16[48,32,128]{2,1,0:T(8,128)(2,1)S(1)}, u32[]{:S(2)}) copy-start(bf16[48,32,128]{2,1,0:T(8,128)(2,1)S(1)} %collective-permute-done.3.rest_8_) | copy-start | bytes 1179652
  43.8 16.5 %copy-start.17 = (bf16[48,32,128]{2,1,0:T(8,128)(2,1)}, bf16[48,32,128]{2,1,0:T(8,128)(2,1)S(1)}, u32[]{:S(2)}) copy-start(bf16[48,32,128]{2,1,0:T(8,128)(2,1)S(1)} %collective-permute-done.4.rest_2_) | copy-start | bytes 1179652
  43.8 12.6 %collective-permute-start.5 = (bf16[48,32,128]{2,1,0:T(8,128)(2,1)S(1)}, bf16[48,32,128]{2,1,0:T(8,128)(2,1)}, u32[]{:S(2)}, u32[]{:S(2)}) collective-permute-start(bf16[48,32,128]{2,1,0:T(8,128)(2,1)S(1)} %collective-permute-done.3.rest_8_), channel_id=1, source_target_pairs={{0,32},{1,225},{2,34},{3,227},{4,36},{5,229},{6,38},{7,231},{32,64... | collective-permute-start | bytes 1179656 | tf_op jit(solution)/shard_map/ppermute | solution.py:150
  46.5 12.3 %collective-permute-start.6 = (bf16[48,32,128]{2,1,0:T(8,128)(2,1)S(1)}, bf16[48,32,128]{2,1,0:T(8,128)(2,1)}, u32[]{:S(2)}, u32[]{:S(2)}) collective-permute-start(bf16[48,32,128]{2,1,0:T(8,128)(2,1)S(1)} %collective-permute-done.4.rest_2_), channel_id=1, source_target_pairs={{0,224},{1,33},{2,226},{3,35},{4,228},{5,37},{6,230},{7,39},{32,0}... | collective-permute-start | bytes 1179656 | tf_op jit(solution)/shard_map/ppermute | solution.py:150
  58.7 25.4 %collective-permute-start.7 = (bf16[48,32,128]{2,1,0:T(8,128)(2,1)}, bf16[48,32,128]{2,1,0:T(8,128)(2,1)S(1)}, u32[]{:S(2)}, u32[]{:S(2)}) collective-permute-start(bf16[48,32,128]{2,1,0:T(8,128)(2,1)} %collective-permute-done.5.rest_7_), channel_id=1, source_target_pairs={{0,32},{1,225},{2,34},{3,227},{4,36},{5,229},{6,38},{7,231},{32,64... | collective-permute-start | bytes 1179656 | tf_op jit(solution)/shard_map/ppermute | solution.py:150
  59.9 25.3 %collective-permute-start.8 = (bf16[48,32,128]{2,1,0:T(8,128)(2,1)}, bf16[48,32,128]{2,1,0:T(8,128)(2,1)S(1)}, u32[]{:S(2)}, u32[]{:S(2)}) collective-permute-start(bf16[48,32,128]{2,1,0:T(8,128)(2,1)} %collective-permute-done.6.rest_3_), channel_id=1, source_target_pairs={{0,224},{1,33},{2,226},{3,35},{4,228},{5,37},{6,230},{7,39},{32,0}... | collective-permute-start | bytes 1179656 | tf_op jit(solution)/shard_map/ppermute | solution.py:150
  60.2 26.4 %copy-start.15 = (bf16[32,4096]{1,0:T(8,128)(2,1)S(1)}, bf16[32,4096]{1,0:T(8,128)(2,1)}, u32[]{:S(2)}) copy-start(bf16[32,4096]{1,0:T(8,128)(2,1)} %param.13) | copy-start | bytes 786436
  86.7 20.7 %collective-permute-start.12 = (bf16[64,32,128]{2,1,0:T(8,128)(2,1)}, bf16[64,32,128]{2,1,0:T(8,128)(2,1)}, u32[]{:S(2)}, u32[]{:S(2)}) collective-permute-start(bf16[64,32,128]{2,1,0:T(8,128)(2,1)} %get-tuple-element.89), channel_id=1, source_target_pairs={{0,224},{1,33},{2,226},{3,35},{4,228},{5,37},{6,230},{7,39},{32,0}... | collective-permute-start | bytes 1572872 | tf_op jit(solution)/shard_map/ppermute | solution.py:150
  88.3 51.8 %all-to-all-start.2 = ((bf16[8,32,4096]{2,1,0:T(8,128)(2,1)}), bf16[8,32,4096]{2,1,0:T(8,128)(2,1)}, u32[]{:S(2)}, u32[]{:S(2)}) async-start(bf16[8,32,4096]{2,1,0:T(8,128)(2,1)} %tile.4), calls=%async_computation.2 | async-start | bytes 4194304 | tf_op jit(solution)/shard_map/all_to_all | solution.py:124
  93.7 16.3 %collective-permute-start.11 = (bf16[64,32,128]{2,1,0:T(8,128)(2,1)}, bf16[64,32,128]{2,1,0:T(8,128)(2,1)S(1)}, u32[]{:S(2)}, u32[]{:S(2)}) collective-permute-start(bf16[64,32,128]{2,1,0:T(8,128)(2,1)} %copy-done.11), channel_id=1, source_target_pairs={{0,32},{1,225},{2,34},{3,227},{4,36},{5,229},{6,38},{7,231},{32,64... | collective-permute-start | bytes 1572872 | tf_op jit(solution)/shard_map/ppermute | solution.py:150
  95.6 18.6 %collective-permute-start.13 = (bf16[48,32,128]{2,1,0:T(8,128)(2,1)}, bf16[48,32,128]{2,1,0:T(8,128)(2,1)}, u32[]{:S(2)}, u32[]{:S(2)}) collective-permute-start(bf16[48,32,128]{2,1,0:T(8,128)(2,1)} %copy-done.18), channel_id=1, source_target_pairs={{0,32},{1,225},{2,34},{3,227},{4,36},{5,229},{6,38},{7,231},{32,64... | collective-permute-start | bytes 1179656 | tf_op jit(solution)/shard_map/ppermute | solution.py:150
  96.2 43.9 %collective-permute-start.10 = (bf16[128,32,128]{2,1,0:T(8,128)(2,1)}, bf16[128,32,128]{2,1,0:T(8,128)(2,1)}, u32[]{:S(2)}, u32[]{:S(2)}) collective-permute-start(bf16[128,32,128]{2,1,0:T(8,128)(2,1)} %copy-done.10), channel_id=1, source_target_pairs={{0,24},{1,9},{2,26},{3,11},{4,28},{5,13},{6,30},{7,15},{8,0},{9,17... | collective-permute-start | bytes 3145736 | tf_op jit(solution)/shard_map/ppermute | solution.py:150
  96.2 43.9 %collective-permute-start.9 = (bf16[128,32,128]{2,1,0:T(8,128)(2,1)}, bf16[128,32,128]{2,1,0:T(8,128)(2,1)}, u32[]{:S(2)}, u32[]{:S(2)}) collective-permute-start(bf16[128,32,128]{2,1,0:T(8,128)(2,1)} %copy-done.9), channel_id=1, source_target_pairs={{0,8},{1,25},{2,10},{3,27},{4,12},{5,29},{6,14},{7,31},{8,16},{9,1... | collective-permute-start | bytes 3145736 | tf_op jit(solution)/shard_map/ppermute | solution.py:150
  114.2 25.9 %collective-permute-start.14 = (bf16[64,32,128]{2,1,0:T(8,128)(2,1)}, bf16[64,32,128]{2,1,0:T(8,128)(2,1)}, u32[]{:S(2)}, u32[]{:S(2)}) collective-permute-start(bf16[64,32,128]{2,1,0:T(8,128)(2,1)} %add_convert_fusion.5), channel_id=1, source_target_pairs={{0,32},{1,225},{2,34},{3,227},{4,36},{5,229},{6,38},{7,231},{32,64... | collective-permute-start | bytes 1572872 | tf_op jit(solution)/shard_map/ppermute | solution.py:150
  115.8 24.3 %collective-permute-start.15 = (bf16[64,32,128]{2,1,0:T(8,128)(2,1)}, bf16[64,32,128]{2,1,0:T(8,128)(2,1)}, u32[]{:S(2)}, u32[]{:S(2)}) collective-permute-start(bf16[64,32,128]{2,1,0:T(8,128)(2,1)} %add_convert_fusion.4), channel_id=1, source_target_pairs={{0,224},{1,33},{2,226},{3,35},{4,228},{5,37},{6,230},{7,39},{32,0}... | collective-permute-start | bytes 1572872 | tf_op jit(solution)/shard_map/ppermute | solution.py:150
  140.1 5.4 %copy-start.3 = (bf16[64,32,128]{2,1,0:T(8,128)(2,1)S(1)}, bf16[64,32,128]{2,1,0:T(8,128)(2,1)}, u32[]{:S(2)}) copy-start(bf16[64,32,128]{2,1,0:T(8,128)(2,1)} %copy-done.2) | copy-start | bytes 1572868
  142.7 20.2 %collective-permute-start.16 = (bf16[128,32,128]{2,1,0:T(8,128)(2,1)}, bf16[128,32,128]{2,1,0:T(8,128)(2,1)S(1)}, u32[]{:S(2)}, u32[]{:S(2)}) collective-permute-start(bf16[128,32,128]{2,1,0:T(8,128)(2,1)} %add_convert_fusion), channel_id=1, source_target_pairs={{0,8},{1,25},{2,10},{3,27},{4,12},{5,29},{6,14},{7,31},{8,16},{9,1... | collective-permute-start | bytes 3145736 | tf_op jit(solution)/shard_map/ppermute | solution.py:150
  147.5 15.4 %collective-permute-start.18 = (bf16[64,32,128]{2,1,0:T(8,128)(2,1)}, bf16[64,32,128]{2,1,0:T(8,128)(2,1)}, u32[]{:S(2)}, u32[]{:S(2)}) collective-permute-start(bf16[64,32,128]{2,1,0:T(8,128)(2,1)} %add_convert_fusion.2), channel_id=1, source_target_pairs={{0,224},{1,33},{2,226},{3,35},{4,228},{5,37},{6,230},{7,39},{32,0}... | collective-permute-start | bytes 1572872 | tf_op jit(solution)/shard_map/ppermute | solution.py:150
  149.5 13.5 %collective-permute-start.17 = (bf16[64,32,128]{2,1,0:T(8,128)(2,1)}, bf16[64,32,128]{2,1,0:T(8,128)(2,1)}, u32[]{:S(2)}, u32[]{:S(2)}) collective-permute-start(bf16[64,32,128]{2,1,0:T(8,128)(2,1)} %add_convert_fusion.3), channel_id=1, source_target_pairs={{0,32},{1,225},{2,34},{3,227},{4,36},{5,229},{6,38},{7,231},{32,64... | collective-permute-start | bytes 1572872 | tf_op jit(solution)/shard_map/ppermute | solution.py:150
  152.1 10.8 %all-to-all-start.3 = ((bf16[32,32,128]{2,1,0:T(8,128)(2,1)}), bf16[32,32,128]{2,1,0:T(8,128)(2,1)S(1)}, u32[]{:S(2)}, u32[]{:S(2)}) async-start(bf16[32,32,128]{2,1,0:T(8,128)(2,1)} %forward.1), calls=%async_computation.3 | async-start | bytes 524288 | tf_op jit(solution)/shard_map/all_to_all | solution.py:124
  158.9 11.0 %copy-start.13 = (bf16[8,32,8,32]{3,2,1,0:T(8,128)(2,1)S(1)}, bf16[8,32,8,32]{3,2,1,0:T(8,128)(2,1)}, u32[]{:S(2)}) copy-start(bf16[8,32,8,32]{3,2,1,0:T(8,128)(2,1)} %copy-done.12) | copy-start | bytes 393220
  162.9 4.0 %copy-start.20 = (bf16[32,32,128]{2,1,0:T(8,128)(2,1)}, bf16[32,32,128]{2,1,0:T(8,128)(2,1)S(1)}, u32[]{:S(2)}) copy-start(bf16[32,32,128]{2,1,0:T(8,128)(2,1)S(1)} %all-to-all-done.3) | copy-start | bytes 786436
  165.0 25.1 %collective-permute-start.21 = (bf16[64,32,128]{2,1,0:T(8,128)(2,1)}, bf16[64,32,128]{2,1,0:T(8,128)(2,1)}, u32[]{:S(2)}, u32[]{:S(2)}) collective-permute-start(bf16[64,32,128]{2,1,0:T(8,128)(2,1)} %add_convert_fusion.1), channel_id=1, source_target_pairs={{0,32},{1,225},{2,34},{3,227},{4,36},{5,229},{6,38},{7,231},{32,64... | collective-permute-start | bytes 1572872 | tf_op jit(solution)/shard_map/ppermute | solution.py:150
  166.9 13.7 %collective-permute-start.19 = (bf16[32,32,128]{2,1,0:T(8,128)(2,1)S(1)}, bf16[32,32,128]{2,1,0:T(8,128)(2,1)S(1)}, u32[]{:S(2)}, u32[]{:S(2)}) collective-permute-start(bf16[32,32,128]{2,1,0:T(8,128)(2,1)S(1)} %get-tuple-element.125), channel_id=1, source_target_pairs={{0,64},{1,193},{2,66},{3,195},{4,68},{5,197},{6,70},{7,199},{32,96... | collective-permute-start | bytes 786440 | tf_op jit(solution)/shard_map/ppermute | solution.py:150
  169.8 14.5 %collective-permute-start.20 = (bf16[32,32,128]{2,1,0:T(8,128)(2,1)S(1)}, bf16[32,32,128]{2,1,0:T(8,128)(2,1)}, u32[]{:S(2)}, u32[]{:S(2)}) collective-permute-start(bf16[32,32,128]{2,1,0:T(8,128)(2,1)S(1)} %get-tuple-element.124), channel_id=1, source_target_pairs={{0,192},{1,65},{2,194},{3,67},{4,196},{5,69},{6,198},{7,71},{32,22... | collective-permute-start | bytes 786440 | tf_op jit(solution)/shard_map/ppermute | solution.py:150
  186.4 15.0 %collective-permute-start.22 = (bf16[16,32,128]{2,1,0:T(8,128)(2,1)}, bf16[16,32,128]{2,1,0:T(8,128)(2,1)S(1)}, u32[]{:S(2)}, u32[]{:S(2)}) collective-permute-start(bf16[16,32,128]{2,1,0:T(8,128)(2,1)} %get-tuple-element.121), channel_id=1, source_target_pairs={{0,64},{1,193},{2,66},{3,195},{4,68},{5,197},{6,70},{7,199},{32,96... | collective-permute-start | bytes 393224 | tf_op jit(solution)/shard_map/ppermute | solution.py:150
  188.1 13.2 %collective-permute-start.23 = (bf16[16,32,128]{2,1,0:T(8,128)(2,1)}, bf16[16,32,128]{2,1,0:T(8,128)(2,1)S(1)}, u32[]{:S(2)}, u32[]{:S(2)}) collective-permute-start(bf16[16,32,128]{2,1,0:T(8,128)(2,1)} %get-tuple-element.122), channel_id=1, source_target_pairs={{0,32},{1,225},{2,34},{3,227},{4,36},{5,229},{6,38},{7,231},{32,64... | collective-permute-start | bytes 393224 | tf_op jit(solution)/shard_map/ppermute | solution.py:150
  189.8 12.7 %copy-start.7 = (bf16[64,32,128]{2,1,0:T(8,128)(2,1)S(1)}, bf16[64,32,128]{2,1,0:T(8,128)(2,1)}, u32[]{:S(2)}) copy-start(bf16[64,32,128]{2,1,0:T(8,128)(2,1)} %copy-done.6) | copy-start | bytes 1572868
  189.9 11.5 %collective-permute-start.24 = (bf16[16,32,128]{2,1,0:T(8,128)(2,1)S(1)}, bf16[16,32,128]{2,1,0:T(8,128)(2,1)}, u32[]{:S(2)}, u32[]{:S(2)}) collective-permute-start(bf16[16,32,128]{2,1,0:T(8,128)(2,1)S(1)} %get-tuple-element.123), channel_id=1, source_target_pairs={{0,224},{1,33},{2,226},{3,35},{4,228},{5,37},{6,230},{7,39},{32,0}... | collective-permute-start | bytes 393224 | tf_op jit(solution)/shard_map/ppermute | solution.py:150
  190.9 22.0 %all-to-all-start.4 = ((bf16[32,32,256]{2,1,0:T(8,128)(2,1)}), bf16[32,32,256]{2,1,0:T(8,128)(2,1)S(1)}, u32[]{:S(2)}, u32[]{:S(2)}) async-start(bf16[32,32,256]{2,1,0:T(8,128)(2,1)} %tile.5), calls=%async_computation.4 | async-start | bytes 1048576 | tf_op jit(solution)/shard_map/all_to_all | solution.py:124
  202.5 10.7 %copy-start.21 = (bf16[8,4,32,128]{3,2,0,1:T(8,128)(2,1)S(1)}, bf16[8,4,32,128]{3,2,0,1:T(8,128)(2,1)}, u32[]{:S(2)}) copy-start(bf16[8,4,32,128]{3,2,0,1:T(8,128)(2,1)} %fusion.2) | copy-start | bytes 786436
  204.0 19.0 %collective-permute-start.25 = (bf16[16,32,128]{2,1,0:T(8,128)(2,1)S(1)}, bf16[16,32,128]{2,1,0:T(8,128)(2,1)S(1)}, u32[]{:S(2)}, u32[]{:S(2)}) collective-permute-start(bf16[16,32,128]{2,1,0:T(8,128)(2,1)S(1)} %get-tuple-element.126), channel_id=1, source_target_pairs={{0,8},{1,25},{2,10},{3,27},{4,12},{5,29},{6,14},{7,31},{8,16},{9,1... | collective-permute-start | bytes 393224 | tf_op jit(solution)/shard_map/ppermute | solution.py:150
  206.6 16.5 %collective-permute-start.26 = (bf16[16,32,128]{2,1,0:T(8,128)(2,1)S(1)}, bf16[16,32,128]{2,1,0:T(8,128)(2,1)S(1)}, u32[]{:S(2)}, u32[]{:S(2)}) collective-permute-start(bf16[16,32,128]{2,1,0:T(8,128)(2,1)S(1)} %get-tuple-element.128), channel_id=1, source_target_pairs={{0,16},{1,17},{2,18},{3,19},{4,20},{5,21},{6,22},{7,23},{8,24},{9,... | collective-permute-start | bytes 393224 | tf_op jit(solution)/shard_map/ppermute | solution.py:150
  207.1 15.9 %collective-permute-start.27 = (bf16[16,32,128]{2,1,0:T(8,128)(2,1)S(1)}, bf16[16,32,128]{2,1,0:T(8,128)(2,1)S(1)}, u32[]{:S(2)}, u32[]{:S(2)}) collective-permute-start(bf16[16,32,128]{2,1,0:T(8,128)(2,1)S(1)} %get-tuple-element.127), channel_id=1, source_target_pairs={{0,24},{1,9},{2,26},{3,11},{4,28},{5,13},{6,30},{7,15},{8,0},{9,17... | collective-permute-start | bytes 393224 | tf_op jit(solution)/shard_map/ppermute | solution.py:150
  214.1 18.4 %all-to-all-start.5 = ((bf16[8,8,32,128]{3,2,1,0:T(8,128)(2,1)}), bf16[8,8,32,128]{3,2,1,0:T(8,128)(2,1)S(1)}, u32[]{:S(2)}, u32[]{:S(2)}) async-start(bf16[8,8,32,128]{3,2,1,0:T(8,128)(2,1)} %copy.60), calls=%async_computation.5 | async-start | bytes 1048576 | tf_op jit(solution)/shard_map/all_to_all | solution.py:124
  223.0 11.2 %copy-start.1 = (bf16[32,4096]{1,0:T(8,128)(2,1)S(1)}, bf16[32,4096]{1,0:T(8,128)(2,1)}, u32[]{:S(2)}) copy-start(bf16[32,4096]{1,0:T(8,128)(2,1)} %param.7) | copy-start | bytes 786436
  (10 other events, 8.5 us)
Sparse Core Ops, SparseCore 0:
  11.2 92.6 all-gather.1

commit v5 on v3

--- a/solution.py
+++ b/solution.py
@@ -237,8 +237,8 @@
     n34 = ring(narrowed(*held(3, 4)), "z", nz, 2)
     n56 = ring(narrowed(*held(5, 6)), "z", nz, -2)
     ahead = ring(narrowed(by_z[1], ahead), "z", nz, 1)
-    n34, n56, term, mixed_full = together(n34, n56, term, mixed_full)
     shares = to_all(term[None], ("z", "x"))
+    n34, n56, shares, mixed_full = together(n34, n56, shares, mixed_full)
     aggregated = jnp.einsum(
         "cfdg,cbfn->dbgn", per_col, mixed_full, preferred_element_type=jnp.float32
     ).astype(jnp.bfloat16)

time: 237 us -> 234 us (0.987)
  waiting for transfers between devices: 56.3 us -> 48 us
  other arithmetic: 18.1 us -> 23.6 us
    all_to_all x5, waiting for transfers between devices: 17.4 us -> 11.6 us  [exchange(): return lax.all_to_all(parts, axis, split_axis=0, concat_axis=0, tiled=True)]
    convert_element_type x8, other arithmetic: 13.6 us -> 17.1 us  [narrowed(): return add(*terms).astype(jnp.bfloat16)]
    ppermute x28, waiting for transfers between devices: 38.8 us -> 36.4 us  [ring(): return lax.ppermute(a, (axis, 'cols'), moves)]
    unnamed x58 -> x56, local copies, waits for them, and re-layouts: 10.9 us -> 10.2 us
  transfers between devices with their start and end apart: 34 -> 34, of which waited for: 14 -> 15; matrix products, arithmetic and copies ran while one was open for 11% -> 11% of each run, Pallas kernels for 15% -> 16%
where the time goes in v5:
time: 234 us
  starting transfers between devices  77.2 us (33%)
  waiting for transfers between devices  48 us (21%)
  Pallas kernels  38.3 us (16%)
  other arithmetic  23.6 us (10%)
  local copies, waits for them, and re-layouts  17.5 us (7%)
  between operations  15.1 us (6%)
  blocking collectives  11.3 us (5%)
  matrix products  3 us (1%)
    ppermute x28, starting transfers between devices, ring(): return lax.ppermute(a, (axis, 'cols'), moves)  44.2 us
    pallas_call x2, Pallas kernels, tile_pass(): pl.pallas_call(body, out_shape=[jax.ShapeDtypeStruct((n, narrow, side), j...  38.3 us
    ppermute x28, waiting for transfers between devices, ring(): return lax.ppermute(a, (axis, 'cols'), moves)  36.4 us
    all_to_all x5, starting transfers between devices, exchange(): return lax.all_to_all(parts, axis, split_axis=0, concat_axis=0, tiled=True)  33 us
    convert_element_type x8, other arithmetic, narrowed(): return add(*terms).astype(jnp.bfloat16)  17.1 us
    all_to_all x5, waiting for transfers between devices, exchange(): return lax.all_to_all(parts, axis, split_axis=0, concat_axis=0, tiled=True)  11.6 us
    all_to_all x1, blocking collectives, exchange(): return lax.all_to_all(parts, axis, split_axis=0, concat_axis=0, tiled=True)  11.3 us
    unnamed x56, local copies, waits for them, and re-layouts  10.2 us
  transfers between devices with their start and end apart: 34, of which 15 were waited for; matrix products, arithmetic and copies ran while one was open for 11% of the time, Pallas kernels for 16%

profile of v5, /device:TPU:1, one launch (start us, length us, event | category | flops | bytes accessed | tf_op | source)
XLA Modules:
  0.0 233.9 jit_solution(15562821252275097750)
XLA Ops:
  8.9 1.0 copy.76
  10.7 6.6 %all-to-all-start = ((bf16[32,32,128]{2,1,0:T(8,128)(2,1)}), bf16[32,32,128]{2,1,0:T(8,128)(2,1)S(1)}, u32[]{:S(2)}, u32[]{:S(2)}) async-start(bf16[32,32,128]{2,1,0:T(8,128)(2,1)} %copy.52), calls=%async_computation | async-start | bytes 524288 | tf_op jit(solution)/shard_map/all_to_all | solution.py:124
  17.3 2.0 collective-permute-start
  21.1 4.0 %collective-permute-done.1 = bf16[12,32,128]{2,1,0:T(8,128)(2,1)S(1)} collective-permute-done((bf16[12,32,128]{2,1,0:T(8,128)(2,1)S(1)}, bf16[12,32,128]{2,1,0:T(8,128)(2,1)S(1)}, u32[]{:S(2)}, u32[]{:S(2)}) %collective-permute-start.1) | collective-permute-done | bytes 98336 | tf_op jit(solution)/shard_map/ppermute | solution.py:150
  26.1 5.7 %collective-permute-start.3 = (bf16[48,32,128]{2,1,0:T(8,128)(2,1)S(1)}, bf16[48,32,128]{2,1,0:T(8,128)(2,1)S(1)}, u32[]{:S(2)}, u32[]{:S(2)}) collective-permute-start(bf16[48,32,128]{2,1,0:T(8,128)(2,1)S(1)} %pad_maximum_fusion.1.rest_1_), channel_id=1, source_target_pairs={{0,32},{1,225},{2,34},{3,227},{4,36},{5,229},{6,38},{7,231},{32,64... | collective-permute-start | bytes 1179656 | tf_op jit(solution)/shard_map/ppermute | solution.py:150
  32.1 11.3 %all_to_all.34.grads_ref = bf16[32,32,128]{2,1,0:T(8,128)(2,1)S(1)} all-to-all(bf16[32,32,128]{2,1,0:T(8,128)(2,1)S(1)} %bitcast.83), channel_id=1, replica_groups=mesh['z'=8,'x'=4,'cols'=8] {'cols'}, dimensions={0} | all-to-all | bytes 524288 | tf_op jit(solution)/shard_map/all_to_all | solution.py:124
  43.8 2.7 %collective-permute-start.5 = (bf16[48,32,128]{2,1,0:T(8,128)(2,1)S(1)}, bf16[48,32,128]{2,1,0:T(8,128)(2,1)}, u32[]{:S(2)}, u32[]{:S(2)}) collective-permute-start(bf16[48,32,128]{2,1,0:T(8,128)(2,1)S(1)} %collective-permute-done.3.rest_8_), channel_id=1, source_target_pairs={{0,32},{1,225},{2,34},{3,227},{4,36},{5,229},{6,38},{7,231},{32,64... | collective-permute-start | bytes 1179656 | tf_op jit(solution)/shard_map/ppermute | solution.py:150
  47.8 8.6 %collective-permute-done.5.rest_7_ = bf16[48,32,128]{2,1,0:T(8,128)(2,1)} collective-permute-done((bf16[48,32,128]{2,1,0:T(8,128)(2,1)S(1)}, bf16[48,32,128]{2,1,0:T(8,128)(2,1)}, u32[]{:S(2)}, u32[]{:S(2)}) %collective-permute-start.5) | collective-permute-done | bytes 393248 | tf_op jit(solution)/shard_map/ppermute | solution.py:150
  56.4 2.4 %collective-permute-done.6.rest_3_ = bf16[48,32,128]{2,1,0:T(8,128)(2,1)} collective-permute-done((bf16[48,32,128]{2,1,0:T(8,128)(2,1)S(1)}, bf16[48,32,128]{2,1,0:T(8,128)(2,1)}, u32[]{:S(2)}, u32[]{:S(2)}) %collective-permute-start.6) | collective-permute-done | bytes 393248 | tf_op jit(solution)/shard_map/ppermute | solution.py:150
  58.7 1.2 collective-permute-start.7
  60.2 16.6 %reverse.1 = (bf16[128,32,128]{2,1,0:T(8,128)(2,1)S(1)}, bf16[128,32,128]{2,1,0:T(8,128)(2,1)S(1)}, bf16[128,32,128]{2,1,0:T(8,128)(2,1)S(1)}, bf16[128,32,128]{...) custom-call(s32[1024]{0:T(1024)S(1)} %copy-done.8, ...), custom_call_target="tpu_custom_call" | custom-call | flops 8589934592 | bytes 42205184 | tf_op jit(solution)/shard_map/reverse/pallas_call | solution.py:105
  81.8 1.0 copy-done.10
  84.4 3.2 %collective-permute-start.12 = (bf16[64,32,128]{2,1,0:T(8,128)(2,1)}, bf16[64,32,128]{2,1,0:T(8,128)(2,1)}, u32[]{:S(2)}, u32[]{:S(2)}) collective-permute-start(bf16[64,32,128]{2,1,0:T(8,128)(2,1)} %get-tuple-element.88), channel_id=1, source_target_pairs={{0,224},{1,33},{2,226},{3,35},{4,228},{5,37},{6,230},{7,39},{32,0}... | collective-permute-start | bytes 1572872 | tf_op jit(solution)/shard_map/ppermute | solution.py:150
  87.6 1.6 tile.4
  89.2 4.6 %all-to-all-start.2 = ((bf16[8,32,4096]{2,1,0:T(8,128)(2,1)}), bf16[8,32,4096]{2,1,0:T(8,128)(2,1)}, u32[]{:S(2)}, u32[]{:S(2)}) async-start(bf16[8,32,4096]{2,1,0:T(8,128)(2,1)} %tile.4), calls=%async_computation.2 | async-start | bytes 4194304 | tf_op jit(solution)/shard_map/all_to_all | solution.py:124
  93.8 4.4 %collective-permute-start.13 = (bf16[48,32,128]{2,1,0:T(8,128)(2,1)}, bf16[48,32,128]{2,1,0:T(8,128)(2,1)}, u32[]{:S(2)}, u32[]{:S(2)}) collective-permute-start(bf16[48,32,128]{2,1,0:T(8,128)(2,1)} %copy-done.20), channel_id=1, source_target_pairs={{0,32},{1,225},{2,34},{3,227},{4,36},{5,229},{6,38},{7,231},{32,64... | collective-permute-start | bytes 1179656 | tf_op jit(solution)/shard_map/ppermute | solution.py:150
  98.3 2.7 %collective-permute-start.9 = (bf16[128,32,128]{2,1,0:T(8,128)(2,1)}, bf16[128,32,128]{2,1,0:T(8,128)(2,1)}, u32[]{:S(2)}, u32[]{:S(2)}) collective-permute-start(bf16[128,32,128]{2,1,0:T(8,128)(2,1)} %copy-done.9), channel_id=1, source_target_pairs={{0,8},{1,25},{2,10},{3,27},{4,12},{5,29},{6,14},{7,31},{8,16},{9,1... | collective-permute-start | bytes 3145736 | tf_op jit(solution)/shard_map/ppermute | solution.py:150
  100.9 5.3 %collective-permute-done.12 = bf16[64,32,128]{2,1,0:T(8,128)(2,1)} collective-permute-done((bf16[64,32,128]{2,1,0:T(8,128)(2,1)}, bf16[64,32,128]{2,1,0:T(8,128)(2,1)}, u32[]{:S(2)}, u32[]{:S(2)}) %collective-permute-start.12) | collective-permute-done | bytes 524320 | tf_op jit(solution)/shard_map/ppermute | solution.py:150
  106.3 2.1 add_convert_fusion.4
  109.2 2.0 add_convert_fusion.5
  111.2 2.2 collective-permute-done.13.rest_5_
  113.4 2.2 collective-permute-start.14
  115.6 21.7 %forward.1 = bf16[32,32,128]{2,1,0:T(8,128)(2,1)} custom-call(s32[1024]{0:T(1024)} %rows_ref.3, s32[1024]{0:T(1024)} %get-tuple-element.127.places_ref, s32[1]{0:T(128)S(6)} %copy.96.count_ref, bf16[640,32,128]{2,1,0:T(8,128)(2,1)} %all-gather.2.cloned.1.call-done.rest_0_, bf16[48,32,128]{2,1,0:T(8,128)(2,1)} %copy-done.14, bf16[48,32,128]{2,1,0:T(8,128)(2,1)} %copy-done.19, ...), custom_call_target="tpu_custom_call" | custom-call | flops 8589934592 | bytes 42205184 | tf_op jit(solution)/shard_map/forward/pallas_call | solution.py:105
  137.3 2.6 %add_convert_fusion = bf16[128,32,128]{2,1,0:T(8,128)(2,1)} fusion(bf16[128,32,128]{2,1,0:T(8,128)(2,1)} %collective-permute-done.9, bf16[128,32,128]{2,1,0:T(8,128)(2,1)S(1)} %get-tuple-element.82), kind=kLoop, calls=%fused_computation | loop fusion | flops 2097152 | bytes 3145728 | tf_op jit(solution)/shard_map/convert_element_type | solution.py:156
  140.0 1.1 collective-permute-start.16
  141.1 2.0 add_convert_fusion.2
  143.1 4.4 %collective-permute-start.18 = (bf16[64,32,128]{2,1,0:T(8,128)(2,1)}, bf16[64,32,128]{2,1,0:T(8,128)(2,1)}, u32[]{:S(2)}, u32[]{:S(2)}) collective-permute-start(bf16[64,32,128]{2,1,0:T(8,128)(2,1)} %add_convert_fusion.2), channel_id=1, source_target_pairs={{0,224},{1,33},{2,226},{3,35},{4,228},{5,37},{6,230},{7,39},{32,0}... | collective-permute-start | bytes 1572872 | tf_op jit(solution)/shard_map/ppermute | solution.py:150
  147.5 2.0 add_convert_fusion.3
  149.5 7.1 %all-to-all-start.3 = ((bf16[32,32,128]{2,1,0:T(8,128)(2,1)}), bf16[32,32,128]{2,1,0:T(8,128)(2,1)S(1)}, u32[]{:S(2)}, u32[]{:S(2)}) async-start(bf16[32,32,128]{2,1,0:T(8,128)(2,1)} %forward.1), calls=%async_computation.3 | async-start | bytes 524288 | tf_op jit(solution)/shard_map/all_to_all | solution.py:124
  156.6 2.4 %convolution_convert_fusion = bf16[32,256]{1,0:T(8,128)(2,1)S(1)} fusion(bf16[256,4096]{1,0:T(8,128)(2,1)} %bitcast.9, bf16[32,32,128]{2,1,0:T(8,128)(2,1)} %forward.1), kind=kOutput, calls=%fused_computation.7 | convolution fusion | flops 67117056 | bytes 2375680 | tf_op jit(solution)/shard_map/dot_general | solution.py:228
  159.0 4.1 %all-to-all-done.3 = bf16[32,32,128]{2,1,0:T(8,128)(2,1)S(1)} async-done(((bf16[32,32,128]{2,1,0:T(8,128)(2,1)}), bf16[32,32,128]{2,1,0:T(8,128)(2,1)S(1)}, u32[]{:S(2)}, u32[]{:S(2)}) %all-to-all-start.3) | async-done | bytes 262176 | tf_op jit(solution)/shard_map/all_to_all | solution.py:124
  163.1 2.4 %add_convert_fusion.1 = bf16[64,32,128]{2,1,0:T(8,128)(2,1)} fusion(bf16[64,32,128]{2,1,0:T(8,128)(2,1)} %collective-permute-done.17, bf16[64,32,128]{2,1,0:T(8,128)(2,1)S(1)} %get-tuple-element.112), kind=kLoop, calls=%fused_computation.9 | loop fusion | flops 1048576 | bytes 1572864 | tf_op jit(solution)/shard_map/convert_element_type | solution.py:156
  167.3 8.3 %all-to-all-start.4 = ((bf16[32,32,256]{2,1,0:T(8,128)(2,1)}), bf16[32,32,256]{2,1,0:T(8,128)(2,1)S(1)}, u32[]{:S(2)}, u32[]{:S(2)}) async-start(bf16[32,32,256]{2,1,0:T(8,128)(2,1)} %tile.5), calls=%async_computation.4 | async-start | bytes 1048576 | tf_op jit(solution)/shard_map/all_to_all | solution.py:124
  175.6 2.3 %fusion.25 = (bf16[64,32,128]{2,1,0:T(8,128)(2,1)S(1)}, f32[64,32,128]{2,1,0:T(8,128)}) fusion(bf16[64,32,128]{2,1,0:T(8,128)(2,1)} %collective-permute-done.18, bf16[64,32,128]{2,1,0:T(8,128)(2,1)S(1)} %collective-permute-done.24, bf16[64,32,128]{2,1,0:T(8,128)(2,1)S(1)} %copy-done.7), kind=kLoop, calls=%fused_computation.75 | loop fusion | flops 1572864 | bytes 3145728 | tf_op jit(solution)/shard_map/convert.4
  178.7 2.4 %collective-permute-start.25 = (bf16[16,32,128]{2,1,0:T(8,128)(2,1)}, bf16[16,32,128]{2,1,0:T(8,128)(2,1)S(1)}, u32[]{:S(2)}, u32[]{:S(2)}) collective-permute-start(bf16[16,32,128]{2,1,0:T(8,128)(2,1)} %get-tuple-element.124), channel_id=1, source_target_pairs={{0,8},{1,25},{2,10},{3,27},{4,12},{5,29},{6,14},{7,31},{8,16},{9,1... | collective-permute-start | bytes 393224 | tf_op jit(solution)/shard_map/ppermute | solution.py:150
  182.3 1.9 add_convert_fusion.6
  184.3 3.4 %collective-permute-start.19 = (bf16[32,32,128]{2,1,0:T(8,128)(2,1)}, bf16[32,32,128]{2,1,0:T(8,128)(2,1)S(1)}, u32[]{:S(2)}, u32[]{:S(2)}) collective-permute-start(bf16[32,32,128]{2,1,0:T(8,128)(2,1)} %get-tuple-element.123), channel_id=1, source_target_pairs={{0,64},{1,193},{2,66},{3,195},{4,68},{5,197},{6,70},{7,199},{32,96... | collective-permute-start | bytes 786440 | tf_op jit(solution)/shard_map/ppermute | solution.py:150
  188.1 2.3 collective-permute-done.25
  190.4 1.4 collective-permute-done.26
  191.8 2.1 collective-permute-done.27
  193.9 1.2 fusion.11
  195.1 5.4 %collective-permute-done.19 = bf16[32,32,128]{2,1,0:T(8,128)(2,1)S(1)} collective-permute-done((bf16[32,32,128]{2,1,0:T(8,128)(2,1)}, bf16[32,32,128]{2,1,0:T(8,128)(2,1)S(1)}, u32[]{:S(2)}, u32[]{:S(2)}) %collective-permute-start.19) | collective-permute-done | bytes 262176 | tf_op jit(solution)/shard_map/ppermute | solution.py:150
  200.5 2.1 add_convert_fusion.11
  202.7 3.0 %collective-permute-start.21 = (bf16[16,32,128]{2,1,0:T(8,128)(2,1)}, bf16[16,32,128]{2,1,0:T(8,128)(2,1)S(1)}, u32[]{:S(2)}, u32[]{:S(2)}) collective-permute-start(bf16[16,32,128]{2,1,0:T(8,128)(2,1)} %get-tuple-element.119), channel_id=1, source_target_pairs={{0,64},{1,193},{2,66},{3,195},{4,68},{5,197},{6,70},{7,199},{32,96... | collective-permute-start | bytes 393224 | tf_op jit(solution)/shard_map/ppermute | solution.py:150
  205.7 2.4 %collective-permute-start.22 = (bf16[16,32,128]{2,1,0:T(8,128)(2,1)}, bf16[16,32,128]{2,1,0:T(8,128)(2,1)S(1)}, u32[]{:S(2)}, u32[]{:S(2)}) collective-permute-start(bf16[16,32,128]{2,1,0:T(8,128)(2,1)} %get-tuple-element.120), channel_id=1, source_target_pairs={{0,32},{1,225},{2,34},{3,227},{4,36},{5,229},{6,38},{7,231},{32,64... | collective-permute-start | bytes 393224 | tf_op jit(solution)/shard_map/ppermute | solution.py:150
  209.5 6.3 %all-to-all-start.5 = ((bf16[8,8,32,128]{3,2,1,0:T(8,128)(2,1)}), bf16[8,8,32,128]{3,2,1,0:T(8,128)(2,1)S(1)}, u32[]{:S(2)}, u32[]{:S(2)}) async-start(bf16[8,8,32,128]{3,2,1,0:T(8,128)(2,1)} %copy.60), calls=%async_computation.5 | async-start | bytes 1048576 | tf_op jit(solution)/shard_map/all_to_all | solution.py:124
  215.9 1.3 add_convert_fusion.8
  217.9 7.5 %all-to-all-done.5 = bf16[8,8,32,128]{3,2,1,0:T(8,128)(2,1)S(1)} async-done(((bf16[8,8,32,128]{3,2,1,0:T(8,128)(2,1)}), bf16[8,8,32,128]{3,2,1,0:T(8,128)(2,1)S(1)}, u32[]{:S(2)}, u32[]{:S(2)}) %all-to-all-start.5) | async-done | bytes 524320 | tf_op jit(solution)/shard_map/all_to_all | solution.py:124
  (119 shorter events, 22.4 us)
Async XLA Ops:
  7.2 13.2 %copy-start.24 = (bf16[256,256]{1,0:T(8,128)(2,1)S(1)}, bf16[256,256]{1,0:T(8,128)(2,1)}, u32[]{:S(2)}) copy-start(bf16[256,256]{1,0:T(8,128)(2,1)} %param.8) | copy-start | bytes 393220
  7.2 108.4 %all-gather.2.cloned.1.call-start = ((), (), s32[]{:S(2)}) async-start(), calls=%async_computation.6 | async-start | bytes 5406720 | tf_op jit(solution)/shard_map/all_gather | solution.py:177
  10.7 15.4 %all-to-all-start = ((bf16[32,32,128]{2,1,0:T(8,128)(2,1)}), bf16[32,32,128]{2,1,0:T(8,128)(2,1)S(1)}, u32[]{:S(2)}, u32[]{:S(2)}) async-start(bf16[32,32,128]{2,1,0:T(8,128)(2,1)} %copy.52), calls=%async_computation | async-start | bytes 524288 | tf_op jit(solution)/shard_map/all_to_all | solution.py:124
  17.2 29.9 %copy-start.26 = (s32[1024]{0:T(1024)S(1)}, s32[1024]{0:T(1024)}, u32[]{:S(2)}) copy-start(s32[1024]{0:T(1024)} %param.11) | copy-start | bytes 12292
  17.3 43.0 %copy-start.8 = (s32[1024]{0:T(1024)S(1)}, s32[1024]{0:T(1024)}, u32[]{:S(2)}) copy-start(s32[1024]{0:T(1024)} %rows_ref.3) | copy-start | bytes 12292
  17.3 3.8 %collective-permute-start = (bf16[12,32,128]{2,1,0:T(8,128)(2,1)S(1)}, bf16[12,32,128]{2,1,0:T(8,128)(2,1)S(1)}, u32[]{:S(2)}, u32[]{:S(2)}) collective-permute-start(bf16[12,32,128]{2,1,0:T(8,128)(2,1)S(1)} %slice.134), channel_id=1, source_target_pairs={{0,8},{1,25},{2,10},{3,27},{4,12},{5,29},{6,14},{7,31},{8,16},{9,1... | collective-permute-start | bytes 294920 | tf_op jit(solution)/shard_map/ppermute | solution.py:150
  19.2 5.9 %collective-permute-start.1 = (bf16[12,32,128]{2,1,0:T(8,128)(2,1)S(1)}, bf16[12,32,128]{2,1,0:T(8,128)(2,1)S(1)}, u32[]{:S(2)}, u32[]{:S(2)}) collective-permute-start(bf16[12,32,128]{2,1,0:T(8,128)(2,1)S(1)} %slice.134), channel_id=1, source_target_pairs={{0,16},{1,17},{2,18},{3,19},{4,20},{5,21},{6,22},{7,23},{8,24},{9,... | collective-permute-start | bytes 294920 | tf_op jit(solution)/shard_map/ppermute | solution.py:150
  19.8 6.3 %collective-permute-start.2 = (bf16[12,32,128]{2,1,0:T(8,128)(2,1)S(1)}, bf16[12,32,128]{2,1,0:T(8,128)(2,1)S(1)}, u32[]{:S(2)}, u32[]{:S(2)}) collective-permute-start(bf16[12,32,128]{2,1,0:T(8,128)(2,1)S(1)} %slice.134), channel_id=1, source_target_pairs={{0,24},{1,9},{2,26},{3,11},{4,28},{5,13},{6,30},{7,15},{8,0},{9,17... | collective-permute-start | bytes 294920 | tf_op jit(solution)/shard_map/ppermute | solution.py:150
  20.6 11.5 %copy-start.12 = (bf16[8,32,8,32]{3,2,1,0:T(8,128)(2,1)}, bf16[8,32,8,32]{3,2,1,0:T(8,128)(2,1)S(1)}, u32[]{:S(2)}) copy-start(bf16[8,32,8,32]{3,2,1,0:T(8,128)(2,1)S(1)} %reshape.64) | copy-start | bytes 393220
  26.1 34.1 %copy-start.14 = (bf16[48,32,128]{2,1,0:T(8,128)(2,1)}, bf16[48,32,128]{2,1,0:T(8,128)(2,1)S(1)}, u32[]{:S(2)}) copy-start(bf16[48,32,128]{2,1,0:T(8,128)(2,1)S(1)} %pad_maximum_fusion.1.rest_1_) | copy-start | bytes 1179652
  26.1 17.3 %collective-permute-start.3 = (bf16[48,32,128]{2,1,0:T(8,128)(2,1)S(1)}, bf16[48,32,128]{2,1,0:T(8,128)(2,1)S(1)}, u32[]{:S(2)}, u32[]{:S(2)}) collective-permute-start(bf16[48,32,128]{2,1,0:T(8,128)(2,1)S(1)} %pad_maximum_fusion.1.rest_1_), channel_id=1, source_target_pairs={{0,32},{1,225},{2,34},{3,227},{4,36},{5,229},{6,38},{7,231},{32,64... | collective-permute-start | bytes 1179656 | tf_op jit(solution)/shard_map/ppermute | solution.py:150
  31.8 12.0 %collective-permute-start.4 = (bf16[48,32,128]{2,1,0:T(8,128)(2,1)S(1)}, bf16[48,32,128]{2,1,0:T(8,128)(2,1)S(1)}, u32[]{:S(2)}, u32[]{:S(2)}) collective-permute-start(bf16[48,32,128]{2,1,0:T(8,128)(2,1)S(1)} %pad_maximum_fusion.1.rest_1_), channel_id=1, source_target_pairs={{0,224},{1,33},{2,226},{3,35},{4,228},{5,37},{6,230},{7,39},{32,0}... | collective-permute-start | bytes 1179656 | tf_op jit(solution)/shard_map/ppermute | solution.py:150
  43.4 16.8 %copy-start.18 = (bf16[48,32,128]{2,1,0:T(8,128)(2,1)}, bf16[48,32,128]{2,1,0:T(8,128)(2,1)S(1)}, u32[]{:S(2)}) copy-start(bf16[48,32,128]{2,1,0:T(8,128)(2,1)S(1)} %collective-permute-done.3.rest_8_) | copy-start | bytes 1179652
  43.8 16.5 %copy-start.19 = (bf16[48,32,128]{2,1,0:T(8,128)(2,1)}, bf16[48,32,128]{2,1,0:T(8,128)(2,1)S(1)}, u32[]{:S(2)}) copy-start(bf16[48,32,128]{2,1,0:T(8,128)(2,1)S(1)} %collective-permute-done.4.rest_2_) | copy-start | bytes 1179652
  43.8 12.6 %collective-permute-start.5 = (bf16[48,32,128]{2,1,0:T(8,128)(2,1)S(1)}, bf16[48,32,128]{2,1,0:T(8,128)(2,1)}, u32[]{:S(2)}, u32[]{:S(2)}) collective-permute-start(bf16[48,32,128]{2,1,0:T(8,128)(2,1)S(1)} %collective-permute-done.3.rest_8_), channel_id=1, source_target_pairs={{0,32},{1,225},{2,34},{3,227},{4,36},{5,229},{6,38},{7,231},{32,64... | collective-permute-start | bytes 1179656 | tf_op jit(solution)/shard_map/ppermute | solution.py:150
  46.5 12.3 %collective-permute-start.6 = (bf16[48,32,128]{2,1,0:T(8,128)(2,1)S(1)}, bf16[48,32,128]{2,1,0:T(8,128)(2,1)}, u32[]{:S(2)}, u32[]{:S(2)}) collective-permute-start(bf16[48,32,128]{2,1,0:T(8,128)(2,1)S(1)} %collective-permute-done.4.rest_2_), channel_id=1, source_target_pairs={{0,224},{1,33},{2,226},{3,35},{4,228},{5,37},{6,230},{7,39},{32,0}... | collective-permute-start | bytes 1179656 | tf_op jit(solution)/shard_map/ppermute | solution.py:150
  58.7 23.1 %collective-permute-start.7 = (bf16[48,32,128]{2,1,0:T(8,128)(2,1)}, bf16[48,32,128]{2,1,0:T(8,128)(2,1)S(1)}, u32[]{:S(2)}, u32[]{:S(2)}) collective-permute-start(bf16[48,32,128]{2,1,0:T(8,128)(2,1)} %collective-permute-done.5.rest_7_), channel_id=1, source_target_pairs={{0,32},{1,225},{2,34},{3,227},{4,36},{5,229},{6,38},{7,231},{32,64... | collective-permute-start | bytes 1179656 | tf_op jit(solution)/shard_map/ppermute | solution.py:150
  59.9 23.0 %collective-permute-start.8 = (bf16[48,32,128]{2,1,0:T(8,128)(2,1)}, bf16[48,32,128]{2,1,0:T(8,128)(2,1)S(1)}, u32[]{:S(2)}, u32[]{:S(2)}) collective-permute-start(bf16[48,32,128]{2,1,0:T(8,128)(2,1)} %collective-permute-done.6.rest_3_), channel_id=1, source_target_pairs={{0,224},{1,33},{2,226},{3,35},{4,228},{5,37},{6,230},{7,39},{32,0}... | collective-permute-start | bytes 1179656 | tf_op jit(solution)/shard_map/ppermute | solution.py:150
  60.2 27.4 %copy-start.15 = (bf16[32,4096]{1,0:T(8,128)(2,1)S(1)}, bf16[32,4096]{1,0:T(8,128)(2,1)}, u32[]{:S(2)}) copy-start(bf16[32,4096]{1,0:T(8,128)(2,1)} %param.13) | copy-start | bytes 786436
  84.4 21.9 %collective-permute-start.12 = (bf16[64,32,128]{2,1,0:T(8,128)(2,1)}, bf16[64,32,128]{2,1,0:T(8,128)(2,1)}, u32[]{:S(2)}, u32[]{:S(2)}) collective-permute-start(bf16[64,32,128]{2,1,0:T(8,128)(2,1)} %get-tuple-element.88), channel_id=1, source_target_pairs={{0,224},{1,33},{2,226},{3,35},{4,228},{5,37},{6,230},{7,39},{32,0}... | collective-permute-start | bytes 1572872 | tf_op jit(solution)/shard_map/ppermute | solution.py:150
  89.2 48.1 %all-to-all-start.2 = ((bf16[8,32,4096]{2,1,0:T(8,128)(2,1)}), bf16[8,32,4096]{2,1,0:T(8,128)(2,1)}, u32[]{:S(2)}, u32[]{:S(2)}) async-start(bf16[8,32,4096]{2,1,0:T(8,128)(2,1)} %tile.4), calls=%async_computation.2 | async-start | bytes 4194304 | tf_op jit(solution)/shard_map/all_to_all | solution.py:124
  93.8 15.3 %collective-permute-start.11 = (bf16[64,32,128]{2,1,0:T(8,128)(2,1)}, bf16[64,32,128]{2,1,0:T(8,128)(2,1)S(1)}, u32[]{:S(2)}, u32[]{:S(2)}) collective-permute-start(bf16[64,32,128]{2,1,0:T(8,128)(2,1)} %copy-done.11), channel_id=1, source_target_pairs={{0,32},{1,225},{2,34},{3,227},{4,36},{5,229},{6,38},{7,231},{32,64... | collective-permute-start | bytes 1572872 | tf_op jit(solution)/shard_map/ppermute | solution.py:150
  93.8 19.6 %collective-permute-start.13 = (bf16[48,32,128]{2,1,0:T(8,128)(2,1)}, bf16[48,32,128]{2,1,0:T(8,128)(2,1)}, u32[]{:S(2)}, u32[]{:S(2)}) collective-permute-start(bf16[48,32,128]{2,1,0:T(8,128)(2,1)} %copy-done.20), channel_id=1, source_target_pairs={{0,32},{1,225},{2,34},{3,227},{4,36},{5,229},{6,38},{7,231},{32,64... | collective-permute-start | bytes 1179656 | tf_op jit(solution)/shard_map/ppermute | solution.py:150
  98.2 39.1 %collective-permute-start.10 = (bf16[128,32,128]{2,1,0:T(8,128)(2,1)}, bf16[128,32,128]{2,1,0:T(8,128)(2,1)}, u32[]{:S(2)}, u32[]{:S(2)}) collective-permute-start(bf16[128,32,128]{2,1,0:T(8,128)(2,1)} %copy-done.10), channel_id=1, source_target_pairs={{0,24},{1,9},{2,26},{3,11},{4,28},{5,13},{6,30},{7,15},{8,0},{9,17... | collective-permute-start | bytes 3145736 | tf_op jit(solution)/shard_map/ppermute | solution.py:150
  98.3 39.1 %collective-permute-start.9 = (bf16[128,32,128]{2,1,0:T(8,128)(2,1)}, bf16[128,32,128]{2,1,0:T(8,128)(2,1)}, u32[]{:S(2)}, u32[]{:S(2)}) collective-permute-start(bf16[128,32,128]{2,1,0:T(8,128)(2,1)} %copy-done.9), channel_id=1, source_target_pairs={{0,8},{1,25},{2,10},{3,27},{4,12},{5,29},{6,14},{7,31},{8,16},{9,1... | collective-permute-start | bytes 3145736 | tf_op jit(solution)/shard_map/ppermute | solution.py:150
  113.4 23.9 %collective-permute-start.14 = (bf16[64,32,128]{2,1,0:T(8,128)(2,1)}, bf16[64,32,128]{2,1,0:T(8,128)(2,1)}, u32[]{:S(2)}, u32[]{:S(2)}) collective-permute-start(bf16[64,32,128]{2,1,0:T(8,128)(2,1)} %add_convert_fusion.5), channel_id=1, source_target_pairs={{0,32},{1,225},{2,34},{3,227},{4,36},{5,229},{6,38},{7,231},{32,64... | collective-permute-start | bytes 1572872 | tf_op jit(solution)/shard_map/ppermute | solution.py:150
  115.6 21.7 %collective-permute-start.15 = (bf16[64,32,128]{2,1,0:T(8,128)(2,1)}, bf16[64,32,128]{2,1,0:T(8,128)(2,1)}, u32[]{:S(2)}, u32[]{:S(2)}) collective-permute-start(bf16[64,32,128]{2,1,0:T(8,128)(2,1)} %add_convert_fusion.4), channel_id=1, source_target_pairs={{0,224},{1,33},{2,226},{3,35},{4,228},{5,37},{6,230},{7,39},{32,0}... | collective-permute-start | bytes 1572872 | tf_op jit(solution)/shard_map/ppermute | solution.py:150
  140.0 23.1 %collective-permute-start.16 = (bf16[128,32,128]{2,1,0:T(8,128)(2,1)}, bf16[128,32,128]{2,1,0:T(8,128)(2,1)S(1)}, u32[]{:S(2)}, u32[]{:S(2)}) collective-permute-start(bf16[128,32,128]{2,1,0:T(8,128)(2,1)} %add_convert_fusion), channel_id=1, source_target_pairs={{0,8},{1,25},{2,10},{3,27},{4,12},{5,29},{6,14},{7,31},{8,16},{9,1... | collective-permute-start | bytes 3145736 | tf_op jit(solution)/shard_map/ppermute | solution.py:150
  143.1 20.0 %collective-permute-start.18 = (bf16[64,32,128]{2,1,0:T(8,128)(2,1)}, bf16[64,32,128]{2,1,0:T(8,128)(2,1)}, u32[]{:S(2)}, u32[]{:S(2)}) collective-permute-start(bf16[64,32,128]{2,1,0:T(8,128)(2,1)} %add_convert_fusion.2), channel_id=1, source_target_pairs={{0,224},{1,33},{2,226},{3,35},{4,228},{5,37},{6,230},{7,39},{32,0}... | collective-permute-start | bytes 1572872 | tf_op jit(solution)/shard_map/ppermute | solution.py:150
  149.5 13.6 %collective-permute-start.17 = (bf16[64,32,128]{2,1,0:T(8,128)(2,1)}, bf16[64,32,128]{2,1,0:T(8,128)(2,1)}, u32[]{:S(2)}, u32[]{:S(2)}) collective-permute-start(bf16[64,32,128]{2,1,0:T(8,128)(2,1)} %add_convert_fusion.3), channel_id=1, source_target_pairs={{0,32},{1,225},{2,34},{3,227},{4,36},{5,229},{6,38},{7,231},{32,64... | collective-permute-start | bytes 1572872 | tf_op jit(solution)/shard_map/ppermute | solution.py:150
  149.5 13.6 %all-to-all-start.3 = ((bf16[32,32,128]{2,1,0:T(8,128)(2,1)}), bf16[32,32,128]{2,1,0:T(8,128)(2,1)S(1)}, u32[]{:S(2)}, u32[]{:S(2)}) async-start(bf16[32,32,128]{2,1,0:T(8,128)(2,1)} %forward.1), calls=%async_computation.3 | async-start | bytes 524288 | tf_op jit(solution)/shard_map/all_to_all | solution.py:124
  159.0 16.7 %copy-start.7 = (bf16[64,32,128]{2,1,0:T(8,128)(2,1)S(1)}, bf16[64,32,128]{2,1,0:T(8,128)(2,1)}, u32[]{:S(2)}) copy-start(bf16[64,32,128]{2,1,0:T(8,128)(2,1)} %copy-done.6) | copy-start | bytes 1572868
  163.1 14.9 %copy-start.22 = (bf16[32,32,128]{2,1,0:T(8,128)(2,1)}, bf16[32,32,128]{2,1,0:T(8,128)(2,1)S(1)}, u32[]{:S(2)}) copy-start(bf16[32,32,128]{2,1,0:T(8,128)(2,1)S(1)} %all-to-all-done.3) | copy-start | bytes 786436
  165.5 10.2 %collective-permute-start.24 = (bf16[64,32,128]{2,1,0:T(8,128)(2,1)}, bf16[64,32,128]{2,1,0:T(8,128)(2,1)S(1)}, u32[]{:S(2)}, u32[]{:S(2)}) collective-permute-start(bf16[64,32,128]{2,1,0:T(8,128)(2,1)} %add_convert_fusion.1), channel_id=1, source_target_pairs={{0,32},{1,225},{2,34},{3,227},{4,36},{5,229},{6,38},{7,231},{32,64... | collective-permute-start | bytes 1572872 | tf_op jit(solution)/shard_map/ppermute | solution.py:150
  167.3 33.2 %all-to-all-start.4 = ((bf16[32,32,256]{2,1,0:T(8,128)(2,1)}), bf16[32,32,256]{2,1,0:T(8,128)(2,1)S(1)}, u32[]{:S(2)}, u32[]{:S(2)}) async-start(bf16[32,32,256]{2,1,0:T(8,128)(2,1)} %tile.5), calls=%async_computation.4 | async-start | bytes 1048576 | tf_op jit(solution)/shard_map/all_to_all | solution.py:124
  175.6 6.7 %copy-start.17 = (bf16[128,32,128]{2,1,0:T(8,128)(2,1)S(1)}, bf16[128,32,128]{2,1,0:T(8,128)(2,1)}, u32[]{:S(2)}) copy-start(bf16[128,32,128]{2,1,0:T(8,128)(2,1)} %copy-done.16) | copy-start | bytes 3145732
  178.0 9.6 %copy-start.13 = (bf16[8,32,8,32]{3,2,1,0:T(8,128)(2,1)S(1)}, bf16[8,32,8,32]{3,2,1,0:T(8,128)(2,1)}, u32[]{:S(2)}) copy-start(bf16[8,32,8,32]{3,2,1,0:T(8,128)(2,1)} %copy-done.12) | copy-start | bytes 393220
  178.7 11.7 %collective-permute-start.25 = (bf16[16,32,128]{2,1,0:T(8,128)(2,1)}, bf16[16,32,128]{2,1,0:T(8,128)(2,1)S(1)}, u32[]{:S(2)}, u32[]{:S(2)}) collective-permute-start(bf16[16,32,128]{2,1,0:T(8,128)(2,1)} %get-tuple-element.124), channel_id=1, source_target_pairs={{0,8},{1,25},{2,10},{3,27},{4,12},{5,29},{6,14},{7,31},{8,16},{9,1... | collective-permute-start | bytes 393224 | tf_op jit(solution)/shard_map/ppermute | solution.py:150
  181.2 10.6 %collective-permute-start.26 = (bf16[16,32,128]{2,1,0:T(8,128)(2,1)}, bf16[16,32,128]{2,1,0:T(8,128)(2,1)}, u32[]{:S(2)}, u32[]{:S(2)}) collective-permute-start(bf16[16,32,128]{2,1,0:T(8,128)(2,1)} %get-tuple-element.126), channel_id=1, source_target_pairs={{0,16},{1,17},{2,18},{3,19},{4,20},{5,21},{6,22},{7,23},{8,24},{9,... | collective-permute-start | bytes 393224 | tf_op jit(solution)/shard_map/ppermute | solution.py:150
  181.8 12.2 %collective-permute-start.27 = (bf16[16,32,128]{2,1,0:T(8,128)(2,1)}, bf16[16,32,128]{2,1,0:T(8,128)(2,1)}, u32[]{:S(2)}, u32[]{:S(2)}) collective-permute-start(bf16[16,32,128]{2,1,0:T(8,128)(2,1)} %get-tuple-element.125), channel_id=1, source_target_pairs={{0,24},{1,9},{2,26},{3,11},{4,28},{5,13},{6,30},{7,15},{8,0},{9,17... | collective-permute-start | bytes 393224 | tf_op jit(solution)/shard_map/ppermute | solution.py:150
  184.3 16.2 %collective-permute-start.19 = (bf16[32,32,128]{2,1,0:T(8,128)(2,1)}, bf16[32,32,128]{2,1,0:T(8,128)(2,1)S(1)}, u32[]{:S(2)}, u32[]{:S(2)}) collective-permute-start(bf16[32,32,128]{2,1,0:T(8,128)(2,1)} %get-tuple-element.123), channel_id=1, source_target_pairs={{0,64},{1,193},{2,66},{3,195},{4,68},{5,197},{6,70},{7,199},{32,96... | collective-permute-start | bytes 786440 | tf_op jit(solution)/shard_map/ppermute | solution.py:150
  187.6 20.5 %copy-start.23 = (bf16[32,32,128]{2,1,0:T(8,128)(2,1)S(1)}, bf16[32,32,128]{2,1,0:T(8,128)(2,1)}, u32[]{:S(2)}) copy-start(bf16[32,32,128]{2,1,0:T(8,128)(2,1)} %copy-done.22) | copy-start | bytes 786436
  187.6 12.9 %collective-permute-start.20 = (bf16[32,32,128]{2,1,0:T(8,128)(2,1)S(1)}, bf16[32,32,128]{2,1,0:T(8,128)(2,1)}, u32[]{:S(2)}, u32[]{:S(2)}) collective-permute-start(bf16[32,32,128]{2,1,0:T(8,128)(2,1)S(1)} %get-tuple-element.122), channel_id=1, source_target_pairs={{0,192},{1,65},{2,194},{3,67},{4,196},{5,69},{6,198},{7,71},{32,22... | collective-permute-start | bytes 786440 | tf_op jit(solution)/shard_map/ppermute | solution.py:150
  202.7 13.2 %collective-permute-start.21 = (bf16[16,32,128]{2,1,0:T(8,128)(2,1)}, bf16[16,32,128]{2,1,0:T(8,128)(2,1)S(1)}, u32[]{:S(2)}, u32[]{:S(2)}) collective-permute-start(bf16[16,32,128]{2,1,0:T(8,128)(2,1)} %get-tuple-element.119), channel_id=1, source_target_pairs={{0,64},{1,193},{2,66},{3,195},{4,68},{5,197},{6,70},{7,199},{32,96... | collective-permute-start | bytes 393224 | tf_op jit(solution)/shard_map/ppermute | solution.py:150
  205.7 10.2 %collective-permute-start.22 = (bf16[16,32,128]{2,1,0:T(8,128)(2,1)}, bf16[16,32,128]{2,1,0:T(8,128)(2,1)S(1)}, u32[]{:S(2)}, u32[]{:S(2)}) collective-permute-start(bf16[16,32,128]{2,1,0:T(8,128)(2,1)} %get-tuple-element.120), channel_id=1, source_target_pairs={{0,32},{1,225},{2,34},{3,227},{4,36},{5,229},{6,38},{7,231},{32,64... | collective-permute-start | bytes 393224 | tf_op jit(solution)/shard_map/ppermute | solution.py:150
  208.0 7.8 %collective-permute-start.23 = (bf16[16,32,128]{2,1,0:T(8,128)(2,1)}, bf16[16,32,128]{2,1,0:T(8,128)(2,1)}, u32[]{:S(2)}, u32[]{:S(2)}) collective-permute-start(bf16[16,32,128]{2,1,0:T(8,128)(2,1)} %get-tuple-element.121), channel_id=1, source_target_pairs={{0,224},{1,33},{2,226},{3,35},{4,228},{5,37},{6,230},{7,39},{32,0}... | collective-permute-start | bytes 393224 | tf_op jit(solution)/shard_map/ppermute | solution.py:150
  209.5 15.8 %all-to-all-start.5 = ((bf16[8,8,32,128]{3,2,1,0:T(8,128)(2,1)}), bf16[8,8,32,128]{3,2,1,0:T(8,128)(2,1)S(1)}, u32[]{:S(2)}, u32[]{:S(2)}) async-start(bf16[8,8,32,128]{3,2,1,0:T(8,128)(2,1)} %copy.60), calls=%async_computation.5 | async-start | bytes 1048576 | tf_op jit(solution)/shard_map/all_to_all | solution.py:124
  215.8 11.2 %copy-start.1 = (bf16[32,4096]{1,0:T(8,128)(2,1)S(1)}, bf16[32,4096]{1,0:T(8,128)(2,1)}, u32[]{:S(2)}) copy-start(bf16[32,4096]{1,0:T(8,128)(2,1)} %param.7) | copy-start | bytes 786436
  (13 other events, 20.0 us)
Sparse Core Ops, SparseCore 0:
  11.2 93.8 all-gather.1

commit v6 on v5

--- a/solution.py
+++ b/solution.py
@@ -160,7 +160,7 @@
     far_x = (turn * (owner % nx - x)) % nx
     far_z = (turn * (owner // nx - z)) % nz
     inner = tile_cols % blocks
-    most = blocks * 5 // 8
+    most = blocks * 3 // 4
     few = blocks - most
     source = jnp.where(
         inner < most, owner * most + inner, nz * nx * most + (far_z * nx + far_x) * few + inner - most

time: 234 us -> 236 us (level)
  starting transfers between devices: 77.2 us -> 70.3 us
  Pallas kernels: 38.3 us -> 42.8 us
  waiting for transfers between devices: 48 us -> 50.7 us
    ppermute x28, starting transfers between devices: 44.2 us -> 39.6 us  [ring(): return lax.ppermute(a, (axis, 'cols'), moves)]
    pallas_call x2, Pallas kernels: 38.3 us -> 42.8 us  [tile_pass(): pl.pallas_call(body, out_shape=[jax.ShapeDtypeStruct((n, narrow, side), j...]
    ppermute x28, waiting for transfers between devices: 36.4 us -> 39.1 us  [ring(): return lax.ppermute(a, (axis, 'cols'), moves)]
    unnamed x56 -> x60, local copies, waits for them, and re-layouts: 10.2 us -> 10.8 us
  transfers between devices with their start and end apart: 34 -> 34, of which waited for: 15 -> 14; matrix products, arithmetic and copies ran while one was open for 11% -> 11% of each run, Pallas kernels for 16% -> 18%
where the time goes in v6:
time: 236 us; the launch traced here: 235 us
  starting transfers between devices  70.3 us (30%)
  waiting for transfers between devices  50.7 us (21%)
  Pallas kernels  42.8 us (18%)
  other arithmetic  23.5 us (10%)
  local copies, waits for them, and re-layouts  18 us (8%)
  between operations  15.1 us (6%)
  blocking collectives  12 us (5%)
  matrix products  3 us (1%)
    pallas_call x2, Pallas kernels, tile_pass(): pl.pallas_call(body, out_shape=[jax.ShapeDtypeStruct((n, narrow, side), j...  42.8 us
    ppermute x28, starting transfers between devices, ring(): return lax.ppermute(a, (axis, 'cols'), moves)  39.6 us
    ppermute x28, waiting for transfers between devices, ring(): return lax.ppermute(a, (axis, 'cols'), moves)  39.1 us
    all_to_all x5, starting transfers between devices, exchange(): return lax.all_to_all(parts, axis, split_axis=0, concat_axis=0, tiled=True)  30.6 us
    convert_element_type x8, other arithmetic, narrowed(): return add(*terms).astype(jnp.bfloat16)  17.2 us
    all_to_all x1, blocking collectives, exchange(): return lax.all_to_all(parts, axis, split_axis=0, concat_axis=0, tiled=True)  12 us
    all_to_all x5, waiting for transfers between devices, exchange(): return lax.all_to_all(parts, axis, split_axis=0, concat_axis=0, tiled=True)  11.6 us
    unnamed x60, local copies, waits for them, and re-layouts  10.8 us
  transfers between devices with their start and end apart: 34, of which 14 were waited for; matrix products, arithmetic and copies ran while one was open for 11% of the time, Pallas kernels for 18%

profile of v6, /device:TPU:1, one launch (start us, length us, event | category | flops | bytes accessed | tf_op | source)
XLA Modules:
  0.0 235.4 jit_solution(11204627971771305341)
XLA Ops:
  8.9 1.0 copy.76
  10.7 6.6 %all-to-all-start = ((bf16[32,32,128]{2,1,0:T(8,128)(2,1)}), bf16[32,32,128]{2,1,0:T(8,128)(2,1)S(1)}, u32[]{:S(2)}, u32[]{:S(2)}) async-start(bf16[32,32,128]{2,1,0:T(8,128)(2,1)} %copy.52), calls=%async_computation | async-start | bytes 524288 | tf_op jit(solution)/shard_map/all_to_all | solution.py:124
  17.3 2.0 collective-permute-start
  20.6 3.7 %collective-permute-done.1 = bf16[8,32,128]{2,1,0:T(8,128)(2,1)S(1)} collective-permute-done((bf16[8,32,128]{2,1,0:T(8,128)(2,1)S(1)}, bf16[8,32,128]{2,1,0:T(8,128)(2,1)S(1)}, u32[]{:S(2)}, u32[]{:S(2)}) %collective-permute-start.1) | collective-permute-done | bytes 65568 | tf_op jit(solution)/shard_map/ppermute | solution.py:150
  24.8 5.7 %collective-permute-start.3 = (bf16[32,32,128]{2,1,0:T(8,128)(2,1)S(1)}, bf16[32,32,128]{2,1,0:T(8,128)(2,1)S(1)}, u32[]{:S(2)}, u32[]{:S(2)}) collective-permute-start(bf16[32,32,128]{2,1,0:T(8,128)(2,1)S(1)} %pad_maximum_fusion.1.rest_1_), channel_id=1, source_target_pairs={{0,32},{1,225},{2,34},{3,227},{4,36},{5,229},{6,38},{7,231},{32,64... | collective-permute-start | bytes 786440 | tf_op jit(solution)/shard_map/ppermute | solution.py:150
  30.8 12.0 %all_to_all.34.grads_ref = bf16[32,32,128]{2,1,0:T(8,128)(2,1)S(1)} all-to-all(bf16[32,32,128]{2,1,0:T(8,128)(2,1)S(1)} %bitcast.83), channel_id=1, replica_groups=mesh['z'=8,'x'=4,'cols'=8] {'cols'}, dimensions={0} | all-to-all | bytes 524288 | tf_op jit(solution)/shard_map/all_to_all | solution.py:124
  42.8 2.0 collective-permute-start.5
  46.1 6.3 %collective-permute-done.5.rest_7_ = bf16[32,32,128]{2,1,0:T(8,128)(2,1)} collective-permute-done((bf16[32,32,128]{2,1,0:T(8,128)(2,1)S(1)}, bf16[32,32,128]{2,1,0:T(8,128)(2,1)}, u32[]{:S(2)}, u32[]{:S(2)}) %collective-permute-start.5) | collective-permute-done | bytes 262176 | tf_op jit(solution)/shard_map/ppermute | solution.py:150
  52.4 3.3 %collective-permute-done.6.rest_3_ = bf16[32,32,128]{2,1,0:T(8,128)(2,1)} collective-permute-done((bf16[32,32,128]{2,1,0:T(8,128)(2,1)S(1)}, bf16[32,32,128]{2,1,0:T(8,128)(2,1)}, u32[]{:S(2)}, u32[]{:S(2)}) %collective-permute-start.6) | collective-permute-done | bytes 262176 | tf_op jit(solution)/shard_map/ppermute | solution.py:150
  55.7 1.5 collective-permute-start.8
  57.2 18.5 %reverse.1 = (bf16[128,32,128]{2,1,0:T(8,128)(2,1)S(1)}, bf16[128,32,128]{2,1,0:T(8,128)(2,1)S(1)}, bf16[128,32,128]{2,1,0:T(8,128)(2,1)S(1)}, bf16[128,32,128]{...) custom-call(s32[1024]{0:T(1024)S(1)} %copy-done.8, ...), custom_call_target="tpu_custom_call" | custom-call | flops 8589934592 | bytes 42205184 | tf_op jit(solution)/shard_map/reverse/pallas_call | solution.py:105
  78.9 1.0 copy-done.9
  80.7 1.0 copy-done.10
  83.1 1.5 tile.4
  84.6 6.8 %all-to-all-start.2 = ((bf16[8,32,4096]{2,1,0:T(8,128)(2,1)}), bf16[8,32,4096]{2,1,0:T(8,128)(2,1)}, u32[]{:S(2)}, u32[]{:S(2)}) async-start(bf16[8,32,4096]{2,1,0:T(8,128)(2,1)} %tile.4), calls=%async_computation.2 | async-start | bytes 4194304 | tf_op jit(solution)/shard_map/all_to_all | solution.py:124
  91.5 1.6 collective-permute-start.13
  93.6 2.2 collective-permute-start.9
  95.8 8.2 %collective-permute-done.12 = bf16[64,32,128]{2,1,0:T(8,128)(2,1)} collective-permute-done((bf16[64,32,128]{2,1,0:T(8,128)(2,1)}, bf16[64,32,128]{2,1,0:T(8,128)(2,1)}, u32[]{:S(2)}, u32[]{:S(2)}) %collective-permute-start.12) | collective-permute-done | bytes 524320 | tf_op jit(solution)/shard_map/ppermute | solution.py:150
  104.0 2.2 add_convert_fusion.4
  106.2 6.8 %collective-permute-done.11 = bf16[64,32,128]{2,1,0:T(8,128)(2,1)S(1)} collective-permute-done((bf16[64,32,128]{2,1,0:T(8,128)(2,1)}, bf16[64,32,128]{2,1,0:T(8,128)(2,1)S(1)}, u32[]{:S(2)}, u32[]{:S(2)}) %collective-permute-start.11) | collective-permute-done | bytes 524320 | tf_op jit(solution)/shard_map/ppermute | solution.py:150
  113.0 2.0 add_convert_fusion.5
  116.5 2.5 %collective-permute-start.14 = (bf16[64,32,128]{2,1,0:T(8,128)(2,1)}, bf16[64,32,128]{2,1,0:T(8,128)(2,1)}, u32[]{:S(2)}, u32[]{:S(2)}) collective-permute-start(bf16[64,32,128]{2,1,0:T(8,128)(2,1)} %add_convert_fusion.5), channel_id=1, source_target_pairs={{0,32},{1,225},{2,34},{3,227},{4,36},{5,229},{6,38},{7,231},{32,64... | collective-permute-start | bytes 1572872 | tf_op jit(solution)/shard_map/ppermute | solution.py:150
  119.0 24.4 %forward.1 = bf16[32,32,128]{2,1,0:T(8,128)(2,1)} custom-call(s32[1024]{0:T(1024)} %rows_ref.3, s32[1024]{0:T(1024)} %get-tuple-element.127.places_ref, s32[1]{0:T(128)S(6)} %copy.96.count_ref, bf16[768,32,128]{2,1,0:T(8,128)(2,1)} %all-gather.2.cloned.1.call-done.rest_0_, bf16[32,32,128]{2,1,0:T(8,128)(2,1)} %copy-done.14, bf16[32,32,128]{2,1,0:T(8,128)(2,1)} %copy-done.19, ...), custom_call_target="tpu_custom_call" | custom-call | flops 8589934592 | bytes 42205184 | tf_op jit(solution)/shard_map/forward/pallas_call | solution.py:105
  143.4 2.5 %add_convert_fusion = bf16[128,32,128]{2,1,0:T(8,128)(2,1)} fusion(bf16[128,32,128]{2,1,0:T(8,128)(2,1)} %collective-permute-done.9, bf16[128,32,128]{2,1,0:T(8,128)(2,1)S(1)} %get-tuple-element.82), kind=kLoop, calls=%fused_computation | loop fusion | flops 2097152 | bytes 3145728 | tf_op jit(solution)/shard_map/convert_element_type | solution.py:156
  145.9 2.0 add_convert_fusion.2
  147.9 2.0 add_convert_fusion.3
  149.9 5.9 %collective-permute-start.17 = (bf16[64,32,128]{2,1,0:T(8,128)(2,1)}, bf16[64,32,128]{2,1,0:T(8,128)(2,1)}, u32[]{:S(2)}, u32[]{:S(2)}) collective-permute-start(bf16[64,32,128]{2,1,0:T(8,128)(2,1)} %add_convert_fusion.3), channel_id=1, source_target_pairs={{0,32},{1,225},{2,34},{3,227},{4,36},{5,229},{6,38},{7,231},{32,64... | collective-permute-start | bytes 1572872 | tf_op jit(solution)/shard_map/ppermute | solution.py:150
  155.8 4.4 %all-to-all-start.3 = ((bf16[32,32,128]{2,1,0:T(8,128)(2,1)}), bf16[32,32,128]{2,1,0:T(8,128)(2,1)S(1)}, u32[]{:S(2)}, u32[]{:S(2)}) async-start(bf16[32,32,128]{2,1,0:T(8,128)(2,1)} %forward.1), calls=%async_computation.3 | async-start | bytes 524288 | tf_op jit(solution)/shard_map/all_to_all | solution.py:124
  160.2 2.4 %convolution_convert_fusion = bf16[32,256]{1,0:T(8,128)(2,1)S(1)} fusion(bf16[256,4096]{1,0:T(8,128)(2,1)} %bitcast.9, bf16[32,32,128]{2,1,0:T(8,128)(2,1)} %forward.1), kind=kOutput, calls=%fused_computation.7 | convolution fusion | flops 67117056 | bytes 2375680 | tf_op jit(solution)/shard_map/dot_general | solution.py:228
  162.7 4.1 %all-to-all-done.3 = bf16[32,32,128]{2,1,0:T(8,128)(2,1)S(1)} async-done(((bf16[32,32,128]{2,1,0:T(8,128)(2,1)}), bf16[32,32,128]{2,1,0:T(8,128)(2,1)S(1)}, u32[]{:S(2)}, u32[]{:S(2)}) %all-to-all-start.3) | async-done | bytes 262176 | tf_op jit(solution)/shard_map/all_to_all | solution.py:124
  166.8 2.4 %add_convert_fusion.1 = bf16[64,32,128]{2,1,0:T(8,128)(2,1)} fusion(bf16[64,32,128]{2,1,0:T(8,128)(2,1)} %collective-permute-done.17, bf16[64,32,128]{2,1,0:T(8,128)(2,1)S(1)} %get-tuple-element.112), kind=kLoop, calls=%fused_computation.9 | loop fusion | flops 1048576 | bytes 1572864 | tf_op jit(solution)/shard_map/convert_element_type | solution.py:156
  169.2 1.5 collective-permute-start.24
  171.5 4.7 %all-to-all-start.4 = ((bf16[32,32,256]{2,1,0:T(8,128)(2,1)}), bf16[32,32,256]{2,1,0:T(8,128)(2,1)S(1)}, u32[]{:S(2)}, u32[]{:S(2)}) async-start(bf16[32,32,256]{2,1,0:T(8,128)(2,1)} %tile.5), calls=%async_computation.4 | async-start | bytes 1048576 | tf_op jit(solution)/shard_map/all_to_all | solution.py:124
  176.2 1.5 collective-permute-done.24
  177.7 2.3 fusion.25
  180.7 1.2 collective-permute-start.25
  183.5 1.9 add_convert_fusion.6
  185.4 2.8 %collective-permute-start.19 = (bf16[32,32,128]{2,1,0:T(8,128)(2,1)}, bf16[32,32,128]{2,1,0:T(8,128)(2,1)S(1)}, u32[]{:S(2)}, u32[]{:S(2)}) collective-permute-start(bf16[32,32,128]{2,1,0:T(8,128)(2,1)} %get-tuple-element.123), channel_id=1, source_target_pairs={{0,64},{1,193},{2,66},{3,195},{4,68},{5,197},{6,70},{7,199},{32,96... | collective-permute-start | bytes 786440 | tf_op jit(solution)/shard_map/ppermute | solution.py:150
  189.6 5.7 %collective-permute-done.27 = bf16[16,32,128]{2,1,0:T(8,128)(2,1)} collective-permute-done((bf16[16,32,128]{2,1,0:T(8,128)(2,1)}, bf16[16,32,128]{2,1,0:T(8,128)(2,1)}, u32[]{:S(2)}, u32[]{:S(2)}) %collective-permute-start.27) | collective-permute-done | bytes 131104 | tf_op jit(solution)/shard_map/ppermute | solution.py:150
  195.3 1.2 fusion.11
  196.5 1.3 collective-permute-done.20
  197.8 2.1 add_convert_fusion.11
  199.9 1.4 collective-permute-start.21
  201.3 4.8 %collective-permute-start.22 = (bf16[16,32,128]{2,1,0:T(8,128)(2,1)}, bf16[16,32,128]{2,1,0:T(8,128)(2,1)S(1)}, u32[]{:S(2)}, u32[]{:S(2)}) collective-permute-start(bf16[16,32,128]{2,1,0:T(8,128)(2,1)} %get-tuple-element.120), channel_id=1, source_target_pairs={{0,32},{1,225},{2,34},{3,227},{4,36},{5,229},{6,38},{7,231},{32,64... | collective-permute-start | bytes 393224 | tf_op jit(solution)/shard_map/ppermute | solution.py:150
  206.1 1.5 collective-permute-start.23
  209.1 8.1 %all-to-all-start.5 = ((bf16[8,8,32,128]{3,2,1,0:T(8,128)(2,1)}), bf16[8,8,32,128]{3,2,1,0:T(8,128)(2,1)S(1)}, u32[]{:S(2)}, u32[]{:S(2)}) async-start(bf16[8,8,32,128]{3,2,1,0:T(8,128)(2,1)} %copy.60), calls=%async_computation.5 | async-start | bytes 1048576 | tf_op jit(solution)/shard_map/all_to_all | solution.py:124
  217.3 1.3 add_convert_fusion.8
  219.3 7.5 %all-to-all-done.5 = bf16[8,8,32,128]{3,2,1,0:T(8,128)(2,1)S(1)} async-done(((bf16[8,8,32,128]{3,2,1,0:T(8,128)(2,1)}), bf16[8,8,32,128]{3,2,1,0:T(8,128)(2,1)S(1)}, u32[]{:S(2)}, u32[]{:S(2)}) %all-to-all-start.5) | async-done | bytes 524320 | tf_op jit(solution)/shard_map/all_to_all | solution.py:124
  (123 shorter events, 21.2 us)
Async XLA Ops:
  7.2 13.2 %copy-start.26 = (bf16[256,256]{1,0:T(8,128)(2,1)S(1)}, bf16[256,256]{1,0:T(8,128)(2,1)}, u32[]{:S(2)}) copy-start(bf16[256,256]{1,0:T(8,128)(2,1)} %param.8) | copy-start | bytes 393220
  7.2 111.8 %all-gather.2.cloned.1.call-start = ((), (), s32[]{:S(2)}) async-start(), calls=%async_computation.6 | async-start | bytes 6488064 | tf_op jit(solution)/shard_map/all_gather | solution.py:177
  10.7 14.1 %all-to-all-start = ((bf16[32,32,128]{2,1,0:T(8,128)(2,1)}), bf16[32,32,128]{2,1,0:T(8,128)(2,1)S(1)}, u32[]{:S(2)}, u32[]{:S(2)}) async-start(bf16[32,32,128]{2,1,0:T(8,128)(2,1)} %copy.52), calls=%async_computation | async-start | bytes 524288 | tf_op jit(solution)/shard_map/all_to_all | solution.py:124
  17.3 28.2 %copy-start.28 = (s32[1024]{0:T(1024)S(1)}, s32[1024]{0:T(1024)}, u32[]{:S(2)}) copy-start(s32[1024]{0:T(1024)} %param.11) | copy-start | bytes 12292
  17.3 40.0 %copy-start.8 = (s32[1024]{0:T(1024)S(1)}, s32[1024]{0:T(1024)}, u32[]{:S(2)}) copy-start(s32[1024]{0:T(1024)} %rows_ref.3) | copy-start | bytes 12292
  17.3 3.4 %collective-permute-start = (bf16[8,32,128]{2,1,0:T(8,128)(2,1)S(1)}, bf16[8,32,128]{2,1,0:T(8,128)(2,1)S(1)}, u32[]{:S(2)}, u32[]{:S(2)}) collective-permute-start(bf16[8,32,128]{2,1,0:T(8,128)(2,1)S(1)} %slice.134), channel_id=1, source_target_pairs={{0,8},{1,25},{2,10},{3,27},{4,12},{5,29},{6,14},{7,31},{8,16},{9,1... | collective-permute-start | bytes 196616 | tf_op jit(solution)/shard_map/ppermute | solution.py:150
  19.2 5.1 %collective-permute-start.1 = (bf16[8,32,128]{2,1,0:T(8,128)(2,1)S(1)}, bf16[8,32,128]{2,1,0:T(8,128)(2,1)S(1)}, u32[]{:S(2)}, u32[]{:S(2)}) collective-permute-start(bf16[8,32,128]{2,1,0:T(8,128)(2,1)S(1)} %slice.134), channel_id=1, source_target_pairs={{0,16},{1,17},{2,18},{3,19},{4,20},{5,21},{6,22},{7,23},{8,24},{9,... | collective-permute-start | bytes 196616 | tf_op jit(solution)/shard_map/ppermute | solution.py:150
  19.8 5.0 %collective-permute-start.2 = (bf16[8,32,128]{2,1,0:T(8,128)(2,1)S(1)}, bf16[8,32,128]{2,1,0:T(8,128)(2,1)S(1)}, u32[]{:S(2)}, u32[]{:S(2)}) collective-permute-start(bf16[8,32,128]{2,1,0:T(8,128)(2,1)S(1)} %slice.134), channel_id=1, source_target_pairs={{0,24},{1,9},{2,26},{3,11},{4,28},{5,13},{6,30},{7,15},{8,0},{9,17... | collective-permute-start | bytes 196616 | tf_op jit(solution)/shard_map/ppermute | solution.py:150
  20.6 10.2 %copy-start.12 = (bf16[8,32,8,32]{3,2,1,0:T(8,128)(2,1)}, bf16[8,32,8,32]{3,2,1,0:T(8,128)(2,1)S(1)}, u32[]{:S(2)}) copy-start(bf16[8,32,8,32]{3,2,1,0:T(8,128)(2,1)S(1)} %reshape.64) | copy-start | bytes 393220
  24.8 32.4 %copy-start.14 = (bf16[32,32,128]{2,1,0:T(8,128)(2,1)}, bf16[32,32,128]{2,1,0:T(8,128)(2,1)S(1)}, u32[]{:S(2)}) copy-start(bf16[32,32,128]{2,1,0:T(8,128)(2,1)S(1)} %pad_maximum_fusion.1.rest_1_) | copy-start | bytes 786436
  24.8 18.0 %collective-permute-start.3 = (bf16[32,32,128]{2,1,0:T(8,128)(2,1)S(1)}, bf16[32,32,128]{2,1,0:T(8,128)(2,1)S(1)}, u32[]{:S(2)}, u32[]{:S(2)}) collective-permute-start(bf16[32,32,128]{2,1,0:T(8,128)(2,1)S(1)} %pad_maximum_fusion.1.rest_1_), channel_id=1, source_target_pairs={{0,32},{1,225},{2,34},{3,227},{4,36},{5,229},{6,38},{7,231},{32,64... | collective-permute-start | bytes 786440 | tf_op jit(solution)/shard_map/ppermute | solution.py:150
  30.5 12.3 %collective-permute-start.4 = (bf16[32,32,128]{2,1,0:T(8,128)(2,1)S(1)}, bf16[32,32,128]{2,1,0:T(8,128)(2,1)S(1)}, u32[]{:S(2)}, u32[]{:S(2)}) collective-permute-start(bf16[32,32,128]{2,1,0:T(8,128)(2,1)S(1)} %pad_maximum_fusion.1.rest_1_), channel_id=1, source_target_pairs={{0,224},{1,33},{2,226},{3,35},{4,228},{5,37},{6,230},{7,39},{32,0}... | collective-permute-start | bytes 786440 | tf_op jit(solution)/shard_map/ppermute | solution.py:150
  42.8 14.4 %copy-start.18 = (bf16[32,32,128]{2,1,0:T(8,128)(2,1)}, bf16[32,32,128]{2,1,0:T(8,128)(2,1)S(1)}, u32[]{:S(2)}) copy-start(bf16[32,32,128]{2,1,0:T(8,128)(2,1)S(1)} %collective-permute-done.3.rest_8_) | copy-start | bytes 786436
  42.8 14.4 %copy-start.19 = (bf16[32,32,128]{2,1,0:T(8,128)(2,1)}, bf16[32,32,128]{2,1,0:T(8,128)(2,1)S(1)}, u32[]{:S(2)}) copy-start(bf16[32,32,128]{2,1,0:T(8,128)(2,1)S(1)} %collective-permute-done.4.rest_2_) | copy-start | bytes 786436
  42.8 9.6 %collective-permute-start.5 = (bf16[32,32,128]{2,1,0:T(8,128)(2,1)S(1)}, bf16[32,32,128]{2,1,0:T(8,128)(2,1)}, u32[]{:S(2)}, u32[]{:S(2)}) collective-permute-start(bf16[32,32,128]{2,1,0:T(8,128)(2,1)S(1)} %collective-permute-done.3.rest_8_), channel_id=1, source_target_pairs={{0,32},{1,225},{2,34},{3,227},{4,36},{5,229},{6,38},{7,231},{32,64... | collective-permute-start | bytes 786440 | tf_op jit(solution)/shard_map/ppermute | solution.py:150
  44.8 11.0 %collective-permute-start.6 = (bf16[32,32,128]{2,1,0:T(8,128)(2,1)S(1)}, bf16[32,32,128]{2,1,0:T(8,128)(2,1)}, u32[]{:S(2)}, u32[]{:S(2)}) collective-permute-start(bf16[32,32,128]{2,1,0:T(8,128)(2,1)S(1)} %collective-permute-done.4.rest_2_), channel_id=1, source_target_pairs={{0,224},{1,33},{2,226},{3,35},{4,228},{5,37},{6,230},{7,39},{32,0}... | collective-permute-start | bytes 786440 | tf_op jit(solution)/shard_map/ppermute | solution.py:150
  55.7 25.0 %collective-permute-start.7 = (bf16[32,32,128]{2,1,0:T(8,128)(2,1)}, bf16[32,32,128]{2,1,0:T(8,128)(2,1)S(1)}, u32[]{:S(2)}, u32[]{:S(2)}) collective-permute-start(bf16[32,32,128]{2,1,0:T(8,128)(2,1)} %collective-permute-done.5.rest_7_), channel_id=1, source_target_pairs={{0,32},{1,225},{2,34},{3,227},{4,36},{5,229},{6,38},{7,231},{32,64... | collective-permute-start | bytes 786440 | tf_op jit(solution)/shard_map/ppermute | solution.py:150
  55.7 26.0 %collective-permute-start.8 = (bf16[32,32,128]{2,1,0:T(8,128)(2,1)}, bf16[32,32,128]{2,1,0:T(8,128)(2,1)S(1)}, u32[]{:S(2)}, u32[]{:S(2)}) collective-permute-start(bf16[32,32,128]{2,1,0:T(8,128)(2,1)} %collective-permute-done.6.rest_3_), channel_id=1, source_target_pairs={{0,224},{1,33},{2,226},{3,35},{4,228},{5,37},{6,230},{7,39},{32,0}... | collective-permute-start | bytes 786440 | tf_op jit(solution)/shard_map/ppermute | solution.py:150
  57.2 25.9 %copy-start.15 = (bf16[32,4096]{1,0:T(8,128)(2,1)S(1)}, bf16[32,4096]{1,0:T(8,128)(2,1)}, u32[]{:S(2)}) copy-start(bf16[32,4096]{1,0:T(8,128)(2,1)} %param.13) | copy-start | bytes 786436
  82.4 21.6 %collective-permute-start.12 = (bf16[64,32,128]{2,1,0:T(8,128)(2,1)}, bf16[64,32,128]{2,1,0:T(8,128)(2,1)}, u32[]{:S(2)}, u32[]{:S(2)}) collective-permute-start(bf16[64,32,128]{2,1,0:T(8,128)(2,1)} %get-tuple-element.88), channel_id=1, source_target_pairs={{0,224},{1,33},{2,226},{3,35},{4,228},{5,37},{6,230},{7,39},{32,0}... | collective-permute-start | bytes 1572872 | tf_op jit(solution)/shard_map/ppermute | solution.py:150
  84.6 58.7 %all-to-all-start.2 = ((bf16[8,32,4096]{2,1,0:T(8,128)(2,1)}), bf16[8,32,4096]{2,1,0:T(8,128)(2,1)}, u32[]{:S(2)}, u32[]{:S(2)}) async-start(bf16[8,32,4096]{2,1,0:T(8,128)(2,1)} %tile.4), calls=%async_computation.2 | async-start | bytes 4194304 | tf_op jit(solution)/shard_map/all_to_all | solution.py:124
  91.5 21.5 %collective-permute-start.11 = (bf16[64,32,128]{2,1,0:T(8,128)(2,1)}, bf16[64,32,128]{2,1,0:T(8,128)(2,1)S(1)}, u32[]{:S(2)}, u32[]{:S(2)}) collective-permute-start(bf16[64,32,128]{2,1,0:T(8,128)(2,1)} %copy-done.11), channel_id=1, source_target_pairs={{0,32},{1,225},{2,34},{3,227},{4,36},{5,229},{6,38},{7,231},{32,64... | collective-permute-start | bytes 1572872 | tf_op jit(solution)/shard_map/ppermute | solution.py:150
  91.5 24.3 %collective-permute-start.13 = (bf16[32,32,128]{2,1,0:T(8,128)(2,1)S(1)}, bf16[32,32,128]{2,1,0:T(8,128)(2,1)S(1)}, u32[]{:S(2)}, u32[]{:S(2)}) collective-permute-start(bf16[32,32,128]{2,1,0:T(8,128)(2,1)S(1)} %copy-done.21), channel_id=1, source_target_pairs={{0,32},{1,225},{2,34},{3,227},{4,36},{5,229},{6,38},{7,231},{32,64... | collective-permute-start | bytes 786440 | tf_op jit(solution)/shard_map/ppermute | solution.py:150
  93.1 50.2 %collective-permute-start.10 = (bf16[128,32,128]{2,1,0:T(8,128)(2,1)}, bf16[128,32,128]{2,1,0:T(8,128)(2,1)}, u32[]{:S(2)}, u32[]{:S(2)}) collective-permute-start(bf16[128,32,128]{2,1,0:T(8,128)(2,1)} %copy-done.10), channel_id=1, source_target_pairs={{0,24},{1,9},{2,26},{3,11},{4,28},{5,13},{6,30},{7,15},{8,0},{9,17... | collective-permute-start | bytes 3145736 | tf_op jit(solution)/shard_map/ppermute | solution.py:150
  93.6 49.8 %collective-permute-start.9 = (bf16[128,32,128]{2,1,0:T(8,128)(2,1)}, bf16[128,32,128]{2,1,0:T(8,128)(2,1)}, u32[]{:S(2)}, u32[]{:S(2)}) collective-permute-start(bf16[128,32,128]{2,1,0:T(8,128)(2,1)} %copy-done.9), channel_id=1, source_target_pairs={{0,8},{1,25},{2,10},{3,27},{4,12},{5,29},{6,14},{7,31},{8,16},{9,1... | collective-permute-start | bytes 3145736 | tf_op jit(solution)/shard_map/ppermute | solution.py:150
  116.5 26.8 %collective-permute-start.14 = (bf16[64,32,128]{2,1,0:T(8,128)(2,1)}, bf16[64,32,128]{2,1,0:T(8,128)(2,1)}, u32[]{:S(2)}, u32[]{:S(2)}) collective-permute-start(bf16[64,32,128]{2,1,0:T(8,128)(2,1)} %add_convert_fusion.5), channel_id=1, source_target_pairs={{0,32},{1,225},{2,34},{3,227},{4,36},{5,229},{6,38},{7,231},{32,64... | collective-permute-start | bytes 1572872 | tf_op jit(solution)/shard_map/ppermute | solution.py:150
  119.0 24.4 %collective-permute-start.15 = (bf16[64,32,128]{2,1,0:T(8,128)(2,1)}, bf16[64,32,128]{2,1,0:T(8,128)(2,1)}, u32[]{:S(2)}, u32[]{:S(2)}) collective-permute-start(bf16[64,32,128]{2,1,0:T(8,128)(2,1)} %add_convert_fusion.4), channel_id=1, source_target_pairs={{0,224},{1,33},{2,226},{3,35},{4,228},{5,37},{6,230},{7,39},{32,0}... | collective-permute-start | bytes 1572872 | tf_op jit(solution)/shard_map/ppermute | solution.py:150
  145.9 20.9 %collective-permute-start.16 = (bf16[128,32,128]{2,1,0:T(8,128)(2,1)}, bf16[128,32,128]{2,1,0:T(8,128)(2,1)S(1)}, u32[]{:S(2)}, u32[]{:S(2)}) collective-permute-start(bf16[128,32,128]{2,1,0:T(8,128)(2,1)} %add_convert_fusion), channel_id=1, source_target_pairs={{0,8},{1,25},{2,10},{3,27},{4,12},{5,29},{6,14},{7,31},{8,16},{9,1... | collective-permute-start | bytes 3145736 | tf_op jit(solution)/shard_map/ppermute | solution.py:150
  147.9 18.8 %collective-permute-start.18 = (bf16[64,32,128]{2,1,0:T(8,128)(2,1)}, bf16[64,32,128]{2,1,0:T(8,128)(2,1)}, u32[]{:S(2)}, u32[]{:S(2)}) collective-permute-start(bf16[64,32,128]{2,1,0:T(8,128)(2,1)} %add_convert_fusion.2), channel_id=1, source_target_pairs={{0,224},{1,33},{2,226},{3,35},{4,228},{5,37},{6,230},{7,39},{32,0}... | collective-permute-start | bytes 1572872 | tf_op jit(solution)/shard_map/ppermute | solution.py:150
  149.9 16.8 %collective-permute-start.17 = (bf16[64,32,128]{2,1,0:T(8,128)(2,1)}, bf16[64,32,128]{2,1,0:T(8,128)(2,1)}, u32[]{:S(2)}, u32[]{:S(2)}) collective-permute-start(bf16[64,32,128]{2,1,0:T(8,128)(2,1)} %add_convert_fusion.3), channel_id=1, source_target_pairs={{0,32},{1,225},{2,34},{3,227},{4,36},{5,229},{6,38},{7,231},{32,64... | collective-permute-start | bytes 1572872 | tf_op jit(solution)/shard_map/ppermute | solution.py:150
  155.8 10.9 %all-to-all-start.3 = ((bf16[32,32,128]{2,1,0:T(8,128)(2,1)}), bf16[32,32,128]{2,1,0:T(8,128)(2,1)S(1)}, u32[]{:S(2)}, u32[]{:S(2)}) async-start(bf16[32,32,128]{2,1,0:T(8,128)(2,1)} %forward.1), calls=%async_computation.3 | async-start | bytes 524288 | tf_op jit(solution)/shard_map/all_to_all | solution.py:124
  162.6 15.1 %copy-start.7 = (bf16[64,32,128]{2,1,0:T(8,128)(2,1)S(1)}, bf16[64,32,128]{2,1,0:T(8,128)(2,1)}, u32[]{:S(2)}) copy-start(bf16[64,32,128]{2,1,0:T(8,128)(2,1)} %copy-done.6) | copy-start | bytes 1572868
  166.7 13.2 %copy-start.24 = (bf16[32,32,128]{2,1,0:T(8,128)(2,1)}, bf16[32,32,128]{2,1,0:T(8,128)(2,1)S(1)}, u32[]{:S(2)}) copy-start(bf16[32,32,128]{2,1,0:T(8,128)(2,1)S(1)} %all-to-all-done.3) | copy-start | bytes 786436
  169.2 8.5 %collective-permute-start.24 = (bf16[64,32,128]{2,1,0:T(8,128)(2,1)}, bf16[64,32,128]{2,1,0:T(8,128)(2,1)S(1)}, u32[]{:S(2)}, u32[]{:S(2)}) collective-permute-start(bf16[64,32,128]{2,1,0:T(8,128)(2,1)} %add_convert_fusion.1), channel_id=1, source_target_pairs={{0,32},{1,225},{2,34},{3,227},{4,36},{5,229},{6,38},{7,231},{32,64... | collective-permute-start | bytes 1572872 | tf_op jit(solution)/shard_map/ppermute | solution.py:150
  171.5 26.3 %all-to-all-start.4 = ((bf16[32,32,256]{2,1,0:T(8,128)(2,1)}), bf16[32,32,256]{2,1,0:T(8,128)(2,1)S(1)}, u32[]{:S(2)}, u32[]{:S(2)}) async-start(bf16[32,32,256]{2,1,0:T(8,128)(2,1)} %tile.5), calls=%async_computation.4 | async-start | bytes 1048576 | tf_op jit(solution)/shard_map/all_to_all | solution.py:124
  176.2 7.3 %copy-start.17 = (bf16[128,32,128]{2,1,0:T(8,128)(2,1)S(1)}, bf16[128,32,128]{2,1,0:T(8,128)(2,1)}, u32[]{:S(2)}) copy-start(bf16[128,32,128]{2,1,0:T(8,128)(2,1)} %copy-done.16) | copy-start | bytes 3145732
  180.0 8.2 %copy-start.13 = (bf16[8,32,8,32]{3,2,1,0:T(8,128)(2,1)S(1)}, bf16[8,32,8,32]{3,2,1,0:T(8,128)(2,1)}, u32[]{:S(2)}) copy-start(bf16[8,32,8,32]{3,2,1,0:T(8,128)(2,1)} %copy-done.12) | copy-start | bytes 393220
  180.7 7.9 %collective-permute-start.25 = (bf16[16,32,128]{2,1,0:T(8,128)(2,1)}, bf16[16,32,128]{2,1,0:T(8,128)(2,1)S(1)}, u32[]{:S(2)}, u32[]{:S(2)}) collective-permute-start(bf16[16,32,128]{2,1,0:T(8,128)(2,1)} %get-tuple-element.124), channel_id=1, source_target_pairs={{0,8},{1,25},{2,10},{3,27},{4,12},{5,29},{6,14},{7,31},{8,16},{9,1... | collective-permute-start | bytes 393224 | tf_op jit(solution)/shard_map/ppermute | solution.py:150
  182.0 7.6 %collective-permute-start.26 = (bf16[16,32,128]{2,1,0:T(8,128)(2,1)}, bf16[16,32,128]{2,1,0:T(8,128)(2,1)}, u32[]{:S(2)}, u32[]{:S(2)}) collective-permute-start(bf16[16,32,128]{2,1,0:T(8,128)(2,1)} %get-tuple-element.126), channel_id=1, source_target_pairs={{0,16},{1,17},{2,18},{3,19},{4,20},{5,21},{6,22},{7,23},{8,24},{9,... | collective-permute-start | bytes 393224 | tf_op jit(solution)/shard_map/ppermute | solution.py:150
  182.6 12.6 %collective-permute-start.27 = (bf16[16,32,128]{2,1,0:T(8,128)(2,1)}, bf16[16,32,128]{2,1,0:T(8,128)(2,1)}, u32[]{:S(2)}, u32[]{:S(2)}) collective-permute-start(bf16[16,32,128]{2,1,0:T(8,128)(2,1)} %get-tuple-element.125), channel_id=1, source_target_pairs={{0,24},{1,9},{2,26},{3,11},{4,28},{5,13},{6,30},{7,15},{8,0},{9,17... | collective-permute-start | bytes 393224 | tf_op jit(solution)/shard_map/ppermute | solution.py:150
  185.4 11.1 %collective-permute-start.19 = (bf16[32,32,128]{2,1,0:T(8,128)(2,1)}, bf16[32,32,128]{2,1,0:T(8,128)(2,1)S(1)}, u32[]{:S(2)}, u32[]{:S(2)}) collective-permute-start(bf16[32,32,128]{2,1,0:T(8,128)(2,1)} %get-tuple-element.123), channel_id=1, source_target_pairs={{0,64},{1,193},{2,66},{3,195},{4,68},{5,197},{6,70},{7,199},{32,96... | collective-permute-start | bytes 786440 | tf_op jit(solution)/shard_map/ppermute | solution.py:150
  188.2 19.6 %copy-start.25 = (bf16[32,32,128]{2,1,0:T(8,128)(2,1)S(1)}, bf16[32,32,128]{2,1,0:T(8,128)(2,1)}, u32[]{:S(2)}) copy-start(bf16[32,32,128]{2,1,0:T(8,128)(2,1)} %copy-done.24) | copy-start | bytes 786436
  188.2 9.6 %collective-permute-start.20 = (bf16[32,32,128]{2,1,0:T(8,128)(2,1)S(1)}, bf16[32,32,128]{2,1,0:T(8,128)(2,1)}, u32[]{:S(2)}, u32[]{:S(2)}) collective-permute-start(bf16[32,32,128]{2,1,0:T(8,128)(2,1)S(1)} %get-tuple-element.122), channel_id=1, source_target_pairs={{0,192},{1,65},{2,194},{3,67},{4,196},{5,69},{6,198},{7,71},{32,22... | collective-permute-start | bytes 786440 | tf_op jit(solution)/shard_map/ppermute | solution.py:150
  199.9 17.3 %collective-permute-start.21 = (bf16[16,32,128]{2,1,0:T(8,128)(2,1)}, bf16[16,32,128]{2,1,0:T(8,128)(2,1)S(1)}, u32[]{:S(2)}, u32[]{:S(2)}) collective-permute-start(bf16[16,32,128]{2,1,0:T(8,128)(2,1)} %get-tuple-element.119), channel_id=1, source_target_pairs={{0,64},{1,193},{2,66},{3,195},{4,68},{5,197},{6,70},{7,199},{32,96... | collective-permute-start | bytes 393224 | tf_op jit(solution)/shard_map/ppermute | solution.py:150
  201.3 16.0 %collective-permute-start.22 = (bf16[16,32,128]{2,1,0:T(8,128)(2,1)}, bf16[16,32,128]{2,1,0:T(8,128)(2,1)S(1)}, u32[]{:S(2)}, u32[]{:S(2)}) collective-permute-start(bf16[16,32,128]{2,1,0:T(8,128)(2,1)} %get-tuple-element.120), channel_id=1, source_target_pairs={{0,32},{1,225},{2,34},{3,227},{4,36},{5,229},{6,38},{7,231},{32,64... | collective-permute-start | bytes 393224 | tf_op jit(solution)/shard_map/ppermute | solution.py:150
  206.1 11.2 %collective-permute-start.23 = (bf16[16,32,128]{2,1,0:T(8,128)(2,1)}, bf16[16,32,128]{2,1,0:T(8,128)(2,1)}, u32[]{:S(2)}, u32[]{:S(2)}) collective-permute-start(bf16[16,32,128]{2,1,0:T(8,128)(2,1)} %get-tuple-element.121), channel_id=1, source_target_pairs={{0,224},{1,33},{2,226},{3,35},{4,228},{5,37},{6,230},{7,39},{32,0}... | collective-permute-start | bytes 393224 | tf_op jit(solution)/shard_map/ppermute | solution.py:150
  209.1 17.6 %all-to-all-start.5 = ((bf16[8,8,32,128]{3,2,1,0:T(8,128)(2,1)}), bf16[8,8,32,128]{3,2,1,0:T(8,128)(2,1)S(1)}, u32[]{:S(2)}, u32[]{:S(2)}) async-start(bf16[8,8,32,128]{3,2,1,0:T(8,128)(2,1)} %copy.60), calls=%async_computation.5 | async-start | bytes 1048576 | tf_op jit(solution)/shard_map/all_to_all | solution.py:124
  217.3 11.2 %copy-start.1 = (bf16[32,4096]{1,0:T(8,128)(2,1)S(1)}, bf16[32,4096]{1,0:T(8,128)(2,1)}, u32[]{:S(2)}) copy-start(bf16[32,4096]{1,0:T(8,128)(2,1)} %param.7) | copy-start | bytes 786436
  (15 other events, 29.8 us)
Sparse Core Ops, SparseCore 0:
  10.6 103.0 all-gather.1
